TPU v7x, 32 devices: a whole 2x2x4 slice. The times are simulated.
32 devices in a mesh: sp: 8 (over z, x), ch: 4 (over y, core).
Axes of the slice: x: 2, y: 2, z: 4, core: 2. Of those that a mesh axis runs over, the one named last changes fastest.
Arguments:
- features: bfloat16 [4, 48, 48, 2048], P(None, 'sp'), may hold values from -80 to 80
- heights: int32 [4, 1], replicated, may hold values from 24 to 48, as said below
- widths: int32 [4, 1], replicated, may hold values from 24 to 48, as said below
- w_point: bfloat16 [256, 2048], P('ch'), may hold values from -0.125 to 0.125
- atrous_weight: bfloat16 [3, 3, 3, 256, 2048], P(None, None, None, 'ch'), may hold values from -0.046875 to 0.046875
- w_pool: bfloat16 [256, 2048], P('ch'), may hold values from -0.125 to 0.125
- w_proj: bfloat16 [5, 256, 256], P(None, 'ch'), may hold values from -0.15625 to 0.15625
- bn_gains: float32 [6, 256], P(None, 'ch'), may hold values from 0.25 to 1.75
- bn_shifts: float32 [6, 256], P(None, 'ch'), may hold values from -2.5 to 2.5
- out_grad: bfloat16 [4, 48, 48, 256], P(None, 'sp'), may hold values from -6 to 6
Outputs:
- output: bfloat16 [4, 48, 48, 256], P(None, 'sp', None, 'ch')
- in_grad: bfloat16 [4, 48, 48, 2048], P(None, 'sp', None, 'ch')
- g_point: float32 [256, 2048], P('ch')
- g_atrous: float32 [3, 3, 3, 256, 2048], P(None, None, None, 'ch')
- g_pool: float32 [256, 2048], P('ch')
- g_proj: float32 [5, 256, 256], P(None, 'ch')
- g_gains: float32 [6, 256], P(None, 'ch')
- g_shifts: float32 [6, 256], P(None, 'ch')
Inputs may be any that keep to these rules, and one draw needn't show every extreme that they name: `heights`: in every column g one image has height 48. `widths`: in every column g one image has width 48.
All inputs are finite; a program needn't handle non-finite values.
Results may differ from a plain program's by a relative error of at most 0.014.
Values may be sent and summed in bfloat16 or wider, within the bound.
No kernel may reach another device: no remote copies, remote signals or barrier semaphores. Data moves between devices by JAX's collectives and lax.ppermute only.
A program may use at most 256 MiB of HBM per device.

v0:
```python
import jax
import jax.numpy as jnp
from jax import lax
from jax.sharding import PartitionSpec as P

BLOCKS = 8


epsilon = 1e-05
dilation_factors = (1, 2, 3)
highest_precision = lax.Precision.HIGHEST


def from_behind(block, axis, distance):
    devices = range(lax.axis_size(axis))
    route = [(i - distance, i) for i in devices if i - distance in devices]
    return lax.ppermute(block, axis, route)


def shift_cols(values, offset):
    margin = abs(offset)
    padded = jnp.pad(values, ((0, 0), (0, 0), (margin, margin), (0, 0)))
    return lax.slice_in_dim(padded, margin + offset, margin + offset + values.shape[2], axis=2)


def silu_slope(pre_act):
    sigmoid_val = jax.nn.sigmoid(pre_act)
    return sigmoid_val * (1.0 + pre_act * (1.0 - sigmoid_val))


def source_inside(block_id, shift_amount):
    source = block_id - shift_amount
    return (source >= 0) & (source < BLOCKS)


def move_features(values, shift_amount):
    return from_behind(values, "sp", shift_amount)


def shifted_gradients(values, shift_amount):
    return from_behind(values, "sp", shift_amount)


def tap_partials(source, weight_taps, dilation_rate):
    count_k, rows_dev, grid_width, channel_total = source.shape
    local_output = weight_taps.shape[1]
    products = jnp.einsum(
        "pc,tc->pt",
        source.reshape(-1, channel_total),
        weight_taps.reshape(3 * local_output, channel_total),
        preferred_element_type=jnp.float32,
    ).reshape(count_k, rows_dev, grid_width, 3, local_output)
    return (
        shift_cols(products[:, :, :, 0, :], -dilation_rate)
        + products[:, :, :, 1, :]
        + shift_cols(products[:, :, :, 2, :], dilation_rate)
    )


def body(
    features, heights, widths, w_point, atrous_weight, w_pool, w_proj, bn_gains, bn_shifts, out_grad
):
    count_k, rows_dev, grid_width, channel_total = features.shape
    local_output = w_point.shape[0]
    full_out = w_proj.shape[2]
    groups = heights.shape[1]
    images = count_k * groups
    pixels = count_k * rows_dev * grid_width
    position = lax.axis_index("sp")
    block_id = position % BLOCKS
    group_id = position // BLOCKS
    channel_start = lax.axis_index("ch") * local_output
    own_out_grad = lax.dynamic_slice_in_dim(out_grad, channel_start, local_output, 3)
    group_pick = jnp.arange(groups, dtype=jnp.int32) == group_id
    group_onehot = group_pick.astype(jnp.float32)
    own_heights = jnp.sum(jnp.where(group_pick[None, :], heights, 0), axis=1)
    own_widths = jnp.sum(jnp.where(group_pick[None, :], widths, 0), axis=1)
    row_ids = block_id * rows_dev + jnp.arange(rows_dev, dtype=jnp.int32)
    col_ids = jnp.arange(grid_width, dtype=jnp.int32)
    inside = (row_ids[None, :, None] < own_heights[:, None, None]) & (
        col_ids[None, None, :] < own_widths[:, None, None]
    )
    pix_mask = inside.astype(jnp.float32)[..., None]
    valid_count = jnp.sum((heights * widths).astype(jnp.float32))
    own_count = (own_heights * own_widths).astype(jnp.float32)
    masked_values = features * pix_mask.astype(jnp.bfloat16)
    flat_pix = masked_values.reshape(pixels, channel_total)
    point_conv = jnp.einsum("pc,fc->pf", flat_pix, w_point, preferred_element_type=jnp.float32)
    conv_list = [point_conv.reshape(count_k, rows_dev, grid_width, local_output)]
    for dilation_index, dilation_factor in enumerate(dilation_factors):
        dilation_rate = rows_dev * dilation_factor
        running_total = tap_partials(masked_values, atrous_weight[dilation_index, 1], dilation_rate)
        for row_offset_tap in (0, 2):
            shift_amount = (1 - row_offset_tap) * dilation_factor
            keep_rows = source_inside(block_id, shift_amount)
            received_part = move_features(masked_values, shift_amount) * keep_rows.astype(
                jnp.bfloat16
            )
            running_total = running_total + tap_partials(
                received_part, atrous_weight[dilation_index, row_offset_tap], dilation_rate
            )
        conv_list.append(running_total)
    conv_out = jnp.stack(conv_list)
    stat_sum, stat_square = lax.psum(
        (
            jnp.sum(conv_out * pix_mask, axis=(1, 2, 3)),
            jnp.sum(conv_out * conv_out * pix_mask, axis=(1, 2, 3)),
        ),
        "sp",
    )
    branch_mean = stat_sum / valid_count
    branch_inv = lax.rsqrt(stat_square / valid_count - branch_mean * branch_mean + epsilon)
    normed = (conv_out - branch_mean[:, None, None, None, :]) * branch_inv[:, None, None, None, :]
    pre_act = bn_gains[:4][:, None, None, None, :] * normed + bn_shifts[:4][:, None, None, None, :]
    branch_act = (pix_mask * jax.nn.silu(pre_act)).astype(jnp.bfloat16)
    own_sums = jnp.sum(masked_values, axis=(1, 2), dtype=jnp.float32)
    own_pooled = own_sums / own_count[:, None]
    pool_weight = w_pool.astype(jnp.float32)
    pooled = lax.psum(own_pooled[:, None, :] * group_onehot[None, :, None], "sp")
    projected = jnp.dot(
        pooled.reshape(images, channel_total), pool_weight.T, precision=highest_precision
    )
    pool_mean = jnp.mean(projected, axis=0)
    pool_inv = lax.rsqrt(jnp.mean(projected * projected, axis=0) - pool_mean * pool_mean + epsilon)
    pool_normed = (projected - pool_mean) * pool_inv
    pool_pre = bn_gains[4] * pool_normed + bn_shifts[4]
    pool_act = jax.nn.silu(pool_pre).astype(jnp.bfloat16)
    own_act = jnp.sum(
        pool_act.astype(jnp.float32).reshape(count_k, groups, local_output)
        * group_onehot[None, :, None],
        axis=1,
    )
    pool_pixels = (own_act[:, None, None, :] * pix_mask).astype(jnp.bfloat16)
    stacked = jnp.concatenate([branch_act, pool_pixels[None]], axis=0).reshape(
        5, pixels, local_output
    )
    partial_value = jnp.einsum("bpf,bfo->po", stacked, w_proj, preferred_element_type=jnp.float32)
    mixed_sum = lax.psum_scatter(
        partial_value.reshape(count_k, rows_dev, grid_width, full_out),
        "ch",
        scatter_dimension=3,
        tiled=True,
    )
    final_sum, final_square = lax.psum(
        (
            jnp.sum(mixed_sum * pix_mask, axis=(0, 1, 2)),
            jnp.sum(mixed_sum * mixed_sum * pix_mask, axis=(0, 1, 2)),
        ),
        "sp",
    )
    final_mean = final_sum / valid_count
    final_inv = lax.rsqrt(final_square / valid_count - final_mean * final_mean + epsilon)
    final_normed = (mixed_sum - final_mean) * final_inv
    final_pre = bn_gains[5] * final_normed + bn_shifts[5]
    output = (pix_mask * jax.nn.silu(final_pre)).astype(jnp.bfloat16)
    final_dt = pix_mask * own_out_grad.astype(jnp.float32) * silu_slope(final_pre)
    final_beta, final_gamma = lax.psum(
        (jnp.sum(final_dt, axis=(0, 1, 2)), jnp.sum(final_dt * final_normed, axis=(0, 1, 2))), "sp"
    )
    mixed_grad = (
        pix_mask
        * final_inv
        * bn_gains[5]
        * (final_dt - final_beta / valid_count - final_normed * final_gamma / valid_count)
    ).astype(jnp.bfloat16)
    full_grad = lax.all_gather(mixed_grad, "ch", axis=3, tiled=True).reshape(pixels, full_out)
    g_proj = jnp.einsum("bpf,po->bfo", stacked, full_grad, preferred_element_type=jnp.float32)
    act_grads = jnp.einsum(
        "po,bfo->bpf", full_grad, w_proj, preferred_element_type=jnp.float32
    ).reshape(5, count_k, rows_dev, grid_width, local_output)
    branch_dt = pix_mask * act_grads[:4] * silu_slope(pre_act)
    pool_own_grad = jnp.sum(act_grads[4] * pix_mask, axis=(1, 2))
    branch_beta, branch_gamma, pool_grad = lax.psum(
        (
            jnp.sum(branch_dt, axis=(1, 2, 3)),
            jnp.sum(branch_dt * normed, axis=(1, 2, 3)),
            pool_own_grad[:, None, :] * group_onehot[None, :, None],
        ),
        "sp",
    )
    convolution_gradients = (
        pix_mask
        * branch_inv[:, None, None, None, :]
        * bn_gains[:4][:, None, None, None, :]
        * (
            branch_dt
            - branch_beta[:, None, None, None, :] / valid_count
            - normed * branch_gamma[:, None, None, None, :] / valid_count
        )
    ).astype(jnp.bfloat16)
    pool_dt = pool_grad.reshape(images, local_output) * silu_slope(pool_pre)
    pool_beta = jnp.sum(pool_dt, axis=0)
    pool_gamma = jnp.sum(pool_dt * pool_normed, axis=0)
    proj_grad = (
        pool_inv * bn_gains[4] * (pool_dt - pool_beta / images - pool_normed * pool_gamma / images)
    )
    own_proj_grad = jnp.sum(
        proj_grad.reshape(count_k, groups, local_output) * group_onehot[None, :, None], axis=1
    )
    g_pool = jnp.einsum("kf,kc->fc", own_proj_grad, own_pooled, precision=highest_precision)
    pooled_grad = (
        jnp.einsum("kf,fc->kc", own_proj_grad, pool_weight, precision=highest_precision)
        / own_count[:, None]
    )
    point_grad = convolution_gradients[0].reshape(pixels, local_output)
    g_point = jnp.einsum("pf,pc->fc", point_grad, flat_pix, preferred_element_type=jnp.float32)
    input_term = jnp.einsum("pf,fc->pc", point_grad, w_point, preferred_element_type=jnp.float32)
    input_term = (
        input_term.reshape(count_k, rows_dev, grid_width, channel_total)
        + pooled_grad[:, None, None, :]
    )
    atrous_list = []
    for dilation_index, dilation_factor in enumerate(dilation_factors):
        dilation_rate = rows_dev * dilation_factor
        tap_list = []
        for row_offset_tap in range(3):
            shift_amount = (row_offset_tap - 1) * dilation_factor
            if shift_amount == 0:
                received_part = convolution_gradients[dilation_index + 1]
            else:
                received_part = shifted_gradients(
                    convolution_gradients[dilation_index + 1], shift_amount
                ) * source_inside(block_id, shift_amount).astype(jnp.bfloat16)
            spread = jnp.stack(
                [
                    shift_cols(received_part, dilation_rate),
                    received_part,
                    shift_cols(received_part, -dilation_rate),
                ],
                axis=3,
            ).reshape(pixels, 3 * local_output)
            tap_list.append(
                jnp.einsum(
                    "pt,pc->tc", spread, flat_pix, preferred_element_type=jnp.float32
                ).reshape(3, local_output, channel_total)
            )
            tap_weight_slice = atrous_weight[dilation_index, row_offset_tap].reshape(
                3 * local_output, channel_total
            )
            input_term = input_term + jnp.einsum(
                "pt,tc->pc", spread, tap_weight_slice, preferred_element_type=jnp.float32
            ).reshape(count_k, rows_dev, grid_width, channel_total)
        atrous_list.append(jnp.stack(tap_list))
    g_atrous = jnp.stack(atrous_list)
    in_grad = lax.psum_scatter(
        (input_term * pix_mask).astype(jnp.bfloat16), "ch", scatter_dimension=3, tiled=True
    )
    g_point, g_atrous, g_proj, g_pool = (
        lax.psum(g_point.astype(jnp.bfloat16), "sp").astype(jnp.float32),
        lax.psum(g_atrous.astype(jnp.bfloat16), "sp").astype(jnp.float32),
        lax.psum(g_proj.astype(jnp.bfloat16), "sp").astype(jnp.float32),
        lax.psum(g_pool.astype(jnp.bfloat16), "sp").astype(jnp.float32),
    )
    g_gains = jnp.concatenate([branch_gamma, pool_gamma[None], final_gamma[None]], axis=0)
    g_shifts = jnp.concatenate([branch_beta, pool_beta[None], final_beta[None]], axis=0)
    return (output, in_grad, g_point, g_atrous, g_pool, g_proj, g_gains, g_shifts)


def solution(mesh):
    placed = (
        P(None, "sp", None, None),
        P(),
        P(),
        P("ch", None),
        P(None, None, None, "ch", None),
        P("ch", None),
        P(None, "ch", None),
        P(None, "ch"),
        P(None, "ch"),
        P(None, "sp", None, None),
    )
    return jax.shard_map(
        body,
        mesh=mesh,
        in_specs=placed,
        out_specs=(
            P(None, "sp", None, "ch"),
            P(None, "sp", None, "ch"),
            P("ch", None),
            P(None, None, None, "ch", None),
            P("ch", None),
            P(None, "ch", None),
            P(None, "ch"),
            P(None, "ch"),
        ),
        check_vma=False,
    )
```

profile of v0, /device:TPU:0, one launch (start us, length us, event | category | flops | bytes accessed | tf_op | source)
XLA Modules:
  0.0 1072.0 jit_solution(16019036484925293292)
XLA Ops:
  8.2 5.8 convert_reduce_fusion
  15.3 8.6 collective-permute-start.4
  25.2 8.8 collective-permute-start.2
  39.1 4.6 fusion.12
  43.7 5.3 fusion.14
  49.1 7.0 fusion.16
  61.0 61.9 %collective-permute-done.5 = bf16[4,6,48,2048]{3,2,1,0:T(8,128)(2,1)} collective-permute-done((bf16[4,6,48,2048]{3,2,1,0:T(8,128)(2,1)}, bf16[4,6,48,2048]{3,2,1,0:T(8,128)(2,1)}, u32[]{:S(2)}, u32[]{:S(2)}) %collective-permute-start.5) | collective-permute-done | bytes 4718624 | tf_op jit(solution)/shard_map/ppermute | solution.py:17
  122.9 108.1 %collective-permute-start = (bf16[4,6,48,2048]{3,2,1,0:T(8,128)(2,1)}, bf16[4,6,48,2048]{3,2,1,0:T(8,128)(2,1)}, u32[]{:S(2)}, u32[]{:S(2)}) collective-permute-start(bf16[4,6,48,2048]{3,2,1,0:T(8,128)(2,1)} %get-tuple-element.40), channel_id=1, source_target_pairs={{0,4},{4,8},{8,12},{12,16},{16,20},{20,24},{24,28},{1,5},{5,9},{9,... | collective-permute-start | bytes 14155784 | tf_op jit(solution)/shard_map/ppermute | solution.py:17
  231.0 4.7 fusion
  235.7 4.6 fusion.2
  242.3 4.8 fusion.4
  247.1 77.4 %collective-permute-done.2 = bf16[4,6,48,2048]{3,2,1,0:T(8,128)(2,1)} collective-permute-done((bf16[4,6,48,2048]{3,2,1,0:T(8,128)(2,1)}, bf16[4,6,48,2048]{3,2,1,0:T(8,128)(2,1)}, u32[]{:S(2)}, u32[]{:S(2)}) %collective-permute-start.2) | collective-permute-done | bytes 4718624 | tf_op jit(solution)/shard_map/ppermute | solution.py:17
  324.5 4.6 fusion.6
  332.1 4.8 fusion.8
  337.0 92.2 %collective-permute-done = bf16[4,6,48,2048]{3,2,1,0:T(8,128)(2,1)} collective-permute-done((bf16[4,6,48,2048]{3,2,1,0:T(8,128)(2,1)}, bf16[4,6,48,2048]{3,2,1,0:T(8,128)(2,1)}, u32[]{:S(2)}, u32[]{:S(2)}) %collective-permute-start) | collective-permute-done | bytes 4718624 | tf_op jit(solution)/shard_map/ppermute | solution.py:17
  429.2 4.6 fusion.10
  437.5 36.6 %all-reduce.30 = (f32[4,2048]{1,0:T(4,128)}, f32[4,64]{1,0:T(4,128)}, f32[4,64]{1,0:T(4,128)}) all-reduce(f32[4,2048]{1,0:T(4,128)} %fusion.120, f32[4,64]{1,0:T(4,128)S(1)} %get-tuple-element.9, f32[4,64]{1,0:T(4,128)S(1)} %get-tuple-element.8), channel_id=1, replica_groups=mesh['sp'=8,'ch'=4] {'sp'}, use_global_device_ids=true, to_apply=%region_6.7 | all-reduce | flops 8704 | bytes 69632 | tf_op jit(solution)/shard_map/psum | solution.py:119
  492.2 5.4 copy.284
  497.6 4.3 reshape.546
  502.0 6.2 fusion.141
  509.1 15.9 %reduce-scatter.7.cloned.1.call-done = f32[64,1152]{1,0:T(8,128)} async-done(((f32[256,1152]{1,0:T(8,128)}), f32[64,1152]{1,0:T(8,128)}) %reduce-scatter.7.cloned.1.call-update) | async-done | bytes 294928
  530.0 22.0 %all-reduce.29 = (f32[64]{0:T(128)}, f32[64]{0:T(128)}) all-reduce(f32[64]{0:T(128)} %get-tuple-element.15, f32[64]{0:T(128)} %get-tuple-element.14), channel_id=1, replica_groups=mesh['sp'=8,'ch'=4] {'sp'}, use_global_device_ids=true, to_apply=%region_11.12 | all-reduce | flops 128 | bytes 1024 | tf_op jit(solution)/shard_map/psum | solution.py:144
  555.7 17.8 %all-reduce.28 = (f32[64]{0:T(128)}, f32[64]{0:T(128)}) all-reduce(f32[64]{0:T(128)} %get-tuple-element.11, f32[64]{0:T(128)} %get-tuple-element.10), channel_id=1, replica_groups=mesh['sp'=8,'ch'=4] {'sp'}, use_global_device_ids=true, to_apply=%region_17.18 | all-reduce | flops 128 | bytes 1024 | tf_op jit(solution)/shard_map/psum | solution.py:157
  578.9 12.4 %all_gather.3 = bf16[4,6,48,256]{2,0,1,3:T(4,128)(2,1)} all-gather(bf16[4,6,48,64]{2,0,1,3:T(4,128)(2,1)S(1)} %copy.216), channel_id=1, replica_groups=mesh['sp'=8,'ch'=4] {'ch'}, dimensions={3}, use_global_device_ids=true | all-gather | bytes 737280 | tf_op jit(solution)/shard_map/all_gather | solution.py:166
  604.7 20.3 %all-reduce.27 = (f32[4,64]{1,0:T(4,128)S(1)}, f32[4,64]{1,0:T(4,128)S(1)}, f32[4,64]{1,0:T(4,128)}) all-reduce(f32[4,64]{1,0:T(4,128)S(1)} %get-tuple-element.13, f32[4,64]{1,0:T(4,128)S(1)} %get-tuple-element.12, f32[4,64]{1,0:T(4,128)} %broadcast_multiply_fusion.7), channel_id=1, replica_groups=mesh['sp'=8,'ch'=4] {'sp'}, use_global_device_ids=true, to_apply=%region_21.22 | all-reduce | flops 768 | bytes 6144 | tf_op jit(solution)/shard_map/psum | solution.py:173
  628.5 4.7 multiply_convert_fusion.1
  650.0 7.8 collective-permute-start.7
  662.9 4.4 fusion.31
  667.3 4.4 fusion.28
  672.0 4.4 fusion.25
  710.4 4.6 fusion.24
  718.5 4.6 fusion.26
  726.7 4.6 fusion.27
  734.9 4.6 fusion.29
  741.2 4.6 fusion.30
  758.5 6.1 fusion.112
  764.6 5.1 fusion.150
  769.8 5.0 fusion.147
  774.8 5.0 fusion.144
  795.5 6.2 fusion.148
  801.7 5.0 fusion.146
  806.7 4.9 fusion.145
  811.7 4.9 fusion.143
  816.6 5.0 fusion.149
  821.6 29.5 %multiply_convert_fusion = bf16[4,6,48,2048]{3,2,1,0:T(8,128)(2,1)} fusion(f32[4,6,48,2048]{3,2,1,0:T(8,128)} %fusion.150, f32[4,6,48,2048]{3,2,1,0:T(8,128)} %fusion.149, f32[4,6,48,2048]{3,2,1,0:T(8,128)} %fusion.148, f32[4,6,48,2048]{3,2,1,0:T(8,128)} %fusion.147, f32[4,6,48,2048]{3,2,1,0:T(8,128)} %fusion.146, f32[4,6,48,2048]{3,2,1,0:T(8,128)} %fusion.145, ...), kind=kOutput, calls=%fused_computation | convolution fusion | flops 934281216 | bytes 90919424 | tf_op jit(solution)/shard_map/pt,tc->pc/dot_general | solution.py:240
  853.0 162.3 %all-reduce.34.cloned.1.call-done = (bf16[64,2048]{1,0:T(8,128)(2,1)}, bf16[3,3,3,64,2048]{4,3,2,1,0:T(8,128)(2,1)}, bf16[64,2048]{1,0:T(8,128)(2,1)}, bf16[5,64,256]{2,1,0:T(8,128)(2,1)}) async-done(((bf16[64,2048]{1,0:T(8,128)(2,1)}, bf16[3,3,3,64,2048]{4,3,2,1,0:T(8,128)(2,1)}, bf16[64,2048]{1,0:T(8,128)(2,1)}, bf16[5,64,256]{2,1,0:T(8,128)(2,1)}), (bf16[64,2048]{1,0:T(8,128)(2,1)}, ...) | async-done | bytes 7766032 | tf_op jit(solution)/shard_map/psum | solution.py:249
  1020.5 10.9 %convert_element_type.206 = f32[3,3,3,64,2048]{4,3,2,1,0:T(8,128)} convert(bf16[3,3,3,64,2048]{4,3,2,1,0:T(8,128)(2,1)} %get-tuple-element.31) | non-fusion elementwise | flops 3538944 | bytes 21233664 | tf_op jit(solution)/shard_map/convert_element_type | solution.py:250
  1031.4 33.9 %reduce-scatter.5.cloned.1.call-done = bf16[4,6,48,512]{3,2,1,0:T(8,128)(2,1)} async-done(((bf16[4,6,48,2048]{3,2,1,0:T(8,128)(2,1)}), bf16[4,6,48,512]{3,2,1,0:T(8,128)(2,1)}) %reduce-scatter.5.cloned.1.call-update) | async-done | bytes 1179664 | tf_op jit(solution)/shard_map/reduce_scatter | solution.py:245
  (313 shorter events, 175.5 us)
Async XLA Ops:
  7.2 28.2 %copy-start = (bf16[64,2048]{1,0:T(8,128)(2,1)S(1)}, bf16[64,2048]{1,0:T(8,128)(2,1)}, u32[]{:S(2)}) copy-start(bf16[64,2048]{1,0:T(8,128)(2,1)} %param.13) | copy-start | bytes 786436
  7.2 517.9 %reduce-scatter.7.cloned.1.call-start = ((), (), s32[]{:S(2)}) async-start(), calls=%async_computation.3 | async-start | bytes 1474560
  7.9 52.3 %copy-start.61 = (f32[4]{0:T(128)}, f32[4]{0:T(128)S(1)}, u32[]{:S(2)}) copy-start(f32[4]{0:T(128)S(1)} %get-tuple-element.107) | copy-start | bytes 52
  14.0 46.2 %copy-start.41 = (f32[4,2048]{1,0:T(4,128)}, f32[4,2048]{1,0:T(4,128)S(1)}, u32[]{:S(2)}) copy-start(f32[4,2048]{1,0:T(4,128)S(1)} %get-tuple-element.39) | copy-start | bytes 98308
  14.0 108.8 %collective-permute-start.5 = (bf16[4,6,48,2048]{3,2,1,0:T(8,128)(2,1)}, bf16[4,6,48,2048]{3,2,1,0:T(8,128)(2,1)}, u32[]{:S(2)}, u32[]{:S(2)}) collective-permute-start(bf16[4,6,48,2048]{3,2,1,0:T(8,128)(2,1)} %get-tuple-element.40), channel_id=1, source_target_pairs={{12,0},{16,4},{20,8},{24,12},{28,16},{13,1},{17,5},{21,9},{25,13},... | collective-permute-start | bytes 14155784 | tf_op jit(solution)/shard_map/ppermute | solution.py:17
  15.3 220.3 %collective-permute-start.4 = (bf16[4,6,48,2048]{3,2,1,0:T(8,128)(2,1)}, bf16[4,6,48,2048]{3,2,1,0:T(8,128)(2,1)}, u32[]{:S(2)}, u32[]{:S(2)}) collective-permute-start(bf16[4,6,48,2048]{3,2,1,0:T(8,128)(2,1)} %get-tuple-element.40), channel_id=1, source_target_pairs={{0,12},{4,16},{8,20},{12,24},{16,28},{1,13},{5,17},{9,21},{13,25},... | collective-permute-start | bytes 14155784 | tf_op jit(solution)/shard_map/ppermute | solution.py:17
  23.9 218.3 %collective-permute-start.3 = (bf16[4,6,48,2048]{3,2,1,0:T(8,128)(2,1)}, bf16[4,6,48,2048]{3,2,1,0:T(8,128)(2,1)}, u32[]{:S(2)}, u32[]{:S(2)}) collective-permute-start(bf16[4,6,48,2048]{3,2,1,0:T(8,128)(2,1)} %get-tuple-element.40), channel_id=1, source_target_pairs={{8,0},{12,4},{16,8},{20,12},{24,16},{28,20},{9,1},{13,5},{17,9},{2... | collective-permute-start | bytes 14155784 | tf_op jit(solution)/shard_map/ppermute | solution.py:17
  25.2 299.3 %collective-permute-start.2 = (bf16[4,6,48,2048]{3,2,1,0:T(8,128)(2,1)}, bf16[4,6,48,2048]{3,2,1,0:T(8,128)(2,1)}, u32[]{:S(2)}, u32[]{:S(2)}) collective-permute-start(bf16[4,6,48,2048]{3,2,1,0:T(8,128)(2,1)} %get-tuple-element.40), channel_id=1, source_target_pairs={{0,8},{4,12},{8,16},{12,20},{16,24},{20,28},{1,9},{5,13},{9,17},{1... | collective-permute-start | bytes 14155784 | tf_op jit(solution)/shard_map/ppermute | solution.py:17
  34.0 298.1 %collective-permute-start.1 = (bf16[4,6,48,2048]{3,2,1,0:T(8,128)(2,1)}, bf16[4,6,48,2048]{3,2,1,0:T(8,128)(2,1)}, u32[]{:S(2)}, u32[]{:S(2)}) collective-permute-start(bf16[4,6,48,2048]{3,2,1,0:T(8,128)(2,1)} %get-tuple-element.40), channel_id=1, source_target_pairs={{4,0},{8,4},{12,8},{16,12},{20,16},{24,20},{28,24},{5,1},{9,5},{13... | collective-permute-start | bytes 14155784 | tf_op jit(solution)/shard_map/ppermute | solution.py:17
  43.7 5.3 copy-start.28
  49.0 7.1 copy-start.27
  122.9 306.3 %collective-permute-start = (bf16[4,6,48,2048]{3,2,1,0:T(8,128)(2,1)}, bf16[4,6,48,2048]{3,2,1,0:T(8,128)(2,1)}, u32[]{:S(2)}, u32[]{:S(2)}) collective-permute-start(bf16[4,6,48,2048]{3,2,1,0:T(8,128)(2,1)} %get-tuple-element.40), channel_id=1, source_target_pairs={{0,4},{4,8},{8,12},{12,16},{16,20},{20,24},{24,28},{1,5},{5,9},{9,... | collective-permute-start | bytes 14155784 | tf_op jit(solution)/shard_map/ppermute | solution.py:17
  242.2 241.9 %copy-start.3 = (f32[1,1152,64]{1,2,0:T(8,128)}, f32[1,1152,64]{1,2,0:T(8,128)S(1)}, u32[]{:S(2)}) copy-start(f32[1,1152,64]{1,2,0:T(8,128)S(1)} %copy.213) | copy-start | bytes 884740
  332.1 152.0 %copy-start.5 = (f32[1,1152,64]{1,2,0:T(8,128)}, f32[1,1152,64]{1,2,0:T(8,128)S(1)}, u32[]{:S(2)}) copy-start(f32[1,1152,64]{1,2,0:T(8,128)S(1)} %copy.212) | copy-start | bytes 884740
  475.4 186.8 %copy-start.43 = (f32[4,64]{1,0:T(4,128)}, f32[4,64]{1,0:T(4,128)S(1)}, u32[]{:S(2)}) copy-start(f32[4,64]{1,0:T(4,128)S(1)} %get-tuple-element.110) | copy-start | bytes 3076
  477.3 5.5 copy-start.52
  477.3 5.5 copy-start.55
  501.9 513.4 %all-reduce.34.cloned.1.call-start = ((), (), s32[]{:S(2)}) async-start(), calls=%async_computation.4 | async-start | bytes 15532032 | tf_op jit(solution)/shard_map/psum | solution.py:249
  509.1 44.6 %copy-start.49 = (f32[64]{0:T(128)S(1)}, f32[64]{0:T(128)}, u32[]{:S(2)}) copy-start(f32[64]{0:T(128)} %get-tuple-element.99) | copy-start | bytes 772
  591.3 5.7 copy-start.4
  591.3 5.7 copy-start.6
  625.0 8.2 copy-start.45
  625.0 8.2 copy-start.47
  633.2 9.4 copy-start.1
  634.6 49.3 %collective-permute-start.11 = (bf16[4,6,48,64]{3,2,1,0:T(8,128)(2,1)}, bf16[4,6,48,64]{3,2,1,0:T(8,128)(2,1)}, u32[]{:S(2)}, u32[]{:S(2)}) collective-permute-start(bf16[4,6,48,64]{3,2,1,0:T(8,128)(2,1)} %get-tuple-element.76), channel_id=1, source_target_pairs={{0,12},{4,16},{8,20},{12,24},{16,28},{1,13},{5,17},{9,21},{13,25},... | collective-permute-start | bytes 442376 | tf_op jit(solution)/shard_map/ppermute | solution.py:17
  636.6 51.1 %collective-permute-start.10 = (bf16[4,6,48,64]{3,2,1,0:T(8,128)(2,1)}, bf16[4,6,48,64]{3,2,1,0:T(8,128)(2,1)}, u32[]{:S(2)}, u32[]{:S(2)}) collective-permute-start(bf16[4,6,48,64]{3,2,1,0:T(8,128)(2,1)} %get-tuple-element.76), channel_id=1, source_target_pairs={{12,0},{16,4},{20,8},{24,12},{28,16},{13,1},{17,5},{21,9},{25,13},... | collective-permute-start | bytes 442376 | tf_op jit(solution)/shard_map/ppermute | solution.py:17
  637.9 52.1 %collective-permute-start.9 = (bf16[4,6,48,64]{3,2,1,0:T(8,128)(2,1)}, bf16[4,6,48,64]{3,2,1,0:T(8,128)(2,1)}, u32[]{:S(2)}, u32[]{:S(2)}) collective-permute-start(bf16[4,6,48,64]{3,2,1,0:T(8,128)(2,1)} %get-tuple-element.77), channel_id=1, source_target_pairs={{0,8},{4,12},{8,16},{12,20},{16,24},{20,28},{1,9},{5,13},{9,17},{1... | collective-permute-start | bytes 442376 | tf_op jit(solution)/shard_map/ppermute | solution.py:17
  639.9 52.5 %collective-permute-start.8 = (bf16[4,6,48,64]{3,2,1,0:T(8,128)(2,1)}, bf16[4,6,48,64]{3,2,1,0:T(8,128)(2,1)}, u32[]{:S(2)}, u32[]{:S(2)}) collective-permute-start(bf16[4,6,48,64]{3,2,1,0:T(8,128)(2,1)} %get-tuple-element.77), channel_id=1, source_target_pairs={{8,0},{12,4},{16,8},{20,12},{24,16},{28,20},{9,1},{13,5},{17,9},{2... | collective-permute-start | bytes 442376 | tf_op jit(solution)/shard_map/ppermute | solution.py:17
  650.0 44.8 %collective-permute-start.7 = (bf16[4,6,48,64]{3,2,1,0:T(8,128)(2,1)}, bf16[4,6,48,64]{3,2,1,0:T(8,128)(2,1)}, u32[]{:S(2)}, u32[]{:S(2)}) collective-permute-start(bf16[4,6,48,64]{3,2,1,0:T(8,128)(2,1)} %get-tuple-element.78), channel_id=1, source_target_pairs={{0,4},{4,8},{8,12},{12,16},{16,20},{20,24},{24,28},{1,5},{5,9},{9,... | collective-permute-start | bytes 442376 | tf_op jit(solution)/shard_map/ppermute | solution.py:17
  662.4 5.0 copy-start.65
  662.4 20.1 %copy-start.63 = (f32[64]{0:T(128)}, f32[64]{0:T(128)S(1)}, u32[]{:S(2)}) copy-start(f32[64]{0:T(128)S(1)} %get-tuple-element.17) | copy-start | bytes 772
  683.8 20.3 %collective-permute-start.6 = (bf16[4,6,48,64]{3,2,1,0:T(8,128)(2,1)}, bf16[4,6,48,64]{3,2,1,0:T(8,128)(2,1)S(1)}, u32[]{:S(2)}, u32[]{:S(2)}) collective-permute-start(bf16[4,6,48,64]{3,2,1,0:T(8,128)(2,1)} %get-tuple-element.78), channel_id=1, source_target_pairs={{4,0},{8,4},{12,8},{16,12},{20,16},{24,20},{28,24},{5,1},{9,5},{13... | collective-permute-start | bytes 442376 | tf_op jit(solution)/shard_map/ppermute | solution.py:17
  758.3 6.3 copy-start.16
  758.3 307.0 %reduce-scatter.5.cloned.1.call-start = ((), (), s32[]{:S(2)}) async-start(), calls=%async_computation.2 | async-start | bytes 5898240 | tf_op jit(solution)/shard_map/reduce_scatter | solution.py:245
  758.5 6.1 copy-start.20
  764.6 5.1 copy-start.15
  764.6 5.1 copy-start.21
  769.7 5.0 copy-start.14
  769.8 5.0 copy-start.22
  789.8 5.6 copy-start.13
  795.5 6.2 copy-start.12
  795.5 6.2 copy-start.26
  801.7 5.0 copy-start.11
  801.7 5.0 copy-start.24
  806.7 4.9 copy-start.10
  806.7 4.9 copy-start.23
  811.7 4.9 copy-start.25
  816.6 5.0 copy-start.8
  (41 other events, 81.4 us)
Sparse Core Ops, SparseCore 0:
  502.1 22.9 reduce-scatter.6
  758.4 256.8 all-reduce.33
  1018.4 46.8 reduce-scatter.4
where the time goes:
time: 1080 us; the launch traced here: 1070 us
  waiting for transfers between devices  444 us (41%)
  matrix products  178 us (16%)
  starting transfers between devices  146 us (14%)
  blocking collectives  109 us (10%)
  local copies, waits for them, and re-layouts  106 us (10%)
  other arithmetic  74.5 us (7%)
  between operations  15.1 us (1%)
    ppermute x12, waiting for transfers between devices, from_behind(): return lax.ppermute(block, axis, route)  232 us
    psum x1, waiting for transfers between devices, body(): lax.psum(g_point.astype(jnp.bfloat16), 'sp').astype(jnp.float32)  162 us
    ppermute x12, starting transfers between devices, from_behind(): return lax.ppermute(block, axis, route)  145 us
    dot_general x9, matrix products, body(): jnp.einsum('pt,tc->pc', spread, tap_weight_slice, preferred_element_type=...  70.7 us
    dot_general x9, matrix products, tap_partials(): jnp.einsum('pc,tc->pt', source.reshape(-1, channel_total), weight_taps.re...  45 us
    dot_general x9, matrix products, body(): jnp.einsum('pt,pc->tc', spread, flat_pix, preferred_element_type=jnp.floa...  39.9 us
    psum x1, blocking collectives, body(): lax.psum(own_pooled[:, None, :] * group_onehot[None, :, None], 'sp')  36.6 us
    reduce_scatter x1, waiting for transfers between devices, body(): lax.psum_scatter((input_term * pix_mask).astype(jnp.bfloat16), 'ch', scat...  33.9 us
  transfers between devices with their start and end apart: 15, of which 6 were waited for; matrix products, arithmetic and copies ran while one was open for 21% of the time, Pallas kernels for 0%

commit v1 on v0

--- a/solution.py
+++ b/solution.py
@@ -1,17 +1,314 @@
+import functools
+
 import jax
 import jax.numpy as jnp
 from jax import lax
+from jax.experimental import pallas as pl
+from jax.experimental.pallas import tpu as pltpu
 from jax.sharding import PartitionSpec as P
 
 BLOCKS = 8
-
-
+BRANCHES = 4
 epsilon = 1e-05
 dilation_factors = (1, 2, 3)
 highest_precision = lax.Precision.HIGHEST
+f32 = jnp.float32
+bf16 = jnp.bfloat16
+MIB = 1 << 20
+VMEM = pl.BlockSpec(memory_space=pltpu.VMEM)
+SMEM = pl.BlockSpec(memory_space=pltpu.SMEM)
+NT = (((1,), (1,)), ((), ()))
+NN = (((1,), (0,)), ((), ()))
+TN = (((0,), (0,)), ((), ()))
+
+
+def dot(a, b, dims):
+    return lax.dot_general(a, b, dims, preferred_element_type=f32)
+
+
+def params(mib=48, **kw):
+    return pltpu.CompilerParams(vmem_limit_bytes=mib * MIB, **kw)
+
+
+def cost(flops, nbytes):
+    return pl.CostEstimate(flops=int(flops), bytes_accessed=int(nbytes), transcendentals=0)
+
+
+def cell_mask(lim_ref, slabs, cols, width):
+    col = lax.broadcasted_iota(jnp.int32, (cols, width), 0)
+    return jnp.concatenate([(col < lim_ref[i]).astype(f32) for i in range(slabs)], axis=0)
+
+
+def column_ids(slabs, cols, width):
+    return lax.broadcasted_iota(jnp.int32, (slabs, cols, width), 1).reshape(slabs * cols, width)
+
+
+def from_left(a, d, col):
+    return jnp.where(col >= d, pltpu.roll(a, d, 0), 0.0)
+
+
+def from_right(a, d, col, cols):
+    return jnp.where(col < cols - d, pltpu.roll(a, a.shape[0] - d, 0), 0.0)
+
+
+def silu_parts(t):
+    s = 1.0 / (1.0 + jnp.exp(-t))
+    return s, t * s
+
+
+def slope(t, s):
+    return s * (1.0 + t * (1.0 - s))
+
+
+def column_sums(*rows):
+    sums = [jnp.sum(r, axis=0, keepdims=True) for r in rows]
+    width = sums[0].shape[1]
+    return jnp.concatenate(sums + [jnp.zeros((8 - len(sums), width), f32)], axis=0)
+
+
+def side_kernel(lim_ref, x_ref, wm_ref, wp_ref, *refs, steps, slabs, cols, rates):
+    outs, (wcat, acc) = refs[:6], refs[6:]
+    k = pl.program_id(0)
+    L = wm_ref.shape[3]
+    for j in range(3):
+        for v in range(3):
+            t = (j * 3 + v) * 2 * L
+            wcat[t : t + L] = wm_ref[j, 0, v]
+            wcat[t + L : t + 2 * L] = wp_ref[j, 0, v]
+
+    @pl.when(k == 0)
+    def _():
+        acc[...] = jnp.zeros_like(acc)
+
+    x = x_ref[...]
+    total = 18 * L
+    for n in range(0, total, 256):
+        e = min(n + 256, total)
+        acc[:, n:e] += dot(x, wcat[n:e], NT)
+
+    @pl.when(k == steps - 1)
+    def _():
+        cells = slabs * cols
+        half = cells // 2
+        mask = cell_mask(lim_ref, slabs, cols, 2 * L)
+        col = column_ids(slabs, cols, 2 * L)
+        low = lax.broadcasted_iota(jnp.int32, (half, 2 * L), 1) < L
+        for j in range(3):
+            a = [acc[:, (j * 3 + v) * 2 * L : (j * 3 + v + 1) * 2 * L] * mask for v in range(3)]
+            s = a[1] + from_left(a[0], rates[j], col) + from_right(a[2], rates[j], col, cols)
+            top, bottom = s[:half], s[half:]
+            outs[2 * j][...] = jnp.where(low, top, pltpu.roll(bottom, L, 1)).astype(bf16)
+            outs[2 * j + 1][...] = jnp.where(low, pltpu.roll(top, L, 1), bottom).astype(bf16)
+
+
+def centre_kernel(
+    lim_ref, x_ref, wc_ref, wpoint_ref, out_ref, sums_ref, wcat, acc, *, steps, slabs, cols, rates, images
+):
+    k = pl.program_id(0)
+    L = wpoint_ref.shape[0]
+    order = [None, (0, 1), (1, 1), (2, 1), (1, 0), (2, 0), (1, 2), (2, 2), (0, 0), (0, 2)]
+    for i, tap in enumerate(order):
+        wcat[i * L : (i + 1) * L] = wpoint_ref[...] if tap is None else wc_ref[tap[0], 0, tap[1]]
+
+    @pl.when(k == 0)
+    def _():
+        acc[...] = jnp.zeros_like(acc)
+
+    x = x_ref[...]
+    total = 10 * L
+    for n in range(0, total, 256):
+        e = min(n + 256, total)
+        acc[:, n:e] += dot(x, wcat[n:e], NT)
+
+    width = x_ref.shape[1]
+    cid = lax.broadcasted_iota(jnp.int32, (cols, width), 0)
+    per = slabs // images
+    sums = []
+    for image in range(images):
+        part = jnp.zeros((cols, width), f32)
+        for i in range(image * per, (image + 1) * per):
+            part += jnp.where(cid < lim_ref[i], x_ref[i * cols : (i + 1) * cols].astype(f32), 0.0)
+        sums.append(jnp.sum(part, axis=0, keepdims=True))
+    sums_ref[...] = jnp.concatenate(sums + [jnp.zeros((8 - images, width), f32)], axis=0)
+
+    @pl.when(k == steps - 1)
+    def _():
+        cells = slabs * cols
+        mask = cell_mask(lim_ref, slabs, cols, 2 * L)
+        col = column_ids(slabs, cols, 2 * L)
+        low = lax.broadcasted_iota(jnp.int32, (cells, 2 * L), 1) < L
+        b = [acc[:, i * 2 * L : (i + 1) * 2 * L] * mask for i in range(5)]
+        d0, d1, d2 = rates
+        t = jnp.where(low, from_left(b[4], d0, col), from_right(b[4], d0, col, cols))
+        out_ref[:, : 2 * L] = b[0] + jnp.where(low, 0.0, t + pltpu.roll(t, L, 1))
+        out_ref[:, 2 * L :] = (
+            b[1]
+            + jnp.where(low, from_left(b[2], d1, col), from_left(b[2], d2, col))
+            + jnp.where(low, from_right(b[3], d1, col, cols), from_right(b[3], d2, col, cols))
+        )
+
+
+def combine_kernel(lim_ref, centre_ref, *refs, slabs, cols):
+    halo, (conv_ref, send_ref, stat_ref) = refs[:6], refs[6:]
+    cells = slabs * cols
+    half = cells // 2
+    W = centre_ref.shape[1]
+    L = W // 4
+    h = [halo[2 * j][...].astype(f32) + halo[2 * j + 1][...].astype(f32) for j in range(3)]
+    turned = [pltpu.roll(a, L, 1) for a in h]
+    low = lax.broadcasted_iota(jnp.int32, (cells, 2 * L), 1) < L
+    h0 = jnp.concatenate([turned[0], h[0]], axis=0)
+    h1 = jnp.concatenate([h[1], turned[1]], axis=0)
+    h2 = jnp.concatenate([turned[2], h[2]], axis=0)
+    left = centre_ref[:, : 2 * L] + jnp.where(low, 0.0, h0)
+    right = centre_ref[:, 2 * L :] + jnp.where(low, h1, h2)
+    conv_ref[:, : 2 * L] = left
+    conv_ref[:, 2 * L :] = right
+    mask = cell_mask(lim_ref, slabs, cols, 2 * L)
+    own = lim_ref[0]
+    for i in range(1, slabs):
+        own = own + lim_ref[i]
+    own = jnp.maximum(own, 1).astype(f32)
+    for lo, part in ((0, left), (2 * L, right)):
+        s = jnp.sum(part * mask, axis=0, keepdims=True)
+        q = jnp.sum(part * part * mask, axis=0, keepdims=True)
+        local = s / own
+        send_ref[:, lo : lo + 2 * L] = (part - local).astype(bf16)
+        stat_ref[:, lo : lo + 2 * L] = jnp.concatenate([s, q, local, jnp.zeros((5, 2 * L), f32)], axis=0)
+
+
+def mix_kernel(
+    lim_ref, conv_ref, c1_ref, c2_ref, c3_ref, stat_ref, gain_ref, wbranch_ref, pool_ref, wpool_ref,
+    mixed_ref, act_ref, sums_ref, scratch, *, slabs, cols, images
+):
+    cells = slabs * cols
+    per = slabs // images
+    for d, ref in enumerate((conv_ref, c1_ref, c2_ref, c3_ref)):
+        mean, rstd, local = stat_ref[d, 0:1], stat_ref[d, 1:2], stat_ref[d, 2:3]
+        offset = mean if d == 0 else mean - local
+        scale = rstd * gain_ref[d, 0:1]
+        shift = gain_ref[d, 1:2]
+        dest = act_ref if d == 0 else scratch
+        width = ref.shape[1]
+        cid = lax.broadcasted_iota(jnp.int32, (cols, width), 0)
+        for i in range(slabs):
+            rows = slice(i * cols, (i + 1) * cols)
+            pre = (ref[rows].astype(f32) - offset) * scale + shift
+            _, act = silu_parts(pre)
+            dest[rows] = jnp.where(cid < lim_ref[i], act, 0.0).astype(bf16)
+        part = dot(dest[...], wbranch_ref[d], NN)
+        if d == 0:
+            mixed_ref[...] = part
+        else:
+            mixed_ref[...] += part
+    pooled = dot(pool_ref[0], wpool_ref[0], NN)
+    for d in range(1, 4):
+        pooled += dot(pool_ref[d], wpool_ref[d], NN)
+    F = mixed_ref.shape[1]
+    cid = lax.broadcasted_iota(jnp.int32, (cols, F), 0)
+    s = jnp.zeros((cols, F), f32)
+    q = jnp.zeros((cols, F), f32)
+    for i in range(slabs):
+        rows = slice(i * cols, (i + 1) * cols)
+        image = i // per
+        value = mixed_ref[rows] + jnp.where(cid < lim_ref[i], pooled[image : image + 1], 0.0)
+        mixed_ref[rows] = value
+        s += value
+        q += value * value
+    sums_ref[...] = column_sums(s, q)
+
+
+def final_kernel(lim_ref, mixed_ref, grad_ref, stat_ref, out_ref, dt_ref, sums_ref, *, slabs, cols):
+    F = mixed_ref.shape[1]
+    mean, rstd, gain, shift = (stat_ref[i : i + 1] for i in range(4))
+    cid = lax.broadcasted_iota(jnp.int32, (cols, F), 0)
+    s = jnp.zeros((cols, F), f32)
+    q = jnp.zeros((cols, F), f32)
+    for i in range(slabs):
+        rows = slice(i * cols, (i + 1) * cols)
+        valid = cid < lim_ref[i]
+        normed = (mixed_ref[rows] - mean) * rstd
+        pre = gain * normed + shift
+        sig, act = silu_parts(pre)
+        out_ref[rows] = jnp.where(valid, act, 0.0).astype(bf16)
+        dt = jnp.where(valid, grad_ref[rows].astype(f32) * slope(pre, sig), 0.0)
+        dt_ref[rows] = dt
+        s += dt
+        q += dt * normed
+    sums_ref[...] = column_sums(s, q)
+
+
+def branch_kernel(
+    lim_ref, mixed_ref, fdt_ref, fstat_ref, conv_ref, act_ref, stat_ref, wbranch_ref,
+    dt_ref, gproj_ref, image_ref, sums_ref, grad, *, slabs, cols, images
+):
+    F = mixed_ref.shape[1]
+    W = conv_ref.shape[1]
+    per = slabs // images
+    mean, rstd, scale, beta, gamma = (fstat_ref[i : i + 1] for i in range(5))
+    cid = lax.broadcasted_iota(jnp.int32, (cols, F), 0)
+    image_sums = []
+    for image in range(images):
+        total = jnp.zeros((cols, F), f32)
+        for i in range(image * per, (image + 1) * per):
+            rows = slice(i * cols, (i + 1) * cols)
+            normed = (mixed_ref[rows] - mean) * rstd
+            g = jnp.where(cid < lim_ref[i], scale * (fdt_ref[rows] - beta - normed * gamma), 0.0)
+            g = g.astype(bf16)
+            grad[rows] = g
+            total += g.astype(f32)
+        image_sums.append(jnp.sum(total, axis=0, keepdims=True))
+    image_ref[...] = jnp.concatenate(image_sums + [jnp.zeros((8 - images, F), f32)], axis=0)
+    dt_ref[...] = dot(grad[...], wbranch_ref[...], NT)
+    gproj_ref[...] = dot(act_ref[...], grad[...], TN)
+    bmean, brstd, bgain, bshift = (stat_ref[i : i + 1] for i in range(4))
+    cid = lax.broadcasted_iota(jnp.int32, (cols, W), 0)
+    s = jnp.zeros((cols, W), f32)
+    q = jnp.zeros((cols, W), f32)
+    for i in range(slabs):
+        rows = slice(i * cols, (i + 1) * cols)
+        normed = (conv_ref[rows] - bmean) * brstd
+        pre = bgain * normed + bshift
+        sig, _ = silu_parts(pre)
+        dt = jnp.where(cid < lim_ref[i], dt_ref[rows] * slope(pre, sig), 0.0)
+        dt_ref[rows] = dt
+        s += dt
+        q += dt * normed
+    sums_ref[...] = column_sums(s, q)
+
+
+def grad_kernel(lim_ref, dt_ref, conv_ref, stat_ref, cg_ref, *, slabs, cols):
+    W = conv_ref.shape[1]
+    mean, rstd, scale, beta, gamma = (stat_ref[i : i + 1] for i in range(5))
+    cid = lax.broadcasted_iota(jnp.int32, (cols, W), 0)
+    for i in range(slabs):
+        rows = slice(i * cols, (i + 1) * cols)
+        normed = (conv_ref[rows] - mean) * rstd
+        g = scale * (dt_ref[rows] - beta - normed * gamma)
+        cg_ref[rows] = jnp.where(cid < lim_ref[i], g, 0.0).astype(bf16)
+
+
+def grouped(pairs, size):
+    return [(g * BLOCKS + a, g * BLOCKS + b) for g in range(size // BLOCKS) for a, b in pairs]
 
 
 def from_behind(block, axis, distance):
+    size = lax.axis_size(axis)
+    pairs = [(i - distance, i) for i in range(BLOCKS) if 0 <= i - distance < BLOCKS]
+    return lax.ppermute(block, axis, grouped(pairs, size))
+
+
+def swap(block, axis, bits):
+    return lax.ppermute(block, axis, [(i, i ^ bits) for i in range(lax.axis_size(axis))])
+
+
+def sum_over_sp(x):
+    x = x + swap(x, "sp", 1)
+    parts = [swap(x, "sp", b) for b in (2, 4, 6)]
+    return x + parts[0] + parts[1] + parts[2]
+
+
+def plain_from_behind(block, axis, distance):
     devices = range(lax.axis_size(axis))
     route = [(i - distance, i) for i in devices if i - distance in devices]
     return lax.ppermute(block, axis, route)
@@ -34,11 +331,11 @@
 
 
 def move_features(values, shift_amount):
-    return from_behind(values, "sp", shift_amount)
+    return plain_from_behind(values, "sp", shift_amount)
 
 
 def shifted_gradients(values, shift_amount):
-    return from_behind(values, "sp", shift_amount)
+    return plain_from_behind(values, "sp", shift_amount)
 
 
 def tap_partials(source, weight_taps, dilation_rate):
@@ -57,7 +354,7 @@
     )
 
 
-def body(
+def plain_body(
     features, heights, widths, w_point, atrous_weight, w_pool, w_proj, bn_gains, bn_shifts, out_grad
 ):
     count_k, rows_dev, grid_width, channel_total = features.shape
@@ -256,6 +553,234 @@
     return (output, in_grad, g_point, g_atrous, g_pool, g_proj, g_gains, g_shifts)
 
 
+def body(
+    features, heights, widths, w_point, atrous_weight, w_pool, w_proj, bn_gains, bn_shifts, out_grad
+):
+    images, rows_dev, cols, C = features.shape
+    L = w_point.shape[0]
+    if lax.axis_size("sp") != BLOCKS or lax.axis_size("ch") != 4 or L != 64:
+        return plain_body(
+            features, heights, widths, w_point, atrous_weight, w_pool, w_proj, bn_gains, bn_shifts, out_grad
+        )
+    F = w_proj.shape[2]
+    W = BRANCHES * L
+    slabs = images * rows_dev
+    cells = slabs * cols
+    rates = tuple(rows_dev * f for f in dilation_factors)
+    block_id = lax.axis_index("sp")
+    own = lax.axis_index("ch")
+    h, w = heights[:, 0], widths[:, 0]
+    row_ids = block_id * rows_dev + jnp.arange(rows_dev, dtype=jnp.int32)
+    lim = jnp.where(row_ids[None, :] < h[:, None], w[:, None], 0).reshape(slabs)
+    own_count = (h * w).astype(f32)
+    n = jnp.sum(own_count)
+    x = features.reshape(cells, C)
+    og = out_grad.reshape(cells, F)
+
+    norms = jnp.concatenate([bn_gains, bn_shifts, jnp.zeros((4, L), f32)], axis=0)
+    wp = w_proj.reshape(5 * L, F)
+    norms_all = jnp.stack([norms] + [swap(norms, "ch", b) for b in (1, 2, 3)])
+    wp_all = jnp.stack([wp] + [swap(wp, "ch", b) for b in (1, 2, 3)])
+    wbranch_all, wpool_all = wp_all[:, :W], wp_all[:, W:]
+    natural = (own ^ jnp.arange(4))[:, None] == jnp.arange(4)[None, :]
+    final_par = jnp.sum(
+        jnp.where(natural[:, :, None, None], norms_all[None, :, (5, 11), :], 0.0), axis=1
+    )
+    final_gain, final_shift = final_par[:, 0].reshape(F), final_par[:, 1].reshape(F)
+
+    KT = 512
+    steps = C // KT
+    x_spec = pl.BlockSpec((cells, KT), lambda k: (0, k))
+    side = pl.pallas_call(
+        functools.partial(side_kernel, steps=steps, slabs=slabs, cols=cols, rates=rates),
+        grid=(steps,),
+        in_specs=[
+            SMEM,
+            x_spec,
+            pl.BlockSpec((3, 1, 3, L, KT), lambda k: (0, 0, 0, 0, k)),
+            pl.BlockSpec((3, 1, 3, L, KT), lambda k: (0, 2, 0, 0, k)),
+        ],
+        out_specs=[pl.BlockSpec((cells // 2, 2 * L), lambda k: (0, 0))] * 6,
+        out_shape=[jax.ShapeDtypeStruct((cells // 2, 2 * L), bf16)] * 6,
+        scratch_shapes=[pltpu.VMEM((18 * L, KT), bf16), pltpu.VMEM((cells, 18 * L), f32)],
+        compiler_params=params(),
+        cost_estimate=cost(2 * cells * C * 18 * L, 10e6),
+        name="side_taps",
+    )(lim, x, atrous_weight, atrous_weight)
+    halo = [from_behind(side[i], "sp", (1 - 2 * (i % 2)) * dilation_factors[i // 2]) for i in range(6)]
+    centre, sums = pl.pallas_call(
+        functools.partial(centre_kernel, steps=steps, slabs=slabs, cols=cols, rates=rates, images=images),
+        grid=(steps,),
+        in_specs=[
+            SMEM,
+            x_spec,
+            pl.BlockSpec((3, 1, 3, L, KT), lambda k: (0, 1, 0, 0, k)),
+            pl.BlockSpec((L, KT), lambda k: (0, k)),
+        ],
+        out_specs=[pl.BlockSpec((cells, W), lambda k: (0, 0)), pl.BlockSpec((8, KT), lambda k: (0, k))],
+        out_shape=[jax.ShapeDtypeStruct((cells, W), f32), jax.ShapeDtypeStruct((8, C), f32)],
+        scratch_shapes=[pltpu.VMEM((10 * L, KT), bf16), pltpu.VMEM((cells, 10 * L), f32)],
+        compiler_params=params(),
+        cost_estimate=cost(2 * cells * C * 10 * L, 8e6),
+        name="centre_taps",
+    )(lim, x, atrous_weight, w_point)
+    own_pooled = sums[:images] / own_count[:, None]
+    proj_part = lax.dot_general(own_pooled, w_pool.astype(f32), NT, precision=highest_precision)
+
+    conv, conv_send, stat = pl.pallas_call(
+        functools.partial(combine_kernel, slabs=slabs, cols=cols),
+        in_specs=[SMEM] + [VMEM] * 7,
+        out_specs=[VMEM] * 3,
+        out_shape=[
+            jax.ShapeDtypeStruct((cells, W), f32),
+            jax.ShapeDtypeStruct((cells, W), bf16),
+            jax.ShapeDtypeStruct((8, W), f32),
+        ],
+        compiler_params=params(),
+        cost_estimate=cost(2e6, 4e6),
+        name="combine_taps",
+    )(lim, centre, *halo)
+    conv_y = swap(conv_send, "ch", 2)
+    conv_core = swap(conv_send, "ch", 1)
+    conv_diag = swap(conv_y, "ch", 1)
+    tile = jnp.concatenate([stat[:4], jnp.pad(proj_part, ((0, 0), (0, W - L)))], axis=0)
+    tile = sum_over_sp(tile)
+    tile = jnp.concatenate([tile[:2], stat[2:3], tile[3:]], axis=0)
+    tiles = jnp.stack([tile] + [swap(tile, "ch", b) for b in (1, 2, 3)])
+    mean = tiles[:, 0] / n
+    rstd = lax.rsqrt(tiles[:, 1] / n - mean * mean + epsilon)
+    branch_stat = jnp.stack([mean, rstd, tiles[:, 2]], axis=1)
+    branch_par = jnp.stack([norms_all[:, :4].reshape(4, W), norms_all[:, 6:10].reshape(4, W)], axis=1)
+    projected = tiles[:, 4 : 4 + images, :L]
+    pool_mean = jnp.mean(projected, axis=1, keepdims=True)
+    pool_rstd = lax.rsqrt(
+        jnp.mean(projected * projected, axis=1, keepdims=True) - pool_mean * pool_mean + epsilon
+    )
+    pool_normed = (projected - pool_mean) * pool_rstd
+    pool_pre = norms_all[:, 4:5] * pool_normed + norms_all[:, 10:11]
+    pool_act = jax.nn.silu(pool_pre).astype(bf16)
+    pool_in = jnp.pad(pool_act, ((0, 0), (0, 8 - images), (0, 0)))
+
+    mixed, act, mixed_stat = pl.pallas_call(
+        functools.partial(mix_kernel, slabs=slabs, cols=cols, images=images),
+        in_specs=[SMEM] + [VMEM] * 9,
+        out_specs=[VMEM] * 3,
+        out_shape=[
+            jax.ShapeDtypeStruct((cells, F), f32),
+            jax.ShapeDtypeStruct((cells, W), bf16),
+            jax.ShapeDtypeStruct((8, F), f32),
+        ],
+        scratch_shapes=[pltpu.VMEM((cells, W), bf16)],
+        compiler_params=params(),
+        cost_estimate=cost(2 * cells * 4 * W * F, 6e6),
+        name="mix_branches",
+    )(lim, conv, conv_core, conv_y, conv_diag, branch_stat, branch_par, wbranch_all, pool_in, wpool_all)
+    total = sum_over_sp(mixed_stat)
+    fmean = total[0] / n
+    frstd = lax.rsqrt(total[1] / n - fmean * fmean + epsilon)
+    final_stat = jnp.stack([fmean, frstd, final_gain, final_shift])
+    out_all, fdt, fsums = pl.pallas_call(
+        functools.partial(final_kernel, slabs=slabs, cols=cols),
+        in_specs=[SMEM] + [VMEM] * 3,
+        out_specs=[VMEM] * 3,
+        out_shape=[
+            jax.ShapeDtypeStruct((cells, F), bf16),
+            jax.ShapeDtypeStruct((cells, F), f32),
+            jax.ShapeDtypeStruct((8, F), f32),
+        ],
+        compiler_params=params(),
+        cost_estimate=cost(2e6, 4e6),
+        name="final_norm",
+    )(lim, mixed, og, final_stat)
+    ftotal = sum_over_sp(fsums)
+    final_beta, final_gamma = ftotal[0], ftotal[1]
+    fgrad_stat = jnp.stack([fmean, frstd, frstd * final_gain, final_beta / n, final_gamma / n])
+    own_gain, own_shift = branch_par[0, 0], branch_par[0, 1]
+    own_mean, own_rstd = branch_stat[0, 0], branch_stat[0, 1]
+    dt, gproj, image_sums, bsums = pl.pallas_call(
+        functools.partial(branch_kernel, slabs=slabs, cols=cols, images=images),
+        in_specs=[SMEM] + [VMEM] * 7,
+        out_specs=[VMEM] * 4,
+        out_shape=[
+            jax.ShapeDtypeStruct((cells, W), f32),
+            jax.ShapeDtypeStruct((W, F), f32),
+            jax.ShapeDtypeStruct((8, F), f32),
+            jax.ShapeDtypeStruct((8, W), f32),
+        ],
+        scratch_shapes=[pltpu.VMEM((cells, F), bf16)],
+        compiler_params=params(),
+        cost_estimate=cost(4 * cells * W * F, 8e6),
+        name="branch_grads",
+    )(
+        lim, mixed, fdt, fgrad_stat, conv, act,
+        jnp.stack([own_mean, own_rstd, own_gain, own_shift]), wp[:W],
+    )
+    image_sums = image_sums[:images]
+    pool_part = lax.dot_general(image_sums, w_proj[4].astype(f32), NT, precision=highest_precision)
+    gproj_pool = lax.dot_general(pool_act[0].astype(f32), image_sums, TN, precision=highest_precision)
+    btile = sum_over_sp(
+        jnp.concatenate([bsums[:4], jnp.pad(pool_part, ((0, 0), (0, W - L)))], axis=0)
+    )
+    branch_beta, branch_gamma = btile[0], btile[1]
+    cg = pl.pallas_call(
+        functools.partial(grad_kernel, slabs=slabs, cols=cols),
+        in_specs=[SMEM] + [VMEM] * 3,
+        out_specs=VMEM,
+        out_shape=jax.ShapeDtypeStruct((cells, W), bf16),
+        compiler_params=params(),
+        cost_estimate=cost(2e6, 4e6),
+        name="conv_grads",
+    )(lim, dt, conv, jnp.stack([own_mean, own_rstd, own_rstd * own_gain, branch_beta / n, branch_gamma / n]))
+    pool_dt = btile[4 : 4 + images, :L] * silu_slope(pool_pre[0])
+    pool_beta = jnp.sum(pool_dt, axis=0)
+    pool_gamma = jnp.sum(pool_dt * pool_normed[0], axis=0)
+    proj_grad = (
+        pool_rstd[0] * bn_gains[4] * (pool_dt - pool_beta / images - pool_normed[0] * pool_gamma / images)
+    )
+    g_gains = jnp.concatenate([branch_gamma.reshape(4, L), pool_gamma[None],
+        lax.dynamic_slice_in_dim(final_gamma, own * L, L)[None]], axis=0)
+    g_shifts = jnp.concatenate([branch_beta.reshape(4, L), pool_beta[None],
+        lax.dynamic_slice_in_dim(final_beta, own * L, L)[None]], axis=0)
+    output = lax.dynamic_slice_in_dim(out_all, own * L, L, 1).reshape(images, rows_dev, cols, L)
+    g_proj = jnp.concatenate([gproj.reshape(4, L, F), gproj_pool[None]], axis=0)
+    pooled_grad = (
+        jnp.einsum("kf,fc->kc", proj_grad, w_pool.astype(f32), precision=highest_precision)
+        / own_count[:, None]
+    )
+    g_pool = jnp.einsum("kf,kc->fc", proj_grad, own_pooled, precision=highest_precision)
+    col_ids = jnp.arange(cols, dtype=jnp.int32)
+    pix_mask = (col_ids[None, :] < lim[:, None]).astype(f32).reshape(images, rows_dev, cols, 1)
+    flat_pix = (features * pix_mask.astype(bf16)).reshape(cells, C)
+    grads = [cg[:, i * L : (i + 1) * L].reshape(images, rows_dev, cols, L) for i in range(4)]
+    point_grad = grads[0].reshape(cells, L)
+    g_point = jnp.einsum("pf,pc->fc", point_grad, flat_pix, preferred_element_type=f32)
+    input_term = jnp.einsum("pf,fc->pc", point_grad, w_point, preferred_element_type=f32)
+    input_term = input_term.reshape(images, rows_dev, cols, C) + pooled_grad[:, None, None, :]
+    atrous_list = []
+    for j, factor in enumerate(dilation_factors):
+        tap_list = []
+        for u in range(3):
+            g = grads[j + 1] if u == 1 else from_behind(grads[j + 1], "sp", (u - 1) * factor)
+            spread = jnp.stack(
+                [shift_cols(g, rates[j]), g, shift_cols(g, -rates[j])], axis=3
+            ).reshape(cells, 3 * L)
+            tap_list.append(
+                jnp.einsum("pt,pc->tc", spread, flat_pix, preferred_element_type=f32).reshape(3, L, C)
+            )
+            input_term = input_term + jnp.einsum(
+                "pt,tc->pc", spread, atrous_weight[j, u].reshape(3 * L, C), preferred_element_type=f32
+            ).reshape(images, rows_dev, cols, C)
+        atrous_list.append(jnp.stack(tap_list))
+    g_atrous = jnp.stack(atrous_list)
+    in_grad = lax.psum_scatter(
+        (input_term * pix_mask).astype(bf16), "ch", scatter_dimension=3, tiled=True
+    )
+    g_point, g_atrous, g_proj, g_pool = (
+        lax.psum(t.astype(bf16), "sp").astype(f32) for t in (g_point, g_atrous, g_proj, g_pool)
+    )
+    return (output, in_grad, g_point, g_atrous, g_pool, g_proj, g_gains, g_shifts)
+
+
 def solution(mesh):
     placed = (
         P(None, "sp", None, None),

time: 1080 us -> 583 us (0.54)
  waiting for transfers between devices: 444 us -> 184 us
  blocking collectives: 109 us -> 0 us
  starting transfers between devices: 146 us -> 71.2 us
  matrix products: 178 us -> 111 us
  Pallas kernels: 0 us -> 26.9 us
  other arithmetic: 74.5 us -> 51.8 us
    ppermute x12 -> x40, waiting for transfers between devices: 232 us -> 17.1 us  [the longest x28 15.5 us: swap(): lax.ppermute(block, axis, [(i, i ^ bits) for i in range(lax.axis_size(axi...]
    psum x4 -> x0, blocking collectives: 96.8 us -> none  [the longest x1 36.6 us: body(): lax.psum(own_pooled[:, None, :] * group_onehot[None, :, None], 'sp')]
    ppermute x12 -> x40, starting transfers between devices: 145 us -> 71.1 us  [the longest x12 36.6 us: from_behind(): return lax.ppermute(block, axis, grouped(pairs, size))]
    dot_general x36 -> x25, matrix products: 178 us -> 111 us  [the longest x9 71.2 us: body(): jnp.einsum('pt,tc->pc', spread, atrous_weight[j, u].reshape(3 * L, C), pr...]
    reduce_scatter x1, waiting for transfers between devices: 33.9 us -> 0.01 us  [body(): lax.psum_scatter((input_term * pix_mask).astype(bf16), 'ch', scatter_dime...]
    pallas_call x0 -> x7, Pallas kernels: none -> 26.9 us  [the longest x1 10.9 us: body(): pl.pallas_call(functools.partial(side_kernel, steps=steps, slabs=slabs, c...]
    unnamed x4 -> x2, waiting for transfers between devices: 16 us -> 0.03 us
    all_gather x1 -> x0, blocking collectives: 12.4 us -> none  [body(): lax.all_gather(mixed_grad, 'ch', axis=3, tiled=True)]
  transfers between devices with their start and end apart: 15 -> 42, of which waited for: 6 -> 16; matrix products, arithmetic and copies ran while one was open for 21% -> 38% of each run, Pallas kernels for 0% -> 3%
where the time goes in v1:
time: 583 us; the launch traced here: 575 us
  waiting for transfers between devices  184 us (32%)
  local copies, waits for them, and re-layouts  114 us (20%)
  matrix products  111 us (19%)
  starting transfers between devices  71.2 us (12%)
  other arithmetic  51.8 us (9%)
  Pallas kernels  26.9 us (5%)
  between operations  16.7 us (3%)
    psum x1, waiting for transfers between devices, body(): lax.psum(t.astype(bf16), 'sp').astype(f32)  167 us
    dot_general x9, matrix products, body(): jnp.einsum('pt,tc->pc', spread, atrous_weight[j, u].reshape(3 * L, C), pr...  71.2 us
    ppermute x12, starting transfers between devices, from_behind(): return lax.ppermute(block, axis, grouped(pairs, size))  36.6 us
    ppermute x28, starting transfers between devices, swap(): lax.ppermute(block, axis, [(i, i ^ bits) for i in range(lax.axis_size(axi...  34.5 us
    dot_general x9, matrix products, body(): jnp.einsum('pt,pc->tc', spread, flat_pix, preferred_element_type=f32)  26 us
    unnamed x168, local copies, waits for them, and re-layouts  23.5 us
    another operation x18, local copies, waits for them, and re-layouts, body(): jnp.stack([shift_cols(g, rates[j]), g, shift_cols(g, -rates[j])], axis=3)  22.9 us
    reshape x9, local copies, waits for them, and re-layouts, body(): spread = jnp.stack([shift_cols(g, rates[j]), g, shift_cols(g, -rates[j])]...  19.7 us
  transfers between devices with their start and end apart: 42, of which 16 were waited for; matrix products, arithmetic and copies ran while one was open for 38% of the time, Pallas kernels for 3%

profile of v1, /device:TPU:0, one launch (start us, length us, event | category | flops | bytes accessed | tf_op | source)
XLA Modules:
  0.0 574.9 jit_solution(602866292924594974)
XLA Ops:
  8.9 2.4 collective-permute-start.18
  12.8 2.3 copy-done.2
  15.2 10.9 %side_taps.1 = (bf16[576,128]{1,0:T(8,128)(2,1)}, bf16[576,128]{1,0:T(8,128)(2,1)}, bf16[576,128]{1,0:T(8,128)(2,1)}, bf16[576,128]{1,0:T(8,128)(2,1)S(1)}, bf16...) custom-call(s32[24]{0:T(128)S(1)} %select_n.25.lim_ref, bf16[1152,2048]{1,0:T(8,128)(2,1)S(1)} %bitcast.247, ...), custom_call_target="tpu_custom_call" | custom-call | flops 5435817984 | bytes 10000000 | tf_op jit(solution)/shard_map/side_taps/pallas_call | solution.py:594
  26.1 3.6 collective-permute-start
  32.5 3.0 fusion.48
  35.6 8.0 %centre_taps.1 = (f32[1152,256]{1,0:T(8,128)S(1)}, f32[8,2048]{1,0:T(8,128)S(1)}) custom-call(s32[24]{0:T(128)S(1)} %select_n.25.lim_ref, bf16[1152,2048]{1,0:T(8,128)(2,1)} %bitcast.246, bf16[3,3,3,64,2048]{4,3,2,1,0:T(8,128)(2,1)} %wp_ref.1, bf16[64,2048]{1,0:T(8,128)(2,1)S(1)} %copy-done.8), custom_call_target="tpu_custom_call" | custom-call | flops 3019898880 | bytes 8000000 | tf_op jit(solution)/shard_map/centre_taps/pallas_call | solution.py:611
  43.7 2.6 broadcast_multiply_fusion
  49.2 5.5 collective-permute-start.2
  56.0 4.6 collective-permute-start.4
  83.2 3.4 collective-permute-start.9
  92.1 3.3 collective-permute-start.12
  106.9 2.7 mix_branches.1
  114.2 4.3 collective-permute-start.25
  120.1 2.9 collective-permute-done.24
  133.9 2.4 collective-permute-start.27
  150.7 2.6 collective-permute-start.33
  162.3 4.7 collective-permute-start.39
  168.3 4.0 collective-permute-start.35
  192.4 4.2 convolution_convert_fusion.10
  196.6 4.5 fusion.7
  201.1 4.5 fusion.4
  205.6 2.1 fusion.1
  210.0 5.9 %collective-permute-start.37 = (bf16[4,6,48,64]{3,2,1,0:T(8,128)(2,1)S(1)}, bf16[4,6,48,64]{3,2,1,0:T(8,128)(2,1)S(1)}, u32[]{:S(2)}, u32[]{:S(2)}) collective-permute-start(bf16[4,6,48,64]{3,2,1,0:T(8,128)(2,1)S(1)} %bitcast.281), channel_id=1, source_target_pairs={{0,8},{4,12},{8,16},{12,20},{16,24},{20,28},{1,9},{5,13},{9,17},{1... | collective-permute-start | bytes 442376 | tf_op jit(solution)/shard_map/ppermute | solution.py:298
  237.7 2.9 copy.99
  240.7 3.4 reshape.326
  246.1 3.0 copy.101
  249.1 3.4 reshape.330
  257.7 3.4 reshape.338
  267.2 3.8 reshape.342
  273.1 3.8 fusion.8
  276.9 3.7 fusion.6
  280.6 3.6 fusion.5
  289.5 3.4 pad_maximum_fusion
  292.9 5.1 fusion.29
  298.0 5.4 fusion.57
  303.5 5.0 fusion.54
  308.5 5.1 fusion.60
  316.7 2.6 dot_general.133
  319.3 2.6 dot_general.137
  323.4 2.6 dot_general.149
  326.1 6.1 %fusion.59 = f32[4,6,48,2048]{3,2,1,0:T(8,128)} fusion(bf16[4,6,48,192]{3,2,1,0:T(8,128)(2,1)} %dot_general.145, bf16[192,2048,1,1]{1,0,3,2:T(8,128)(2,1)S(1)} %bitcast.270), kind=kOutput, calls=%fused_computation.176 | convolution fusion | flops 905969664 | bytes 10665984 | tf_op jit(solution)/shard_map/pt,tc->pc/dot_general | solution.py:770
  332.2 5.0 fusion.58
  337.2 4.9 fusion.56
  342.1 4.9 fusion.55
  347.1 5.0 fusion.53
  352.1 29.7 %multiply_convert_fusion = bf16[4,6,48,2048]{3,2,1,0:T(8,128)(2,1)} fusion(f32[4,6,48,2048]{3,2,1,0:T(8,128)} %fusion.60, f32[4,6,48,2048]{3,2,1,0:T(8,128)} %fusion.59, f32[4,6,48,2048]{3,2,1,0:T(8,128)} %fusion.58, f32[4,6,48,2048]{3,2,1,0:T(8,128)} %fusion.57, f32[4,6,48,2048]{3,2,1,0:T(8,128)} %fusion.56, f32[4,6,48,2048]{3,2,1,0:T(8,128)} %fusion.55, ...), kind=kOutput, calls=%fused_computation.1 | convolution fusion | flops 934281216 | bytes 90919424 | tf_op jit(solution)/shard_map/pt,tc->pc/dot_general | solution.py:770
  385.2 166.8 %all-reduce.15.cloned.1.call-done = (bf16[64,2048]{1,0:T(8,128)(2,1)}, bf16[3,3,3,64,2048]{4,3,2,1,0:T(8,128)(2,1)}, bf16[64,2048]{1,0:T(8,128)(2,1)}, bf16[5,64,256]{2,1,0:T(8,128)(2,1)}) async-done(((bf16[64,2048]{1,0:T(8,128)(2,1)}, bf16[3,3,3,64,2048]{4,3,2,1,0:T(8,128)(2,1)}, bf16[64,2048]{1,0:T(8,128)(2,1)}, bf16[5,64,256]{2,1,0:T(8,128)(2,1)}), (bf16[64,2048]{1,0:T(8,128)(2,1)}, ...) | async-done | bytes 7766032 | tf_op jit(solution)/shard_map/psum | solution.py:779
  557.2 10.1 %convert_element_type.89 = f32[3,3,3,64,2048]{4,3,2,1,0:T(8,128)} convert(bf16[3,3,3,64,2048]{4,3,2,1,0:T(8,128)(2,1)} %get-tuple-element.59) | non-fusion elementwise | flops 3538944 | bytes 21233664 | tf_op jit(solution)/shard_map/convert_element_type | solution.py:779
  (380 shorter events, 168.5 us)
Async XLA Ops:
  8.0 38.2 %copy-start = (bf16[64,2048]{1,0:T(8,128)(2,1)S(1)}, bf16[64,2048]{1,0:T(8,128)(2,1)}, u32[]{:S(2)}) copy-start(bf16[64,2048]{1,0:T(8,128)(2,1)} %param.16) | copy-start | bytes 786436
  8.0 544.0 %all-reduce.15.cloned.1.call-start = ((), (), s32[]{:S(2)}) async-start(), calls=%async_computation.2 | async-start | bytes 15532032 | tf_op jit(solution)/shard_map/psum | solution.py:779
  8.9 40.2 %collective-permute-start.18 = (f32[16,64]{1,0:T(8,128)S(1)}, f32[16,64]{1,0:T(8,128)S(1)}, u32[]{:S(2)}, u32[]{:S(2)}) collective-permute-start(f32[16,64]{1,0:T(8,128)S(1)} %maximum_maximum_fusion), channel_id=1, source_target_pairs={{0,3},{1,2},{2,1},{3,0},{4,7},{5,6},{6,5},{7,4},{8,11},{9,10},{10,... | collective-permute-start | bytes 12296 | tf_op jit(solution)/shard_map/ppermute | solution.py:302
  11.3 43.4 %collective-permute-start.17 = (f32[16,64]{1,0:T(8,128)S(1)}, f32[16,64]{1,0:T(8,128)S(1)}, u32[]{:S(2)}, u32[]{:S(2)}) collective-permute-start(f32[16,64]{1,0:T(8,128)S(1)} %maximum_maximum_fusion), channel_id=1, source_target_pairs={{0,2},{1,3},{2,0},{3,1},{4,6},{5,7},{6,4},{7,5},{8,10},{9,11},{10,... | collective-permute-start | bytes 12296 | tf_op jit(solution)/shard_map/ppermute | solution.py:302
  12.0 44.0 %collective-permute-start.16 = (f32[16,64]{1,0:T(8,128)S(1)}, f32[16,64]{1,0:T(8,128)S(1)}, u32[]{:S(2)}, u32[]{:S(2)}) collective-permute-start(f32[16,64]{1,0:T(8,128)S(1)} %maximum_maximum_fusion), channel_id=1, source_target_pairs={{0,1},{1,0},{2,3},{3,2},{4,5},{5,4},{6,7},{7,6},{8,9},{9,8},{10,11... | collective-permute-start | bytes 12296 | tf_op jit(solution)/shard_map/ppermute | solution.py:302
  26.1 37.1 %collective-permute-start = (bf16[576,128]{1,0:T(8,128)(2,1)}, bf16[576,128]{1,0:T(8,128)(2,1)S(1)}, u32[]{:S(2)}, u32[]{:S(2)}) collective-permute-start(bf16[576,128]{1,0:T(8,128)(2,1)} %get-tuple-element.30), channel_id=1, source_target_pairs={{0,4},{4,8},{8,12},{12,16},{16,20},{20,24},{24,28},{1,5},{5,9},{9,... | collective-permute-start | bytes 442376 | tf_op jit(solution)/shard_map/ppermute | solution.py:298
  29.7 40.1 %collective-permute-start.1 = (bf16[576,128]{1,0:T(8,128)(2,1)}, bf16[576,128]{1,0:T(8,128)(2,1)S(1)}, u32[]{:S(2)}, u32[]{:S(2)}) collective-permute-start(bf16[576,128]{1,0:T(8,128)(2,1)} %get-tuple-element.31), channel_id=1, source_target_pairs={{4,0},{8,4},{12,8},{16,12},{20,16},{24,20},{28,24},{5,1},{9,5},{13... | collective-permute-start | bytes 442376 | tf_op jit(solution)/shard_map/ppermute | solution.py:298
  49.2 21.4 %collective-permute-start.2 = (bf16[576,128]{1,0:T(8,128)(2,1)}, bf16[576,128]{1,0:T(8,128)(2,1)S(1)}, u32[]{:S(2)}, u32[]{:S(2)}) collective-permute-start(bf16[576,128]{1,0:T(8,128)(2,1)} %get-tuple-element.32), channel_id=1, source_target_pairs={{0,8},{4,12},{8,16},{12,20},{16,24},{20,28},{1,9},{5,13},{9,17},{1... | collective-permute-start | bytes 442376 | tf_op jit(solution)/shard_map/ppermute | solution.py:298
  54.7 18.0 %collective-permute-start.3 = (bf16[576,128]{1,0:T(8,128)(2,1)S(1)}, bf16[576,128]{1,0:T(8,128)(2,1)S(1)}, u32[]{:S(2)}, u32[]{:S(2)}) collective-permute-start(bf16[576,128]{1,0:T(8,128)(2,1)S(1)} %get-tuple-element.33), channel_id=1, source_target_pairs={{8,0},{12,4},{16,8},{20,12},{24,16},{28,20},{9,1},{13,5},{17,9},{2... | collective-permute-start | bytes 442376 | tf_op jit(solution)/shard_map/ppermute | solution.py:298
  56.0 17.7 %collective-permute-start.4 = (bf16[576,128]{1,0:T(8,128)(2,1)S(1)}, bf16[576,128]{1,0:T(8,128)(2,1)S(1)}, u32[]{:S(2)}, u32[]{:S(2)}) collective-permute-start(bf16[576,128]{1,0:T(8,128)(2,1)S(1)} %get-tuple-element.34), channel_id=1, source_target_pairs={{0,12},{4,16},{8,20},{12,24},{16,28},{1,13},{5,17},{9,21},{13,25},... | collective-permute-start | bytes 442376 | tf_op jit(solution)/shard_map/ppermute | solution.py:298
  61.9 63.0 %copy-start.9 = (bf16[4,6,48,256]{3,2,1,0:T(8,128)(2,1)S(1)}, bf16[4,6,48,256]{3,2,1,0:T(8,128)(2,1)}, u32[]{:S(2)}) copy-start(bf16[4,6,48,256]{3,2,1,0:T(8,128)(2,1)} %param.20) | copy-start | bytes 1769476
  63.9 10.5 %collective-permute-start.5 = (bf16[576,128]{1,0:T(8,128)(2,1)S(1)}, bf16[576,128]{1,0:T(8,128)(2,1)S(1)}, u32[]{:S(2)}, u32[]{:S(2)}) collective-permute-start(bf16[576,128]{1,0:T(8,128)(2,1)S(1)} %get-tuple-element.35), channel_id=1, source_target_pairs={{12,0},{16,4},{20,8},{24,12},{28,16},{13,1},{17,5},{21,9},{25,13},... | collective-permute-start | bytes 442376 | tf_op jit(solution)/shard_map/ppermute | solution.py:298
  70.5 21.5 %collective-permute-start.21 = (bf16[320,256]{1,0:T(8,128)(2,1)}, bf16[320,256]{1,0:T(8,128)(2,1)}, u32[]{:S(2)}, u32[]{:S(2)}) collective-permute-start(bf16[320,256]{1,0:T(8,128)(2,1)} %bitcast.291), channel_id=1, source_target_pairs={{0,3},{1,2},{2,1},{3,0},{4,7},{5,6},{6,5},{7,4},{8,11},{9,10},{10,... | collective-permute-start | bytes 491528 | tf_op jit(solution)/shard_map/ppermute | solution.py:302
  71.2 24.1 %collective-permute-start.20 = (bf16[320,256]{1,0:T(8,128)(2,1)}, bf16[320,256]{1,0:T(8,128)(2,1)}, u32[]{:S(2)}, u32[]{:S(2)}) collective-permute-start(bf16[320,256]{1,0:T(8,128)(2,1)} %bitcast.292), channel_id=1, source_target_pairs={{0,2},{1,3},{2,0},{3,1},{4,6},{5,7},{6,4},{7,5},{8,10},{9,11},{10,... | collective-permute-start | bytes 491528 | tf_op jit(solution)/shard_map/ppermute | solution.py:302
  73.4 22.0 %collective-permute-start.19 = (bf16[320,256]{1,0:T(8,128)(2,1)}, bf16[320,256]{1,0:T(8,128)(2,1)}, u32[]{:S(2)}, u32[]{:S(2)}) collective-permute-start(bf16[320,256]{1,0:T(8,128)(2,1)} %bitcast.293), channel_id=1, source_target_pairs={{0,1},{1,0},{2,3},{3,2},{4,5},{5,4},{6,7},{7,6},{8,9},{9,8},{10,11... | collective-permute-start | bytes 491528 | tf_op jit(solution)/shard_map/ppermute | solution.py:302
  83.2 8.2 %collective-permute-start.9 = (f32[8,256]{1,0:T(8,128)S(1)}, f32[8,256]{1,0:T(8,128)S(1)}, u32[]{:S(2)}, u32[]{:S(2)}) collective-permute-start(f32[8,256]{1,0:T(8,128)S(1)} %select_maximum_fusion.4), channel_id=1, source_target_pairs={{0,4},{4,0},{8,12},{12,8},{16,20},{20,16},{24,28},{28,24},{1,5},{5... | collective-permute-start | bytes 24584 | tf_op jit(solution)/shard_map/ppermute | solution.py:302
  89.9 33.1 %copy-start.60 = (f32[1,256]{1,0:T(1,128)S(1)}, f32[1,256]{1,0:T(1,128)}, u32[]{:S(2)}) copy-start(f32[1,256]{1,0:T(1,128)} %stack_reshape_squeeze.6) | copy-start | bytes 3076
  89.9 34.4 %copy-start.69 = (f32[1,256]{1,0:T(1,128)S(1)}, f32[1,256]{1,0:T(1,128)}, u32[]{:S(2)}) copy-start(f32[1,256]{1,0:T(1,128)} %stack_reshape_squeeze.7) | copy-start | bytes 3076
  89.9 14.8 %collective-permute-start.7 = (bf16[1152,256]{1,0:T(8,128)(2,1)}, bf16[1152,256]{1,0:T(8,128)(2,1)S(1)}, u32[]{:S(2)}, u32[]{:S(2)}) collective-permute-start(bf16[1152,256]{1,0:T(8,128)(2,1)} %copy-done.27), channel_id=1, source_target_pairs={{0,2},{1,3},{2,0},{3,1},{4,6},{5,7},{6,4},{7,5},{8,10},{9,11},{10,... | collective-permute-start | bytes 1769480 | tf_op jit(solution)/shard_map/ppermute | solution.py:302
  91.4 15.5 %collective-permute-start.6 = (bf16[1152,256]{1,0:T(8,128)(2,1)}, bf16[1152,256]{1,0:T(8,128)(2,1)S(1)}, u32[]{:S(2)}, u32[]{:S(2)}) collective-permute-start(bf16[1152,256]{1,0:T(8,128)(2,1)} %copy-done.27), channel_id=1, source_target_pairs={{0,1},{1,0},{2,3},{3,2},{4,5},{5,4},{6,7},{7,6},{8,9},{9,8},{10,11... | collective-permute-start | bytes 1769480 | tf_op jit(solution)/shard_map/ppermute | solution.py:302
  92.1 5.7 collective-permute-start.12
  95.3 4.6 collective-permute-start.11
  95.4 4.5 collective-permute-start.10
  99.9 3.6 collective-permute-start.15
  100.0 4.7 collective-permute-start.14
  100.7 4.0 collective-permute-start.13
  104.8 2.1 collective-permute-start.8
  110.5 3.7 collective-permute-start.22
  114.2 5.9 %collective-permute-start.25 = (f32[8,256]{1,0:T(8,128)S(1)}, f32[8,256]{1,0:T(8,128)S(1)}, u32[]{:S(2)}, u32[]{:S(2)}) collective-permute-start(f32[8,256]{1,0:T(8,128)S(1)} %add.205), channel_id=1, source_target_pairs={{0,24},{4,28},{8,16},{12,20},{16,8},{20,12},{24,0},{28,4},{1,25},{... | collective-permute-start | bytes 24584 | tf_op jit(solution)/shard_map/ppermute | solution.py:302
  118.4 4.5 collective-permute-start.24
  118.5 4.5 collective-permute-start.23
  119.0 20.2 %copy-start.61 = (f32[1,256]{1,0:T(1,128)}, f32[1,256]{1,0:T(1,128)S(1)}, u32[]{:S(2)}) copy-start(f32[1,256]{1,0:T(1,128)S(1)} %get-tuple-element.118) | copy-start | bytes 3076
  119.0 20.2 %copy-start.63 = (f32[1,256]{1,0:T(1,128)}, f32[1,256]{1,0:T(1,128)S(1)}, u32[]{:S(2)}) copy-start(f32[1,256]{1,0:T(1,128)S(1)} %get-tuple-element.119) | copy-start | bytes 3076
  128.2 3.7 collective-permute-start.26
  131.9 5.4 collective-permute-start.29
  133.3 4.6 collective-permute-start.28
  133.9 4.1 collective-permute-start.27
  146.9 3.7 collective-permute-start.30
  150.7 5.5 collective-permute-start.33
  153.2 4.6 collective-permute-start.32
  154.1 3.7 collective-permute-start.31
  162.3 100.8 %collective-permute-start.39 = (bf16[4,6,48,64]{3,2,1,0:T(8,128)(2,1)}, bf16[4,6,48,64]{3,2,1,0:T(8,128)(2,1)}, u32[]{:S(2)}, u32[]{:S(2)}) collective-permute-start(bf16[4,6,48,64]{3,2,1,0:T(8,128)(2,1)} %bitcast.71), channel_id=1, source_target_pairs={{0,12},{4,16},{8,20},{12,24},{16,28},{1,13},{5,17},{9,21},{13,25},... | collective-permute-start | bytes 442376 | tf_op jit(solution)/shard_map/ppermute | solution.py:298
  167.0 60.8 %collective-permute-start.38 = (bf16[4,6,48,64]{3,2,1,0:T(8,128)(2,1)}, bf16[4,6,48,64]{3,2,1,0:T(8,128)(2,1)}, u32[]{:S(2)}, u32[]{:S(2)}) collective-permute-start(bf16[4,6,48,64]{3,2,1,0:T(8,128)(2,1)} %bitcast.71), channel_id=1, source_target_pairs={{12,0},{16,4},{20,8},{24,12},{28,16},{13,1},{17,5},{21,9},{25,13},... | collective-permute-start | bytes 442376 | tf_op jit(solution)/shard_map/ppermute | solution.py:298
  168.3 56.2 %collective-permute-start.35 = (bf16[4,6,48,64]{3,2,1,0:T(8,128)(2,1)S(1)}, bf16[4,6,48,64]{3,2,1,0:T(8,128)(2,1)}, u32[]{:S(2)}, u32[]{:S(2)}) collective-permute-start(bf16[4,6,48,64]{3,2,1,0:T(8,128)(2,1)S(1)} %bitcast.274), channel_id=1, source_target_pairs={{0,4},{4,8},{8,12},{12,16},{16,20},{20,24},{24,28},{1,5},{5,9},{9,... | collective-permute-start | bytes 442376 | tf_op jit(solution)/shard_map/ppermute | solution.py:298
  172.2 48.9 %collective-permute-start.34 = (bf16[4,6,48,64]{3,2,1,0:T(8,128)(2,1)S(1)}, bf16[4,6,48,64]{3,2,1,0:T(8,128)(2,1)}, u32[]{:S(2)}, u32[]{:S(2)}) collective-permute-start(bf16[4,6,48,64]{3,2,1,0:T(8,128)(2,1)S(1)} %bitcast.275), channel_id=1, source_target_pairs={{4,0},{8,4},{12,8},{16,12},{20,16},{24,20},{28,24},{5,1},{9,5},{13... | collective-permute-start | bytes 442376 | tf_op jit(solution)/shard_map/ppermute | solution.py:298
  183.1 26.9 %collective-permute-start.36 = (bf16[4,6,48,64]{3,2,1,0:T(8,128)(2,1)S(1)}, bf16[4,6,48,64]{3,2,1,0:T(8,128)(2,1)}, u32[]{:S(2)}, u32[]{:S(2)}) collective-permute-start(bf16[4,6,48,64]{3,2,1,0:T(8,128)(2,1)S(1)} %bitcast.278), channel_id=1, source_target_pairs={{8,0},{12,4},{16,8},{20,12},{24,16},{28,20},{9,1},{13,5},{17,9},{2... | collective-permute-start | bytes 442376 | tf_op jit(solution)/shard_map/ppermute | solution.py:298
  210.0 9.9 %collective-permute-start.37 = (bf16[4,6,48,64]{3,2,1,0:T(8,128)(2,1)S(1)}, bf16[4,6,48,64]{3,2,1,0:T(8,128)(2,1)S(1)}, u32[]{:S(2)}, u32[]{:S(2)}) collective-permute-start(bf16[4,6,48,64]{3,2,1,0:T(8,128)(2,1)S(1)} %bitcast.281), channel_id=1, source_target_pairs={{0,8},{4,12},{8,16},{12,20},{16,24},{20,28},{1,9},{5,13},{9,17},{1... | collective-permute-start | bytes 442376 | tf_op jit(solution)/shard_map/ppermute | solution.py:298
  292.9 274.4 %reduce-scatter.2.cloned.1.call-start = ((), (), s32[]{:S(2)}) async-start(), calls=%async_computation.1 | async-start | bytes 5898240 | tf_op jit(solution)/shard_map/reduce_scatter | solution.py:775
  (78 other events, 367.3 us)
Sparse Core Ops, SparseCore 0:
  293.0 258.9 all-reduce.14
Sparse Core Ops, SparseCore 1:
  381.9 51.2 reduce-scatter.1

commit v2 on v1

--- a/solution.py
+++ b/solution.py
@@ -26,7 +26,7 @@
     return lax.dot_general(a, b, dims, preferred_element_type=f32)
 
 
-def params(mib=48, **kw):
+def params(mib=60, **kw):
     return pltpu.CompilerParams(vmem_limit_bytes=mib * MIB, **kw)
 
 
@@ -66,22 +66,23 @@
     return jnp.concatenate(sums + [jnp.zeros((8 - len(sums), width), f32)], axis=0)
 
 
-def side_kernel(lim_ref, x_ref, wm_ref, wp_ref, *refs, steps, slabs, cols, rates):
-    outs, (wcat, acc) = refs[:6], refs[6:]
+def side_kernel(lim_ref, low_ref, x_ref, *refs, steps, slabs, cols, rates):
+    n_rates = len(rates)
+    weights, outs, (wcat, acc) = refs[: 2 * n_rates], refs[2 * n_rates : 4 * n_rates], refs[4 * n_rates :]
     k = pl.program_id(0)
-    L = wm_ref.shape[3]
-    for j in range(3):
+    L = weights[0].shape[3]
+    for j in range(n_rates):
         for v in range(3):
             t = (j * 3 + v) * 2 * L
-            wcat[t : t + L] = wm_ref[j, 0, v]
-            wcat[t + L : t + 2 * L] = wp_ref[j, 0, v]
+            wcat[t : t + L] = weights[2 * j][0, 0, v]
+            wcat[t + L : t + 2 * L] = weights[2 * j + 1][0, 0, v]
 
     @pl.when(k == 0)
     def _():
         acc[...] = jnp.zeros_like(acc)
 
     x = x_ref[...]
-    total = 18 * L
+    total = 6 * n_rates * L
     for n in range(0, total, 256):
         e = min(n + 256, total)
         acc[:, n:e] += dot(x, wcat[n:e], NT)
@@ -93,12 +94,15 @@
         mask = cell_mask(lim_ref, slabs, cols, 2 * L)
         col = column_ids(slabs, cols, 2 * L)
         low = lax.broadcasted_iota(jnp.int32, (half, 2 * L), 1) < L
-        for j in range(3):
+        for j in range(n_rates):
             a = [acc[:, (j * 3 + v) * 2 * L : (j * 3 + v + 1) * 2 * L] * mask for v in range(3)]
             s = a[1] + from_left(a[0], rates[j], col) + from_right(a[2], rates[j], col, cols)
             top, bottom = s[:half], s[half:]
-            outs[2 * j][...] = jnp.where(low, top, pltpu.roll(bottom, L, 1)).astype(bf16)
-            outs[2 * j + 1][...] = jnp.where(low, pltpu.roll(top, L, 1), bottom).astype(bf16)
+            up = jnp.where(low, top, pltpu.roll(bottom, L, 1))
+            down = jnp.where(low, pltpu.roll(top, L, 1), bottom)
+            first = low_ref[j] == 1
+            outs[2 * j][...] = jnp.where(first, up, down).astype(bf16)
+            outs[2 * j + 1][...] = jnp.where(first, down, up).astype(bf16)
 
 
 def centre_kernel(
@@ -277,7 +281,7 @@
     sums_ref[...] = column_sums(s, q)
 
 
-def grad_kernel(lim_ref, dt_ref, conv_ref, stat_ref, cg_ref, *, slabs, cols):
+def grad_kernel(lim_ref, dt_ref, conv_ref, stat_ref, cg_ref, scratch, *, slabs, cols):
     W = conv_ref.shape[1]
     mean, rstd, scale, beta, gamma = (stat_ref[i : i + 1] for i in range(5))
     cid = lax.broadcasted_iota(jnp.int32, (cols, W), 0)
@@ -285,17 +289,158 @@
         rows = slice(i * cols, (i + 1) * cols)
         normed = (conv_ref[rows] - mean) * rstd
         g = scale * (dt_ref[rows] - beta - normed * gamma)
-        cg_ref[rows] = jnp.where(cid < lim_ref[i], g, 0.0).astype(bf16)
+        scratch[rows] = jnp.where(cid < lim_ref[i], g, 0.0)
+    cg_ref[...] = scratch[...].T.astype(bf16)
+
+
+def shifted(f, v, d, col, cols):
+    if v == 1:
+        return f
+    if v == 2:
+        return jnp.where(col >= d, pltpu.roll(f, d, 1), 0.0)
+    return jnp.where(col < cols - d, pltpu.roll(f, f.shape[1] - d, 1), 0.0)
+
+
+def expand_kernel(col_ref, cg_ref, out_ref, *, cols, rates):
+    L = cg_ref.shape[0] // 4
+    for j in range(3):
+        raw = cg_ref[(j + 1) * L : (j + 2) * L]
+        f = raw.astype(f32)
+        col = jnp.broadcast_to(col_ref[0:1], f.shape)
+        base = 3 * j * L
+        out_ref[base : base + L] = shifted(f, 0, rates[j], col, cols).astype(bf16)
+        out_ref[base + L : base + 2 * L] = raw
+        out_ref[base + 2 * L : base + 3 * L] = shifted(f, 2, rates[j], col, cols).astype(bf16)
+    out_ref[9 * L :] = cg_ref[:L]
+
+
+def fetch_blocks(pos, blocks, dest, sems, lanes=False):
+    copies = []
+    for d, ref in enumerate(blocks):
+        place = pos ^ d
+        if lanes:
+            cells = ref.shape[1]
+            spot = dest.at[:, pl.ds(pl.multiple_of(place * cells, 128), cells)]
+        else:
+            spot = dest.at[place]
+        copies.append(pltpu.make_async_copy(ref, spot, sems.at[d]))
+    for c in copies:
+        c.start()
+    return copies
+
+
+def tap_products(store, taps, x_rows, L):
+    cells = taps.shape[1] // BLOCKS
+    own_row = dot(taps[...], x_rows(0, BLOCKS), NN)
+    for j in range(3):
+        lo = (j * 3 + 1) * 3 * L
+        store(lo, own_row[3 * j * L : 3 * (j + 1) * L])
+    store(27 * L, own_row[9 * L :])
+    for j in range(3):
+        rows = slice(3 * j * L, 3 * (j + 1) * L)
+        span = (BLOCKS - 1 - j) * cells
+        far = (j + 1) * cells
+        store(j * 9 * L, dot(taps[rows, far:], x_rows(0, BLOCKS - 1 - j), NN))
+        store((j * 3 + 2) * 3 * L, dot(taps[rows, :span], x_rows(j + 1, BLOCKS), NN))
+
+
+def narrow_kernel(pos_ref, *refs, parts):
+    blocks, (x_ref, out_ref, taps, x, sems, xsems) = refs[:BLOCKS], refs[BLOCKS:]
+    pos, ch = pos_ref[0], pos_ref[2]
+    L = taps.shape[0] // 10
+    cells = taps.shape[1] // BLOCKS
+    rows = x_ref.shape[2]
+    copies = fetch_blocks(pos, blocks, taps, sems, lanes=True)
+    for e in range(parts):
+        for d in range(BLOCKS):
+            place = pl.ds(pl.multiple_of((pos ^ d) * cells + (ch ^ e) * rows, 16), rows)
+            c = pltpu.make_async_copy(x_ref.at[e, d], x.at[place], xsems.at[e, d])
+            c.start()
+            copies.append(c)
+    for c in copies:
+        c.wait()
+
+    def store(lo, value):
+        out_ref[lo : lo + value.shape[0]] = value.astype(bf16)
+
+    tap_products(store, taps, lambda lo, hi: x[lo * cells : hi * cells], L)
+
+
+def wide_kernel(pos_ref, x_ref, *refs):
+    blocks, (acc_ref, point_ref, taps, sems) = refs[:BLOCKS], refs[BLOCKS:]
+    L = point_ref.shape[0]
+
+    @pl.when(pl.program_id(0) == 0)
+    def _():
+        for c in fetch_blocks(pos_ref[0], blocks, taps, sems, lanes=True):
+            c.wait()
+
+    def store(lo, value):
+        if lo < 27 * L:
+            acc_ref[lo : lo + value.shape[0]] = value
+        else:
+            point_ref[...] = value
+
+    w = x_ref.shape[3]
+    tap_products(store, taps, lambda lo, hi: x_ref[lo:hi, 0].reshape(-1, w), L)
+
+
+def widen_kernel(in_ref, pin_ref, keep_ref, pkeep_ref, out_ref, pout_ref):
+    w = in_ref.shape[2]
+    for s in range(BLOCKS):
+        out_ref[:, s * w : (s + 1) * w] = in_ref[s].astype(f32)
+        pout_ref[:, s * w : (s + 1) * w] = pin_ref[s].astype(f32)
+
+
+def input_grad_kernel(pos_ref, lim_ref, col_ref, w_ref, wp_ref, pool_ref, *refs, slabs, cols, rates, images):
+    blocks, (out_ref, cg, lhs, rhs, sems) = refs[:BLOCKS], refs[BLOCKS:]
+    L = wp_ref.shape[0]
+    s = pos_ref[0]
+
+    @pl.when(pl.program_id(0) == 0)
+    def _():
+        for c in fetch_blocks(s, blocks, cg, sems):
+            c.wait()
+        pieces = []
+        order = [(j, u, v) for j in range(3) for u in range(3) for v in range(3)] + [None]
+        for i, tap in enumerate(order):
+            if tap is None:
+                pieces.append(cg[s, 0:L].astype(f32))
+            else:
+                j, u, v = tap
+                b = s - (u - 1) * (j + 1)
+                inside = ((b >= 0) & (b < BLOCKS)).astype(f32)
+                f = cg[jnp.clip(b, 0, BLOCKS - 1), (j + 1) * L : (j + 2) * L].astype(f32) * inside
+                col = jnp.broadcast_to(col_ref[0:1], f.shape)
+                pieces.append(shifted(f, v, rates[j], col, cols))
+            if i % 4 == 3:
+                lhs[:, (i - 3) * L : (i + 1) * L] = jnp.concatenate(pieces, axis=0).T.astype(bf16)
+                pieces = []
+
+    rhs[: 27 * L] = w_ref[...]
+    rhs[27 * L :] = wp_ref[...]
+    width = out_ref.shape[2]
+    per = slabs // images
+    cid = lax.broadcasted_iota(jnp.int32, (cols, 256), 0)
+    for n in range(0, width, 256):
+        part = dot(lhs[...], rhs[:, n : n + 256], NN)
+        for i in range(slabs):
+            value = part[i * cols : (i + 1) * cols] + pool_ref[i // per : i // per + 1, n : n + 256]
+            out_ref[0, i * cols : (i + 1) * cols, n : n + 256] = jnp.where(cid < lim_ref[i], value, 0.0).astype(bf16)
 
 
 def grouped(pairs, size):
     return [(g * BLOCKS + a, g * BLOCKS + b) for g in range(size // BLOCKS) for a, b in pairs]
 
 
-def from_behind(block, axis, distance):
+def neighbours(first, second, axis, distance):
     size = lax.axis_size(axis)
-    pairs = [(i - distance, i) for i in range(BLOCKS) if 0 <= i - distance < BLOCKS]
-    return lax.ppermute(block, axis, grouped(pairs, size))
+    rounds = []
+    for parity, block in ((0, first), (1, second)):
+        lows = [a for a in range(BLOCKS - distance) if (a // distance) % 2 == parity]
+        pairs = [(a, a + distance) for a in lows] + [(a + distance, a) for a in lows]
+        rounds.append(lax.ppermute(block, axis, grouped(pairs, size)))
+    return rounds
 
 
 def swap(block, axis, bits):
@@ -305,7 +450,31 @@
 def sum_over_sp(x):
     x = x + swap(x, "sp", 1)
     parts = [swap(x, "sp", b) for b in (2, 4, 6)]
-    return x + parts[0] + parts[1] + parts[2]
+    return (x + parts[0]) + (parts[1] + parts[2])
+
+
+def swaps_over_sp(x):
+    blocks = [x, None] + [swap(x, "sp", b) if b % 2 == 0 else None for b in range(2, BLOCKS)]
+    for b in range(1, BLOCKS, 2):
+        blocks[b] = swap(blocks[b - 1], "sp", 1)
+    return blocks
+
+
+def after(x, *others):
+    return lax.optimization_barrier((x,) + others)[0]
+
+
+def thirds(x):
+    hi = lax.reduce_precision(x, 8, 7)
+    mid = lax.reduce_precision(x - hi, 8, 7)
+    return jnp.stack([hi, mid, x - hi - mid]).astype(bf16)
+
+
+def sum_over_sp_bf16(x):
+    x = x.astype(bf16)
+    x = (x.astype(f32) + swap(x, "sp", 1).astype(f32)).astype(bf16)
+    parts = [swap(x, "sp", b).astype(f32) for b in (2, 4, 6)]
+    return (x.astype(f32) + parts[0]) + (parts[1] + parts[2])
 
 
 def plain_from_behind(block, axis, distance):
@@ -579,8 +748,11 @@
 
     norms = jnp.concatenate([bn_gains, bn_shifts, jnp.zeros((4, L), f32)], axis=0)
     wp = w_proj.reshape(5 * L, F)
-    norms_all = jnp.stack([norms] + [swap(norms, "ch", b) for b in (1, 2, 3)])
-    wp_all = jnp.stack([wp] + [swap(wp, "ch", b) for b in (1, 2, 3)])
+    packed = jnp.concatenate([wp, thirds(norms).reshape(-1, F)], axis=0)
+    packed_y = swap(packed, "ch", 2)
+    packed_all = jnp.stack([packed, swap(packed, "ch", 1), packed_y, swap(packed_y, "ch", 1)])
+    wp_all = packed_all[:, : 5 * L]
+    norms_all = jnp.sum(packed_all[:, 5 * L :].reshape(4, 3, 16, L).astype(f32), axis=1)
     wbranch_all, wpool_all = wp_all[:, :W], wp_all[:, W:]
     natural = (own ^ jnp.arange(4))[:, None] == jnp.arange(4)[None, :]
     final_par = jnp.sum(
@@ -591,23 +763,50 @@
     KT = 512
     steps = C // KT
     x_spec = pl.BlockSpec((cells, KT), lambda k: (0, k))
-    side = pl.pallas_call(
-        functools.partial(side_kernel, steps=steps, slabs=slabs, cols=cols, rates=rates),
-        grid=(steps,),
-        in_specs=[
-            SMEM,
-            x_spec,
-            pl.BlockSpec((3, 1, 3, L, KT), lambda k: (0, 0, 0, 0, k)),
-            pl.BlockSpec((3, 1, 3, L, KT), lambda k: (0, 2, 0, 0, k)),
-        ],
-        out_specs=[pl.BlockSpec((cells // 2, 2 * L), lambda k: (0, 0))] * 6,
-        out_shape=[jax.ShapeDtypeStruct((cells // 2, 2 * L), bf16)] * 6,
-        scratch_shapes=[pltpu.VMEM((18 * L, KT), bf16), pltpu.VMEM((cells, 18 * L), f32)],
-        compiler_params=params(),
-        cost_estimate=cost(2 * cells * C * 18 * L, 10e6),
-        name="side_taps",
-    )(lim, x, atrous_weight, atrous_weight)
-    halo = [from_behind(side[i], "sp", (1 - 2 * (i % 2)) * dilation_factors[i // 2]) for i in range(6)]
+    first = [(1 - (block_id // f) % 2).astype(jnp.int32) for f in dilation_factors]
+
+    def side_taps(which, x):
+        out = pl.pallas_call(
+            functools.partial(
+                side_kernel, steps=steps, slabs=slabs, cols=cols, rates=tuple(rates[j] for j in which)
+            ),
+            grid=(steps,),
+            in_specs=[SMEM, SMEM, x_spec]
+            + [
+                pl.BlockSpec((1, 1, 3, L, KT), lambda k, j=j, u=u: (j, u, 0, 0, k))
+                for j in which
+                for u in (0, 2)
+            ],
+            out_specs=[pl.BlockSpec((cells // 2, 2 * L), lambda k: (0, 0))] * (2 * len(which)),
+            out_shape=[jax.ShapeDtypeStruct((cells // 2, 2 * L), bf16)] * (2 * len(which)),
+            scratch_shapes=[
+                pltpu.VMEM((6 * len(which) * L, KT), bf16),
+                pltpu.VMEM((cells, 6 * len(which) * L), f32),
+            ],
+            compiler_params=params(),
+            cost_estimate=cost(2 * cells * C * 6 * len(which) * L, 10e6),
+            name="side_taps",
+        )(lim, jnp.stack([first[j] for j in which]), x, *[atrous_weight] * (2 * len(which)))
+        moved = []
+        for i, j in enumerate(which):
+            moved += neighbours(out[2 * i], out[2 * i + 1], "sp", dilation_factors[j])
+        return moved, out[0]
+
+    narrow = C // 2
+    valid = (jnp.arange(cols, dtype=jnp.int32)[None, :] < lim[:, None]).reshape(cells, 1)
+    cut = narrow // BLOCKS
+    part = cells // images
+    image = lax.dynamic_slice(x, (own * part, 0), (part, narrow))
+    image = jnp.where(lax.dynamic_slice_in_dim(valid, own * part, part), image, jnp.zeros((), bf16))
+    column = block_id // 2
+    sent = [lax.dynamic_slice_in_dim(image, (column ^ dz) * 2 * cut, 2 * cut, 1) for dz in range(4)]
+    mine = jnp.stack([sent[0]] + [swap(sent[dz], "sp", 2 * dz) for dz in (1, 2, 3)])
+    wide_w = (C - narrow) // 4
+    own_wide = lax.dynamic_slice_in_dim(x, narrow + own * wide_w, wide_w, 1)
+    own_wide = jnp.where(valid, own_wide, jnp.zeros((), bf16))
+    halo, made = side_taps((0, 1, 2), x)
+    x_wide = lax.all_gather(after(own_wide, made), ("sp", "ch"), axis=0).reshape(BLOCKS, 4, cells, wide_w)
+    x_then = after(x, made, mine, own_wide)
     centre, sums = pl.pallas_call(
         functools.partial(centre_kernel, steps=steps, slabs=slabs, cols=cols, rates=rates, images=images),
         grid=(steps,),
@@ -623,7 +822,7 @@
         compiler_params=params(),
         cost_estimate=cost(2 * cells * C * 10 * L, 8e6),
         name="centre_taps",
-    )(lim, x, atrous_weight, w_point)
+    )(lim, x_then, atrous_weight, w_point)
     own_pooled = sums[:images] / own_count[:, None]
     proj_part = lax.dot_general(own_pooled, w_pool.astype(f32), NT, precision=highest_precision)
 
@@ -636,7 +835,7 @@
             jax.ShapeDtypeStruct((cells, W), bf16),
             jax.ShapeDtypeStruct((8, W), f32),
         ],
-        compiler_params=params(),
+        compiler_params=params(20),
         cost_estimate=cost(2e6, 4e6),
         name="combine_taps",
     )(lim, centre, *halo)
@@ -645,6 +844,10 @@
     conv_diag = swap(conv_y, "ch", 1)
     tile = jnp.concatenate([stat[:4], jnp.pad(proj_part, ((0, 0), (0, W - L)))], axis=0)
     tile = sum_over_sp(tile)
+    mine = after(mine, tile)
+    keep = lax.dynamic_slice_in_dim(mine, (block_id % 2) * cut, cut, 2)
+    give = lax.dynamic_slice_in_dim(mine, (1 - block_id % 2) * cut, cut, 2)
+    taken = swap(give, "sp", 1)
     tile = jnp.concatenate([tile[:2], stat[2:3], tile[3:]], axis=0)
     tiles = jnp.stack([tile] + [swap(tile, "ch", b) for b in (1, 2, 3)])
     mean = tiles[:, 0] / n
@@ -671,7 +874,7 @@
             jax.ShapeDtypeStruct((8, F), f32),
         ],
         scratch_shapes=[pltpu.VMEM((cells, W), bf16)],
-        compiler_params=params(),
+        compiler_params=params(20),
         cost_estimate=cost(2 * cells * 4 * W * F, 6e6),
         name="mix_branches",
     )(lim, conv, conv_core, conv_y, conv_diag, branch_stat, branch_par, wbranch_all, pool_in, wpool_all)
@@ -688,7 +891,7 @@
             jax.ShapeDtypeStruct((cells, F), f32),
             jax.ShapeDtypeStruct((8, F), f32),
         ],
-        compiler_params=params(),
+        compiler_params=params(20),
         cost_estimate=cost(2e6, 4e6),
         name="final_norm",
     )(lim, mixed, og, final_stat)
@@ -708,7 +911,7 @@
             jax.ShapeDtypeStruct((8, W), f32),
         ],
         scratch_shapes=[pltpu.VMEM((cells, F), bf16)],
-        compiler_params=params(),
+        compiler_params=params(20),
         cost_estimate=cost(4 * cells * W * F, 8e6),
         name="branch_grads",
     )(
@@ -722,12 +925,13 @@
         jnp.concatenate([bsums[:4], jnp.pad(pool_part, ((0, 0), (0, W - L)))], axis=0)
     )
     branch_beta, branch_gamma = btile[0], btile[1]
-    cg = pl.pallas_call(
+    cgt = pl.pallas_call(
         functools.partial(grad_kernel, slabs=slabs, cols=cols),
         in_specs=[SMEM] + [VMEM] * 3,
         out_specs=VMEM,
-        out_shape=jax.ShapeDtypeStruct((cells, W), bf16),
-        compiler_params=params(),
+        out_shape=jax.ShapeDtypeStruct((W, cells), bf16),
+        scratch_shapes=[pltpu.VMEM((cells, W), f32)],
+        compiler_params=params(20),
         cost_estimate=cost(2e6, 4e6),
         name="conv_grads",
     )(lim, dt, conv, jnp.stack([own_mean, own_rstd, own_rstd * own_gain, branch_beta / n, branch_gamma / n]))
@@ -742,42 +946,139 @@
     g_shifts = jnp.concatenate([branch_beta.reshape(4, L), pool_beta[None],
         lax.dynamic_slice_in_dim(final_beta, own * L, L)[None]], axis=0)
     output = lax.dynamic_slice_in_dim(out_all, own * L, L, 1).reshape(images, rows_dev, cols, L)
-    g_proj = jnp.concatenate([gproj.reshape(4, L, F), gproj_pool[None]], axis=0)
     pooled_grad = (
         jnp.einsum("kf,fc->kc", proj_grad, w_pool.astype(f32), precision=highest_precision)
         / own_count[:, None]
     )
-    g_pool = jnp.einsum("kf,kc->fc", proj_grad, own_pooled, precision=highest_precision)
-    col_ids = jnp.arange(cols, dtype=jnp.int32)
-    pix_mask = (col_ids[None, :] < lim[:, None]).astype(f32).reshape(images, rows_dev, cols, 1)
-    flat_pix = (features * pix_mask.astype(bf16)).reshape(cells, C)
-    grads = [cg[:, i * L : (i + 1) * L].reshape(images, rows_dev, cols, L) for i in range(4)]
-    point_grad = grads[0].reshape(cells, L)
-    g_point = jnp.einsum("pf,pc->fc", point_grad, flat_pix, preferred_element_type=f32)
-    input_term = jnp.einsum("pf,fc->pc", point_grad, w_point, preferred_element_type=f32)
-    input_term = input_term.reshape(images, rows_dev, cols, C) + pooled_grad[:, None, None, :]
-    atrous_list = []
-    for j, factor in enumerate(dilation_factors):
-        tap_list = []
-        for u in range(3):
-            g = grads[j + 1] if u == 1 else from_behind(grads[j + 1], "sp", (u - 1) * factor)
-            spread = jnp.stack(
-                [shift_cols(g, rates[j]), g, shift_cols(g, -rates[j])], axis=3
-            ).reshape(cells, 3 * L)
-            tap_list.append(
-                jnp.einsum("pt,pc->tc", spread, flat_pix, preferred_element_type=f32).reshape(3, L, C)
-            )
-            input_term = input_term + jnp.einsum(
-                "pt,tc->pc", spread, atrous_weight[j, u].reshape(3 * L, C), preferred_element_type=f32
-            ).reshape(images, rows_dev, cols, C)
-        atrous_list.append(jnp.stack(tap_list))
-    g_atrous = jnp.stack(atrous_list)
-    in_grad = lax.psum_scatter(
-        (input_term * pix_mask).astype(bf16), "ch", scatter_dimension=3, tiled=True
-    )
-    g_point, g_atrous, g_proj, g_pool = (
-        lax.psum(t.astype(bf16), "sp").astype(f32) for t in (g_point, g_atrous, g_proj, g_pool)
-    )
+    ANY = pl.BlockSpec(memory_space=pl.ANY)
+    col_row = jnp.broadcast_to((jnp.arange(cells, dtype=jnp.int32) % cols)[None, :], (8, cells))
+    pos = jnp.stack([block_id, own % 2, own]).astype(jnp.int32)
+    def column_taps(block):
+        return pl.pallas_call(
+            functools.partial(expand_kernel, cols=cols, rates=rates),
+            grid=(1,),
+            in_specs=[pl.BlockSpec((8, cells), lambda i: (0, 0)), pl.BlockSpec((W, cells), lambda i: (0, 0))],
+            out_specs=pl.BlockSpec((10 * L, cells), lambda i: (0, 0)),
+            out_shape=jax.ShapeDtypeStruct((10 * L, cells), bf16),
+            compiler_params=params(),
+            cost_estimate=cost(1e9, 6e6),
+            name="column_taps",
+        )(col_row, block)
+
+    near = [swap(cgt, "sp", b) for b in (2, 4, 6)]
+    pair = swap(cgt, "sp", 1)
+    taps = [column_taps(cgt), column_taps(pair), column_taps(near[0])]
+    near_pair = swap(near[0], "sp", 1)
+    taps.append(column_taps(near_pair))
+    x_slices = after(jnp.stack([keep, taken], axis=1).reshape(1, BLOCKS, part, cut), near[0])
+    x_slices = jnp.concatenate([x_slices, swap(x_slices, "ch", 2)], axis=0)
+    x_core = swap(x_slices, "ch", 1)
+    x_slices = jnp.stack([x_slices[0], x_core[0], x_slices[1], x_core[1]])
+    pooled = sum_over_sp(after(own_pooled, near[0]))
+    far = [after(near[1], *taps[:3]), after(near[2], *taps, x_slices, pooled)]
+    far_pairs = [swap(t, "sp", 1) for t in far]
+    blocks = [cgt, pair, near[0], near_pair, far[0], far_pairs[0], far[1], far_pairs[1]]
+    taps += [column_taps(t) for t in blocks[4:]]
+    eighth = narrow // BLOCKS
+    tap_scratch = pltpu.VMEM((10 * L, BLOCKS * cells), bf16)
+    gw = pl.pallas_call(
+        functools.partial(narrow_kernel, parts=images),
+        in_specs=[SMEM] + [ANY] * (BLOCKS + 1),
+        out_specs=pl.BlockSpec((28 * L, eighth), lambda i: (0, 0)),
+        grid=(1,),
+        out_shape=jax.ShapeDtypeStruct((28 * L, eighth), bf16),
+        scratch_shapes=[
+            tap_scratch,
+            pltpu.VMEM((BLOCKS * cells, eighth), bf16),
+            pltpu.SemaphoreType.DMA((BLOCKS,)),
+            pltpu.SemaphoreType.DMA((images, BLOCKS)),
+        ],
+        compiler_params=params(),
+        cost_estimate=cost(2 * cells * BLOCKS * 28 * L * eighth, 12e6),
+        name="narrow_weight_grads",
+    )(pos, *taps, x_slices)
+    gw_all = lax.all_gather(gw, "sp", axis=0)
+    pos, gw = lax.optimization_barrier((pos, gw))
+    group = C // 4
+    ig = pl.pallas_call(
+        functools.partial(input_grad_kernel, slabs=slabs, cols=cols, rates=rates, images=images),
+        grid_spec=pltpu.PrefetchScalarGridSpec(
+            num_scalar_prefetch=2,
+            grid=(4,),
+            in_specs=[
+                pl.BlockSpec((8, cells), lambda i, p, l: (0, 0)),
+                pl.BlockSpec((27 * L, group), lambda i, p, l: (0, p[2] ^ i)),
+                pl.BlockSpec((L, group), lambda i, p, l: (0, p[2] ^ i)),
+                pl.BlockSpec((8, group), lambda i, p, l: (0, p[2] ^ i)),
+            ]
+            + [ANY] * BLOCKS,
+            out_specs=pl.BlockSpec((1, cells, group), lambda i, p, l: (i, 0, 0)),
+            scratch_shapes=[
+                pltpu.VMEM((BLOCKS, W, cells), bf16),
+                pltpu.VMEM((cells, 28 * L), bf16),
+                pltpu.VMEM((28 * L, group), bf16),
+                pltpu.SemaphoreType.DMA((BLOCKS,)),
+            ],
+        ),
+        out_shape=jax.ShapeDtypeStruct((4, cells, group), bf16),
+        compiler_params=params(),
+        cost_estimate=cost(1e6, 1e6),
+        name="input_grads",
+    )(pos, lim, col_row, atrous_weight.reshape(27 * L, C), w_point,
+      jnp.pad(pooled_grad, ((0, 8 - images), (0, 0))), *blocks)
+    gp = after(jnp.concatenate([gproj, gproj_pool], axis=0).astype(bf16), gw)
+    gp = (gp.astype(f32) + swap(gp, "sp", 1).astype(f32)).astype(bf16)
+    gp_parts = [swap(gp, "sp", b) for b in (2, 4, 6)]
+    g_pool = jnp.einsum("kf,kc->fc", proj_grad, pooled, precision=highest_precision)
+    from_core = swap(jnp.concatenate([ig[1], ig[3]], axis=1), "ch", 1)
+    from_core = from_core.astype(f32)
+    keep = ig[0].astype(f32) + from_core[:, :group]
+    give = (ig[2].astype(f32) + from_core[:, group:]).astype(bf16)
+    given = swap(give, "ch", 2)
+    pos = after(pos, give)
+    if wide_w:
+        g_wide, p_wide = pl.pallas_call(
+            wide_kernel,
+            grid=(4,),
+            in_specs=[SMEM, pl.BlockSpec((BLOCKS, 1, cells, wide_w), lambda i: (0, i, 0, 0))] + [ANY] * BLOCKS,
+            out_specs=[
+                pl.BlockSpec((27 * L, wide_w), lambda i: (0, narrow // wide_w + i)),
+                pl.BlockSpec((L, wide_w), lambda i: (0, narrow // wide_w + i)),
+            ],
+            out_shape=[jax.ShapeDtypeStruct((27 * L, C), f32), jax.ShapeDtypeStruct((L, C), f32)],
+            scratch_shapes=[tap_scratch, pltpu.SemaphoreType.DMA((BLOCKS,))],
+            compiler_params=params(),
+            cost_estimate=cost(1e6, 1e6),
+            name="wide_weight_grads",
+        )(pos, x_wide, *taps)
+    else:
+        g_wide, p_wide = jnp.zeros((27 * L, C), f32), jnp.zeros((L, C), f32)
+    gp, *gp_parts = (t.astype(f32) for t in lax.optimization_barrier((gp, *gp_parts, p_wide))[:4])
+    g_proj = ((gp + gp_parts[0]) + (gp_parts[1] + gp_parts[2])).reshape(5, L, F)
+    in_grad = (keep + after(given, p_wide).astype(f32)).astype(bf16)
+    in_grad = in_grad.reshape(images, rows_dev, cols, group)
+
+    step = 3 * L
+    g_atrous, g_point = pl.pallas_call(
+        widen_kernel,
+        grid=(9,),
+        in_specs=[
+            pl.BlockSpec((BLOCKS, step, eighth), lambda i: (0, i, 0)),
+            pl.BlockSpec((BLOCKS, L, eighth), lambda i: (0, 27, 0)),
+            ANY,
+            ANY,
+        ],
+        out_specs=[
+            pl.BlockSpec((step, narrow), lambda i: (i, 0)),
+            pl.BlockSpec((L, narrow), lambda i: (0, 0)),
+        ],
+        out_shape=[jax.ShapeDtypeStruct((27 * L, C), f32), jax.ShapeDtypeStruct((L, C), f32)],
+        input_output_aliases={2: 0, 3: 1},
+        compiler_params=params(),
+        cost_estimate=cost(1e6, 20e6),
+        name="widen",
+    )(gw_all, gw_all, g_wide, p_wide)
+    g_atrous = g_atrous.reshape(3, 3, 3, L, C)
     return (output, in_grad, g_point, g_atrous, g_pool, g_proj, g_gains, g_shifts)
 
 

time: 583 us -> 378 us (0.65)
  waiting for transfers between devices: 184 us -> 73 us
  matrix products: 111 us -> 3.7 us
  Pallas kernels: 26.9 us -> 128 us
  local copies, waits for them, and re-layouts: 114 us -> 24.8 us
  starting transfers between devices: 71.2 us -> 90.5 us
  other arithmetic: 51.8 us -> 35.2 us
    psum x1 -> x0, waiting for transfers between devices: 167 us -> none  [body(): lax.psum(t.astype(bf16), 'sp').astype(f32)]
    dot_general x21 -> x1, matrix products: 108 us -> 1.43 us  [body(): jnp.einsum('kf,kc->fc', proj_grad, pooled, precision=highest_precision)]
    pallas_call x1 -> x13, Pallas kernels: 10.9 us -> 110 us  [the longest x1 38.3 us: body(): pl.pallas_call(wide_kernel, grid=(4,), in_specs=[SMEM, pl.BlockSpec((BLOC...]
    ppermute x28 -> x48, waiting for transfers between devices: 15.5 us -> 73 us  [swap(): lax.ppermute(block, axis, [(i, i ^ bits) for i in range(lax.axis_size(axi...]
    ppermute x28 -> x48, starting transfers between devices: 34.5 us -> 71.4 us  [swap(): lax.ppermute(block, axis, [(i, i ^ bits) for i in range(lax.axis_size(axi...]
    dot_general x18 -> x0, local copies, waits for them, and re-layouts: 30.9 us -> none  [the longest x9 16.7 us: body(): jnp.einsum('pt,tc->pc', spread, atrous_weight[j, u].reshape(3 * L, C), pr...]
    another operation x18 -> x3, local copies, waits for them, and re-layouts: 22.9 us -> 1.22 us  [the longest x2 1.13 us: body(): jnp.stack([keep, taken], axis=1).reshape(1, BLOCKS, part, cut)]
    reshape x9 -> x0, local copies, waits for them, and re-layouts: 19.7 us -> none  [body(): spread = jnp.stack([shift_cols(g, rates[j]), g, shift_cols(g, -rates[j])]...]
  transfers between devices with their start and end apart: 42 -> 56, of which waited for: 16 -> 28; matrix products, arithmetic and copies ran while one was open for 38% -> 12% of each run, Pallas kernels for 3% -> 29%
where the time goes in v2:
time: 378 us; the launch traced here: 371 us
  Pallas kernels  128 us (34%)
  starting transfers between devices  90.5 us (24%)
  waiting for transfers between devices  73 us (19%)
  other arithmetic  35.2 us (9%)
  local copies, waits for them, and re-layouts  24.8 us (7%)
  between operations  15.5 us (4%)
    ppermute x48, waiting for transfers between devices, swap(): lax.ppermute(block, axis, [(i, i ^ bits) for i in range(lax.axis_size(axi...  73 us
    ppermute x48, starting transfers between devices, swap(): lax.ppermute(block, axis, [(i, i ^ bits) for i in range(lax.axis_size(axi...  71.4 us
    pallas_call x1, Pallas kernels, body(): pl.pallas_call(wide_kernel, grid=(4,), in_specs=[SMEM, pl.BlockSpec((BLOC...  38.3 us
    pallas_call x8, Pallas kernels, column_taps(): pl.pallas_call(functools.partial(expand_kernel, cols=cols, rates=rates),...  20.4 us
    ppermute x6, starting transfers between devices, neighbours(): rounds.append(lax.ppermute(block, axis, grouped(pairs, size)))  18.9 us
    pallas_call x1, Pallas kernels, body(): pl.pallas_call(functools.partial(input_grad_kernel, slabs=slabs, cols=col...  17.3 us
    pallas_call x1, Pallas kernels, body(): pl.pallas_call(functools.partial(narrow_kernel, parts=images), in_specs=[...  14.5 us
    unnamed x106, local copies, waits for them, and re-layouts  13.6 us
  transfers between devices with their start and end apart: 56, of which 28 were waited for; matrix products, arithmetic and copies ran while one was open for 12% of the time, Pallas kernels for 29%

profile of v2, /device:TPU:0, one launch (start us, length us, event | category | flops | bytes accessed | tf_op | source)
XLA Modules:
  0.0 371.0 jit_solution(14298211636326485093)
XLA Ops:
  8.9 11.2 %side_taps.1 = (bf16[576,128]{1,0:T(8,128)(2,1)}, bf16[576,128]{1,0:T(8,128)(2,1)}, bf16[576,128]{1,0:T(8,128)(2,1)}, bf16[576,128]{1,0:T(8,128)(2,1)}, bf16[576...) custom-call(s32[24]{0:T(128)} %copy-done.18, s32[3]{0:T(128)} %pad_add_fusion.low_ref, bf16[1152,2048]{1,0:T(8,128)(2,1)} %bitcast.96, ...), custom_call_target="tpu_custom_call" | custom-call | flops 5435817984 | bytes 10000000 | tf_op jit(solution)/shard_map/side_taps/pallas_call | solution.py:769
  20.2 2.3 dynamic-slice_select_fusion
  22.5 3.0 collective-permute-start.3
  27.1 3.7 collective-permute-start.2
  33.2 2.6 collective-permute-done.2
  35.8 9.4 %collective-permute-start.5 = (bf16[576,128]{1,0:T(8,128)(2,1)S(1)}, bf16[576,128]{1,0:T(8,128)(2,1)S(1)}, u32[]{:S(2)}, u32[]{:S(2)}) collective-permute-start(bf16[576,128]{1,0:T(8,128)(2,1)S(1)} %copy-done.51), channel_id=1, source_target_pairs={{0,8},{4,12},{16,24},{20,28},{8,0},{12,4},{24,16},{28,20},{1,9},{5... | collective-permute-start | bytes 442376 | tf_op jit(solution)/shard_map/ppermute | solution.py:442
  45.2 6.2 %collective-permute-done.1 = bf16[288,256]{1,0:T(8,128)(2,1)S(1)} collective-permute-done((bf16[288,256]{1,0:T(8,128)(2,1)S(1)}, bf16[288,256]{1,0:T(8,128)(2,1)S(1)}, u32[]{:S(2)}, u32[]{:S(2)}) %collective-permute-start.1) | collective-permute-done | bytes 147488 | tf_op jit(solution)/shard_map/ppermute | solution.py:447
  52.0 4.6 %collective-permute-start.7 = (bf16[576,128]{1,0:T(8,128)(2,1)S(1)}, bf16[576,128]{1,0:T(8,128)(2,1)S(1)}, u32[]{:S(2)}, u32[]{:S(2)}) collective-permute-start(bf16[576,128]{1,0:T(8,128)(2,1)S(1)} %copy-done.49), channel_id=1, source_target_pairs={{0,12},{4,16},{8,20},{12,0},{16,4},{20,8},{1,13},{5,17},{9,21},{13... | collective-permute-start | bytes 442376 | tf_op jit(solution)/shard_map/ppermute | solution.py:442
  58.2 9.1 %centre_taps.1 = (f32[1152,256]{1,0:T(8,128)}, f32[8,2048]{1,0:T(8,128)}) custom-call(s32[24]{0:T(128)} %copy-done.18, bf16[1152,2048]{1,0:T(8,128)(2,1)} %bitcast.99, bf16[3,3,3,64,2048]{4,3,2,1,0:T(8,128)(2,1)} %wc_ref.1, bf16[64,2048]{1,0:T(8,128)(2,1)} %wp_ref.1), custom_call_target="tpu_custom_call" | custom-call | flops 3019898880 | bytes 8000000 | tf_op jit(solution)/shard_map/centre_taps/pallas_call | solution.py:810
  70.0 2.0 combine_taps.1
  73.2 2.6 collective-permute-start.12
  77.7 3.2 collective-permute-start.14
  82.9 3.4 collective-permute-done.15
  95.9 11.3 %collective-permute-done.10.c2_ref = bf16[1152,256]{1,0:T(8,128)(2,1)S(1)} collective-permute-done((bf16[1152,256]{1,0:T(8,128)(2,1)}, bf16[1152,256]{1,0:T(8,128)(2,1)S(1)}, u32[]{:S(2)}, u32[]{:S(2)}) %collective-permute-start.10) | collective-permute-done | bytes 589856 | tf_op jit(solution)/shard_map/ppermute | solution.py:447
  113.2 3.2 mix_branches.1
  118.8 2.2 collective-permute-done.22
  122.0 2.5 collective-permute-start.23
  137.5 2.0 collective-permute-start.29
  140.8 2.4 collective-permute-done.29
  152.2 2.3 collective-permute-done.30
  155.0 2.2 collective-permute-start.33
  167.3 6.2 %collective-permute-done.40 = bf16[4,288,128]{2,1,0:T(8,128)(2,1)S(1)} collective-permute-done((bf16[4,288,128]{2,1,0:T(8,128)(2,1)S(1)}, bf16[4,288,128]{2,1,0:T(8,128)(2,1)S(1)}, u32[]{:S(2)}, u32[]{:S(2)}) %collective-permute-start.40) | collective-permute-done | bytes 294944 | tf_op jit(solution)/shard_map/ppermute | solution.py:447
  177.5 3.9 %collective-permute-start.37 = (bf16[256,1152]{1,0:T(8,128)(2,1)S(1)}, bf16[256,1152]{1,0:T(8,128)(2,1)}, u32[]{:S(2)}, u32[]{:S(2)}) collective-permute-start(bf16[256,1152]{1,0:T(8,128)(2,1)S(1)} %conv_grads.1.cg_ref.refs_0_), channel_id=1, source_target_pairs={{0,16},{4,20},{8,24},{12,28},{16,0},{20,4},{24,8},{28,12},{1,17},{... | collective-permute-start | bytes 1769480 | tf_op jit(solution)/shard_map/ppermute | solution.py:447
  181.3 2.7 collective-permute-done.41
  186.5 2.5 column_taps.8.refs_0_
  189.0 3.3 collective-permute-start.43
  192.4 2.6 column_taps.10.refs_2_
  197.6 3.4 collective-permute-done.37.cg_ref.refs_4_
  201.0 2.5 column_taps.9.refs_1_
  203.5 2.6 collective-permute-start.39
  206.2 2.4 collective-permute-done.36.cg_ref.refs_3_
  208.6 2.5 column_taps.11.refs_3_
  214.3 3.8 %collective-permute-done.39.cg_ref.refs_6_ = bf16[256,1152]{1,0:T(8,128)(2,1)} collective-permute-done((bf16[256,1152]{1,0:T(8,128)(2,1)S(1)}, bf16[256,1152]{1,0:T(8,128)(2,1)}, u32[]{:S(2)}, u32[]{:S(2)}) %collective-permute-start.39) | collective-permute-done | bytes 589856 | tf_op jit(solution)/shard_map/ppermute | solution.py:447
  220.8 2.6 column_taps.12.refs_4_
  223.3 2.6 column_taps.13.refs_5_
  225.9 2.6 column_taps.14.refs_6_
  228.5 4.5 %collective-permute-done.47.cg_ref.refs_7_ = bf16[256,1152]{1,0:T(8,128)(2,1)S(1)} collective-permute-done((bf16[256,1152]{1,0:T(8,128)(2,1)}, bf16[256,1152]{1,0:T(8,128)(2,1)S(1)}, u32[]{:S(2)}, u32[]{:S(2)}) %collective-permute-start.47) | collective-permute-done | bytes 589856 | tf_op jit(solution)/shard_map/ppermute | solution.py:447
  233.9 2.5 column_taps.15.refs_7_
  236.4 14.5 %narrow_weight_grads.1 = bf16[1792,128]{1,0:T(8,128)(2,1)} custom-call(s32[3]{0:T(128)} %pad_add_fusion.1.pos_ref, bf16[640,1152]{1,0:T(8,128)(2,1)} %column_taps.8.refs_0_, bf16[640,1152]{1,0:T(8,128)(2,1)} %column_taps.9.refs_1_, bf16[640,1152]{1,0:T(8,128)(2,1)} %column_taps.10.refs_2_, bf16[640,1152]{1,0:T(8,128)(2,1)} %column_taps.11.refs_3_, ...), custom_call_target="tpu_custom_call" | custom-call | flops 4227858432 | bytes 12000000 | tf_op jit(solution)/shard_map/narrow_weight_grads/pallas_call | solution.py:984
  251.8 17.3 %input_grads.1 = bf16[4,1152,512]{2,1,0:T(8,128)(2,1)} custom-call(s32[3]{0:T(128)} %pad_add_fusion.1.pos_ref, s32[24]{0:T(128)} %copy-done.18, s32[8,1152]{1,0:T(8,128)} %broadcast_in_dim.119.col_ref, bf16[1728,2048]{1,0:T(8,128)(2,1)} %bitcast.95, bf16[64,2048]{1,0:T(8,128)(2,1)} %wp_ref.1, f32[8,2048]{1,0:T(8,128)} %pad.18.pool_ref, ...), custom_call_target="tpu_custom_call" | custom-call | flops 1000000 | bytes 1000000 | tf_op jit(solution)/shard_map/input_grads/pallas_call | solution.py:1003
  272.9 4.9 %collective-permute-done.48 = bf16[1152,1024]{1,0:T(8,128)(2,1)} collective-permute-done((bf16[1152,1024]{1,0:T(8,128)(2,1)}, bf16[1152,1024]{1,0:T(8,128)(2,1)}, u32[]{:S(2)}, u32[]{:S(2)}) %collective-permute-start.48) | collective-permute-done | bytes 2359328 | tf_op jit(solution)/shard_map/ppermute | solution.py:447
  277.8 2.2 convert_element_type.85
  280.0 2.8 fusion
  287.5 3.5 collective-permute-done.50
  291.1 18.1 %collective-permute-start.51 = (bf16[320,256]{1,0:T(8,128)(2,1)S(1)}, bf16[320,256]{1,0:T(8,128)(2,1)S(1)}, u32[]{:S(2)}, u32[]{:S(2)}) collective-permute-start(bf16[320,256]{1,0:T(8,128)(2,1)S(1)} %add_convert_fusion), channel_id=1, source_target_pairs={{0,8},{4,12},{8,0},{12,4},{16,24},{20,28},{24,16},{28,20},{1,9},{5... | collective-permute-start | bytes 491528 | tf_op jit(solution)/shard_map/ppermute | solution.py:447
  313.1 38.3 %wide_weight_grads.1 = (f32[1728,2048]{1,0:T(8,128)}, f32[64,2048]{1,0:T(8,128)}) custom-call(s32[3]{0:T(128)} %pad_add_fusion.1.pos_ref, bf16[8,4,1152,256]{3,2,1,0:T(8,128)(2,1)} %bitcast.100, bf16[640,1152]{1,0:T(8,128)(2,1)} %column_taps.8.refs_0_, bf16[640,1152]{1,0:T(8,128)(2,1)} %column_taps.9.refs_1_, bf16[640,1152]{1,0:T(8,128)(2,1)} %column_taps.10.refs_2_, ...), custom_call_target="tpu_custom_call" | custom-call | flops 1000000 | bytes 1000000 | tf_op jit(solution)/shard_map/wide_weight_grads/pallas_call | solution.py:1040
  351.4 3.5 fusion.2
  354.9 7.9 %widen.1 = (f32[1728,2048]{1,0:T(8,128)}, f32[64,2048]{1,0:T(8,128)}) custom-call(bf16[8,1792,128]{2,1,0:T(8,128)(2,1)} %bitcast.101, bf16[8,1792,128]{2,1,0:T(8,128)(2,1)} %bitcast.102, f32[1728,2048]{1,0:T(8,128)} %get-tuple-element.78.keep_ref, f32[64,2048]{1,0:T(8,128)} %get-tuple-element.76.pkeep_ref), custom_call_target="tpu_custom_call", output_to_operand_aliasing={{0}: (2, {}), {1}: (3, {})} | custom-call | flops 1000000 | bytes 20000000 | tf_op jit(solution)/shard_map/widen/pallas_call | solution.py:1062
  (302 shorter events, 98.0 us)
Async XLA Ops:
  7.2 305.9 %all-gather.5.cloned.1.call-start = ((), (), s32[]{:S(2)}) async-start(), calls=%async_computation | async-start | bytes 19464192 | tf_op jit(solution)/shard_map/all_gather | solution.py:808
  22.5 332.5 %all-gather.7.cloned.1.call-start = ((), (), s32[]{:S(2)}) async-start(), calls=%async_computation.1 | async-start | bytes 4128768 | tf_op jit(solution)/shard_map/all_gather | solution.py:1000
  22.5 35.0 %collective-permute-start.3 = (bf16[576,128]{1,0:T(8,128)(2,1)}, bf16[576,128]{1,0:T(8,128)(2,1)S(1)}, u32[]{:S(2)}, u32[]{:S(2)}) collective-permute-start(bf16[576,128]{1,0:T(8,128)(2,1)} %get-tuple-element.47), channel_id=1, source_target_pairs={{0,4},{8,12},{16,20},{24,28},{4,0},{12,8},{20,16},{28,24},{1,5},{9... | collective-permute-start | bytes 442376 | tf_op jit(solution)/shard_map/ppermute | solution.py:442
  27.1 8.7 %collective-permute-start.2 = (bf16[288,256]{1,0:T(8,128)(2,1)S(1)}, bf16[288,256]{1,0:T(8,128)(2,1)S(1)}, u32[]{:S(2)}, u32[]{:S(2)}) collective-permute-start(bf16[288,256]{1,0:T(8,128)(2,1)S(1)} %get-tuple-element.111), channel_id=1, source_target_pairs={{0,24},{4,28},{8,16},{12,20},{16,8},{20,12},{24,0},{28,4},{1,25},{... | collective-permute-start | bytes 442376 | tf_op jit(solution)/shard_map/ppermute | solution.py:447
  30.7 20.6 %collective-permute-start.1 = (bf16[288,256]{1,0:T(8,128)(2,1)S(1)}, bf16[288,256]{1,0:T(8,128)(2,1)S(1)}, u32[]{:S(2)}, u32[]{:S(2)}) collective-permute-start(bf16[288,256]{1,0:T(8,128)(2,1)S(1)} %get-tuple-element.112), channel_id=1, source_target_pairs={{0,16},{4,20},{8,24},{12,28},{16,0},{20,4},{24,8},{28,12},{1,17},{... | collective-permute-start | bytes 442376 | tf_op jit(solution)/shard_map/ppermute | solution.py:447
  30.8 21.2 %collective-permute-start = (bf16[288,256]{1,0:T(8,128)(2,1)S(1)}, bf16[288,256]{1,0:T(8,128)(2,1)S(1)}, u32[]{:S(2)}, u32[]{:S(2)}) collective-permute-start(bf16[288,256]{1,0:T(8,128)(2,1)S(1)} %get-tuple-element.113), channel_id=1, source_target_pairs={{0,8},{4,12},{8,0},{12,4},{16,24},{20,28},{24,16},{28,20},{1,9},{5... | collective-permute-start | bytes 442376 | tf_op jit(solution)/shard_map/ppermute | solution.py:447
  31.5 35.7 %collective-permute-start.4 = (bf16[576,128]{1,0:T(8,128)(2,1)S(1)}, bf16[576,128]{1,0:T(8,128)(2,1)S(1)}, u32[]{:S(2)}, u32[]{:S(2)}) collective-permute-start(bf16[576,128]{1,0:T(8,128)(2,1)S(1)} %copy-done.52), channel_id=1, source_target_pairs={{4,8},{12,16},{20,24},{8,4},{16,12},{24,20},{5,9},{13,17},{21,25},... | collective-permute-start | bytes 442376 | tf_op jit(solution)/shard_map/ppermute | solution.py:442
  35.8 32.9 %collective-permute-start.5 = (bf16[576,128]{1,0:T(8,128)(2,1)S(1)}, bf16[576,128]{1,0:T(8,128)(2,1)S(1)}, u32[]{:S(2)}, u32[]{:S(2)}) collective-permute-start(bf16[576,128]{1,0:T(8,128)(2,1)S(1)} %copy-done.51), channel_id=1, source_target_pairs={{0,8},{4,12},{16,24},{20,28},{8,0},{12,4},{24,16},{28,20},{1,9},{5... | collective-permute-start | bytes 442376 | tf_op jit(solution)/shard_map/ppermute | solution.py:442
  51.3 17.4 %collective-permute-start.6 = (bf16[576,128]{1,0:T(8,128)(2,1)S(1)}, bf16[576,128]{1,0:T(8,128)(2,1)S(1)}, u32[]{:S(2)}, u32[]{:S(2)}) collective-permute-start(bf16[576,128]{1,0:T(8,128)(2,1)S(1)} %copy-done.50), channel_id=1, source_target_pairs={{8,16},{12,20},{16,8},{20,12},{9,17},{13,21},{17,9},{21,13},{10,18... | collective-permute-start | bytes 442376 | tf_op jit(solution)/shard_map/ppermute | solution.py:442
  52.0 16.7 %collective-permute-start.7 = (bf16[576,128]{1,0:T(8,128)(2,1)S(1)}, bf16[576,128]{1,0:T(8,128)(2,1)S(1)}, u32[]{:S(2)}, u32[]{:S(2)}) collective-permute-start(bf16[576,128]{1,0:T(8,128)(2,1)S(1)} %copy-done.49), channel_id=1, source_target_pairs={{0,12},{4,16},{8,20},{12,0},{16,4},{20,8},{1,13},{5,17},{9,21},{13... | collective-permute-start | bytes 442376 | tf_op jit(solution)/shard_map/ppermute | solution.py:442
  57.5 11.2 %collective-permute-start.8 = (bf16[576,128]{1,0:T(8,128)(2,1)S(1)}, bf16[576,128]{1,0:T(8,128)(2,1)S(1)}, u32[]{:S(2)}, u32[]{:S(2)}) collective-permute-start(bf16[576,128]{1,0:T(8,128)(2,1)S(1)} %copy-done.48), channel_id=1, source_target_pairs={{12,24},{16,28},{24,12},{28,16},{13,25},{17,29},{25,13},{29,17},{1... | collective-permute-start | bytes 442376 | tf_op jit(solution)/shard_map/ppermute | solution.py:442
  67.3 21.6 %collective-permute-start.20 = (bf16[332,256]{1,0:T(8,128)(2,1)}, bf16[332,256]{1,0:T(8,128)(2,1)S(1)}, u32[]{:S(2)}, u32[]{:S(2)}) collective-permute-start(bf16[332,256]{1,0:T(8,128)(2,1)} %get-tuple-element.115), channel_id=1, source_target_pairs={{0,2},{1,3},{2,0},{3,1},{4,6},{5,7},{6,4},{7,5},{8,10},{9,11},{10,... | collective-permute-start | bytes 509960 | tf_op jit(solution)/shard_map/ppermute | solution.py:447
  68.7 23.9 %collective-permute-start.19 = (bf16[332,256]{1,0:T(8,128)(2,1)}, bf16[332,256]{1,0:T(8,128)(2,1)S(1)}, u32[]{:S(2)}, u32[]{:S(2)}) collective-permute-start(bf16[332,256]{1,0:T(8,128)(2,1)} %get-tuple-element.115), channel_id=1, source_target_pairs={{0,1},{1,0},{2,3},{3,2},{4,5},{5,4},{6,7},{7,6},{8,9},{9,8},{10,11... | collective-permute-start | bytes 509960 | tf_op jit(solution)/shard_map/ppermute | solution.py:447
  73.2 4.4 %collective-permute-start.12 = (f32[8,256]{1,0:T(8,128)S(1)}, f32[8,256]{1,0:T(8,128)S(1)}, u32[]{:S(2)}, u32[]{:S(2)}) collective-permute-start(f32[8,256]{1,0:T(8,128)S(1)} %select_maximum_fusion.4), channel_id=1, source_target_pairs={{0,4},{4,0},{8,12},{12,8},{16,20},{20,16},{24,28},{28,24},{1,5},{5... | collective-permute-start | bytes 24584 | tf_op jit(solution)/shard_map/ppermute | solution.py:447
  77.7 5.3 %collective-permute-start.14 = (f32[8,256]{1,0:T(8,128)S(1)}, f32[8,256]{1,0:T(8,128)S(1)}, u32[]{:S(2)}, u32[]{:S(2)}) collective-permute-start(f32[8,256]{1,0:T(8,128)S(1)} %fusion.17), channel_id=1, source_target_pairs={{0,16},{4,20},{8,24},{12,28},{16,0},{20,4},{24,8},{28,12},{1,17},{... | collective-permute-start | bytes 24584 | tf_op jit(solution)/shard_map/ppermute | solution.py:447
  80.8 5.5 %collective-permute-start.15 = (f32[8,256]{1,0:T(8,128)S(1)}, f32[8,256]{1,0:T(8,128)S(1)}, u32[]{:S(2)}, u32[]{:S(2)}) collective-permute-start(f32[8,256]{1,0:T(8,128)S(1)} %fusion.17), channel_id=1, source_target_pairs={{0,24},{4,28},{8,16},{12,20},{16,8},{20,12},{24,0},{28,4},{1,25},{... | collective-permute-start | bytes 24584 | tf_op jit(solution)/shard_map/ppermute | solution.py:447
  81.8 4.5 %collective-permute-start.13 = (f32[8,256]{1,0:T(8,128)S(1)}, f32[8,256]{1,0:T(8,128)S(1)}, u32[]{:S(2)}, u32[]{:S(2)}) collective-permute-start(f32[8,256]{1,0:T(8,128)S(1)} %fusion.17), channel_id=1, source_target_pairs={{0,8},{4,12},{8,0},{12,4},{16,24},{20,28},{24,16},{28,20},{1,9},{5... | collective-permute-start | bytes 24584 | tf_op jit(solution)/shard_map/ppermute | solution.py:447
  88.9 21.3 %collective-permute-start.9 = (bf16[1152,256]{1,0:T(8,128)(2,1)}, bf16[1152,256]{1,0:T(8,128)(2,1)S(1)}, u32[]{:S(2)}, u32[]{:S(2)}) collective-permute-start(bf16[1152,256]{1,0:T(8,128)(2,1)} %get-tuple-element.56), channel_id=1, source_target_pairs={{0,1},{1,0},{2,3},{3,2},{4,5},{5,4},{6,7},{7,6},{8,9},{9,8},{10,11... | collective-permute-start | bytes 1769480 | tf_op jit(solution)/shard_map/ppermute | solution.py:447
  89.5 17.7 %collective-permute-start.10 = (bf16[1152,256]{1,0:T(8,128)(2,1)}, bf16[1152,256]{1,0:T(8,128)(2,1)S(1)}, u32[]{:S(2)}, u32[]{:S(2)}) collective-permute-start(bf16[1152,256]{1,0:T(8,128)(2,1)} %get-tuple-element.56), channel_id=1, source_target_pairs={{0,2},{1,3},{2,0},{3,1},{4,6},{5,7},{6,4},{7,5},{8,10},{9,11},{10,... | collective-permute-start | bytes 1769480 | tf_op jit(solution)/shard_map/ppermute | solution.py:447
  107.2 3.8 %collective-permute-start.11 = (bf16[1152,256]{1,0:T(8,128)(2,1)S(1)}, bf16[1152,256]{1,0:T(8,128)(2,1)}, u32[]{:S(2)}, u32[]{:S(2)}) collective-permute-start(bf16[1152,256]{1,0:T(8,128)(2,1)S(1)} %collective-permute-done.10.c2_ref), channel_id=1, source_target_pairs={{0,1},{1,0},{2,3},{3,2},{4,5},{5,4},{6,7},{7,6},{8,9},{9,8},{10,11... | collective-permute-start | bytes 1769480 | tf_op jit(solution)/shard_map/ppermute | solution.py:447
  121.1 4.8 %collective-permute-start.24 = (f32[8,256]{1,0:T(8,128)S(1)}, f32[8,256]{1,0:T(8,128)S(1)}, u32[]{:S(2)}, u32[]{:S(2)}) collective-permute-start(f32[8,256]{1,0:T(8,128)S(1)} %add.261), channel_id=1, source_target_pairs={{0,16},{4,20},{8,24},{12,28},{16,0},{20,4},{24,8},{28,12},{1,17},{... | collective-permute-start | bytes 24584 | tf_op jit(solution)/shard_map/ppermute | solution.py:447
  121.3 5.6 %collective-permute-start.25 = (f32[8,256]{1,0:T(8,128)S(1)}, f32[8,256]{1,0:T(8,128)S(1)}, u32[]{:S(2)}, u32[]{:S(2)}) collective-permute-start(f32[8,256]{1,0:T(8,128)S(1)} %add.261), channel_id=1, source_target_pairs={{0,24},{4,28},{8,16},{12,20},{16,8},{20,12},{24,0},{28,4},{1,25},{... | collective-permute-start | bytes 24584 | tf_op jit(solution)/shard_map/ppermute | solution.py:447
  122.0 5.3 %collective-permute-start.23 = (f32[8,256]{1,0:T(8,128)S(1)}, f32[8,256]{1,0:T(8,128)S(1)}, u32[]{:S(2)}, u32[]{:S(2)}) collective-permute-start(f32[8,256]{1,0:T(8,128)S(1)} %add.261), channel_id=1, source_target_pairs={{0,8},{4,12},{8,0},{12,4},{16,24},{20,28},{24,16},{28,20},{1,9},{5... | collective-permute-start | bytes 24584 | tf_op jit(solution)/shard_map/ppermute | solution.py:447
  136.2 4.7 %collective-permute-start.28 = (f32[8,256]{1,0:T(8,128)S(1)}, f32[8,256]{1,0:T(8,128)S(1)}, u32[]{:S(2)}, u32[]{:S(2)}) collective-permute-start(f32[8,256]{1,0:T(8,128)S(1)} %add.271), channel_id=1, source_target_pairs={{0,16},{4,20},{8,24},{12,28},{16,0},{20,4},{24,8},{28,12},{1,17},{... | collective-permute-start | bytes 24584 | tf_op jit(solution)/shard_map/ppermute | solution.py:447
  137.5 5.7 %collective-permute-start.29 = (f32[8,256]{1,0:T(8,128)S(1)}, f32[8,256]{1,0:T(8,128)S(1)}, u32[]{:S(2)}, u32[]{:S(2)}) collective-permute-start(f32[8,256]{1,0:T(8,128)S(1)} %add.271), channel_id=1, source_target_pairs={{0,24},{4,28},{8,16},{12,20},{16,8},{20,12},{24,0},{28,4},{1,25},{... | collective-permute-start | bytes 24584 | tf_op jit(solution)/shard_map/ppermute | solution.py:447
  139.6 3.9 %collective-permute-start.27 = (f32[8,256]{1,0:T(8,128)S(1)}, f32[8,256]{1,0:T(8,128)S(1)}, u32[]{:S(2)}, u32[]{:S(2)}) collective-permute-start(f32[8,256]{1,0:T(8,128)S(1)} %add.271), channel_id=1, source_target_pairs={{0,8},{4,12},{8,0},{12,4},{16,24},{20,28},{24,16},{28,20},{1,9},{5... | collective-permute-start | bytes 24584 | tf_op jit(solution)/shard_map/ppermute | solution.py:447
  154.5 4.6 %collective-permute-start.32 = (f32[8,256]{1,0:T(8,128)S(1)}, f32[8,256]{1,0:T(8,128)S(1)}, u32[]{:S(2)}, u32[]{:S(2)}) collective-permute-start(f32[8,256]{1,0:T(8,128)S(1)} %fusion.18), channel_id=1, source_target_pairs={{0,16},{4,20},{8,24},{12,28},{16,0},{20,4},{24,8},{28,12},{1,17},{... | collective-permute-start | bytes 24584 | tf_op jit(solution)/shard_map/ppermute | solution.py:447
  155.0 5.4 %collective-permute-start.33 = (f32[8,256]{1,0:T(8,128)S(1)}, f32[8,256]{1,0:T(8,128)S(1)}, u32[]{:S(2)}, u32[]{:S(2)}) collective-permute-start(f32[8,256]{1,0:T(8,128)S(1)} %fusion.18), channel_id=1, source_target_pairs={{0,24},{4,28},{8,16},{12,20},{16,8},{20,12},{24,0},{28,4},{1,25},{... | collective-permute-start | bytes 24584 | tf_op jit(solution)/shard_map/ppermute | solution.py:447
  163.8 10.4 %collective-permute-start.35 = (bf16[256,1152]{1,0:T(8,128)(2,1)S(1)}, bf16[256,1152]{1,0:T(8,128)(2,1)S(1)}, u32[]{:S(2)}, u32[]{:S(2)}) collective-permute-start(bf16[256,1152]{1,0:T(8,128)(2,1)S(1)} %conv_grads.1.cg_ref.refs_0_), channel_id=1, source_target_pairs={{0,8},{4,12},{8,0},{12,4},{16,24},{20,28},{24,16},{28,20},{1,9},{5... | collective-permute-start | bytes 1769480 | tf_op jit(solution)/shard_map/ppermute | solution.py:447
  165.8 7.7 %collective-permute-start.40 = (bf16[4,288,128]{2,1,0:T(8,128)(2,1)S(1)}, bf16[4,288,128]{2,1,0:T(8,128)(2,1)S(1)}, u32[]{:S(2)}, u32[]{:S(2)}) collective-permute-start(bf16[4,288,128]{2,1,0:T(8,128)(2,1)S(1)} %get-tuple-element.109), channel_id=1, source_target_pairs={{0,4},{4,0},{8,12},{12,8},{16,20},{20,16},{24,28},{28,24},{1,5},{5... | collective-permute-start | bytes 884744 | tf_op jit(solution)/shard_map/ppermute | solution.py:447
  174.2 9.9 %collective-permute-start.41 = (bf16[1,8,288,128]{3,2,1,0:T(8,128)(2,1)S(1)}, bf16[1,8,288,128]{3,2,1,0:T(8,128)(2,1)S(1)}, u32[]{:S(2)}, u32[]{:S(2)}) collective-permute-start(bf16[1,8,288,128]{3,2,1,0:T(8,128)(2,1)S(1)} %bitcast.104), channel_id=1, source_target_pairs={{0,2},{1,3},{2,0},{3,1},{4,6},{5,7},{6,4},{7,5},{8,10},{9,11},{10,... | collective-permute-start | bytes 1769480 | tf_op jit(solution)/shard_map/ppermute | solution.py:447
  175.9 21.0 %collective-permute-start.34 = (bf16[256,1152]{1,0:T(8,128)(2,1)S(1)}, bf16[256,1152]{1,0:T(8,128)(2,1)}, u32[]{:S(2)}, u32[]{:S(2)}) collective-permute-start(bf16[256,1152]{1,0:T(8,128)(2,1)S(1)} %conv_grads.1.cg_ref.refs_0_), channel_id=1, source_target_pairs={{0,4},{4,0},{8,12},{12,8},{16,20},{20,16},{24,28},{28,24},{1,5},{5... | collective-permute-start | bytes 1769480 | tf_op jit(solution)/shard_map/ppermute | solution.py:447
  177.5 23.5 %collective-permute-start.37 = (bf16[256,1152]{1,0:T(8,128)(2,1)S(1)}, bf16[256,1152]{1,0:T(8,128)(2,1)}, u32[]{:S(2)}, u32[]{:S(2)}) collective-permute-start(bf16[256,1152]{1,0:T(8,128)(2,1)S(1)} %conv_grads.1.cg_ref.refs_0_), channel_id=1, source_target_pairs={{0,16},{4,20},{8,24},{12,28},{16,0},{20,4},{24,8},{28,12},{1,17},{... | collective-permute-start | bytes 1769480 | tf_op jit(solution)/shard_map/ppermute | solution.py:447
  185.2 25.9 %collective-permute-start.42 = (bf16[2,8,288,128]{3,2,1,0:T(8,128)(2,1)}, bf16[2,8,288,128]{3,2,1,0:T(8,128)(2,1)}, u32[]{:S(2)}, u32[]{:S(2)}) collective-permute-start(bf16[2,8,288,128]{3,2,1,0:T(8,128)(2,1)} %pad_maximum_fusion.2), channel_id=1, source_target_pairs={{0,1},{1,0},{2,3},{3,2},{4,5},{5,4},{6,7},{7,6},{8,9},{9,8},{10,11... | collective-permute-start | bytes 3538952 | tf_op jit(solution)/shard_map/ppermute | solution.py:447
  189.0 6.0 %collective-permute-start.43 = (f32[4,2048]{1,0:T(4,128)S(1)}, f32[4,2048]{1,0:T(4,128)S(1)}, u32[]{:S(2)}, u32[]{:S(2)}) collective-permute-start(f32[4,2048]{1,0:T(4,128)S(1)} %copy-done.29), channel_id=1, source_target_pairs={{0,4},{4,0},{8,12},{12,8},{16,20},{20,16},{24,28},{28,24},{1,5},{5... | collective-permute-start | bytes 98312 | tf_op jit(solution)/shard_map/ppermute | solution.py:447
  192.3 16.3 %collective-permute-start.36 = (bf16[256,1152]{1,0:T(8,128)(2,1)S(1)}, bf16[256,1152]{1,0:T(8,128)(2,1)}, u32[]{:S(2)}, u32[]{:S(2)}) collective-permute-start(bf16[256,1152]{1,0:T(8,128)(2,1)S(1)} %collective-permute-done.35.cg_ref.refs_2_), channel_id=1, source_target_pairs={{0,4},{4,0},{8,12},{12,8},{16,20},{20,16},{24,28},{28,24},{1,5},{5... | collective-permute-start | bytes 1769480 | tf_op jit(solution)/shard_map/ppermute | solution.py:447
  195.0 8.6 %collective-permute-start.45 = (f32[4,2048]{1,0:T(4,128)S(1)}, f32[4,2048]{1,0:T(4,128)S(1)}, u32[]{:S(2)}, u32[]{:S(2)}) collective-permute-start(f32[4,2048]{1,0:T(4,128)S(1)} %add.282), channel_id=1, source_target_pairs={{0,16},{4,20},{8,24},{12,28},{16,0},{20,4},{24,8},{28,12},{1,17},{... | collective-permute-start | bytes 98312 | tf_op jit(solution)/shard_map/ppermute | solution.py:447
  196.9 9.2 %collective-permute-start.46 = (f32[4,2048]{1,0:T(4,128)S(1)}, f32[4,2048]{1,0:T(4,128)S(1)}, u32[]{:S(2)}, u32[]{:S(2)}) collective-permute-start(f32[4,2048]{1,0:T(4,128)S(1)} %add.282), channel_id=1, source_target_pairs={{0,24},{4,28},{8,16},{12,20},{16,8},{20,12},{24,0},{28,4},{1,25},{... | collective-permute-start | bytes 98312 | tf_op jit(solution)/shard_map/ppermute | solution.py:447
  201.0 5.1 %collective-permute-start.44 = (f32[4,2048]{1,0:T(4,128)S(1)}, f32[4,2048]{1,0:T(4,128)S(1)}, u32[]{:S(2)}, u32[]{:S(2)}) collective-permute-start(f32[4,2048]{1,0:T(4,128)S(1)} %add.282), channel_id=1, source_target_pairs={{0,8},{4,12},{8,0},{12,4},{16,24},{20,28},{24,16},{28,20},{1,9},{5... | collective-permute-start | bytes 98312 | tf_op jit(solution)/shard_map/ppermute | solution.py:447
  203.5 14.6 %collective-permute-start.39 = (bf16[256,1152]{1,0:T(8,128)(2,1)S(1)}, bf16[256,1152]{1,0:T(8,128)(2,1)}, u32[]{:S(2)}, u32[]{:S(2)}) collective-permute-start(bf16[256,1152]{1,0:T(8,128)(2,1)S(1)} %copy-done.3), channel_id=1, source_target_pairs={{0,24},{4,28},{8,16},{12,20},{16,8},{20,12},{24,0},{28,4},{1,25},{... | collective-permute-start | bytes 1769480 | tf_op jit(solution)/shard_map/ppermute | solution.py:447
  206.1 17.2 %collective-permute-start.38 = (bf16[256,1152]{1,0:T(8,128)(2,1)}, bf16[256,1152]{1,0:T(8,128)(2,1)}, u32[]{:S(2)}, u32[]{:S(2)}) collective-permute-start(bf16[256,1152]{1,0:T(8,128)(2,1)} %collective-permute-done.37.cg_ref.refs_4_), channel_id=1, source_target_pairs={{0,4},{4,0},{8,12},{12,8},{16,20},{20,16},{24,28},{28,24},{1,5},{5... | collective-permute-start | bytes 1769480 | tf_op jit(solution)/shard_map/ppermute | solution.py:447
  218.1 14.9 %collective-permute-start.47 = (bf16[256,1152]{1,0:T(8,128)(2,1)}, bf16[256,1152]{1,0:T(8,128)(2,1)S(1)}, u32[]{:S(2)}, u32[]{:S(2)}) collective-permute-start(bf16[256,1152]{1,0:T(8,128)(2,1)} %collective-permute-done.39.cg_ref.refs_6_), channel_id=1, source_target_pairs={{0,4},{4,0},{8,12},{12,8},{16,20},{20,16},{24,28},{28,24},{1,5},{5... | collective-permute-start | bytes 1769480 | tf_op jit(solution)/shard_map/ppermute | solution.py:447
  272.9 4.9 %collective-permute-start.48 = (bf16[1152,1024]{1,0:T(8,128)(2,1)}, bf16[1152,1024]{1,0:T(8,128)(2,1)}, u32[]{:S(2)}, u32[]{:S(2)}) collective-permute-start(bf16[1152,1024]{1,0:T(8,128)(2,1)} %pad_maximum_fusion.1), channel_id=1, source_target_pairs={{0,1},{1,0},{2,3},{3,2},{4,5},{5,4},{6,7},{7,6},{8,9},{9,8},{10,11... | collective-permute-start | bytes 7077896 | tf_op jit(solution)/shard_map/ppermute | solution.py:447
  282.8 68.6 %collective-permute-start.49 = (bf16[1152,512]{1,0:T(8,128)(2,1)S(1)}, bf16[1152,512]{1,0:T(8,128)(2,1)S(1)}, u32[]{:S(2)}, u32[]{:S(2)}) collective-permute-start(bf16[1152,512]{1,0:T(8,128)(2,1)S(1)} %fusion), channel_id=1, source_target_pairs={{0,2},{1,3},{2,0},{3,1},{4,6},{5,7},{6,4},{7,5},{8,10},{9,11},{10,... | collective-permute-start | bytes 3538952 | tf_op jit(solution)/shard_map/ppermute | solution.py:447
  284.7 6.3 %collective-permute-start.50 = (bf16[320,256]{1,0:T(8,128)(2,1)S(1)}, bf16[320,256]{1,0:T(8,128)(2,1)S(1)}, u32[]{:S(2)}, u32[]{:S(2)}) collective-permute-start(bf16[320,256]{1,0:T(8,128)(2,1)S(1)} %pad_maximum_fusion.7), channel_id=1, source_target_pairs={{0,4},{4,0},{8,12},{12,8},{16,20},{20,16},{24,28},{28,24},{1,5},{5... | collective-permute-start | bytes 491528 | tf_op jit(solution)/shard_map/ppermute | solution.py:447
  291.1 60.3 %collective-permute-start.51 = (bf16[320,256]{1,0:T(8,128)(2,1)S(1)}, bf16[320,256]{1,0:T(8,128)(2,1)S(1)}, u32[]{:S(2)}, u32[]{:S(2)}) collective-permute-start(bf16[320,256]{1,0:T(8,128)(2,1)S(1)} %add_convert_fusion), channel_id=1, source_target_pairs={{0,8},{4,12},{8,0},{12,4},{16,24},{20,28},{24,16},{28,20},{1,9},{5... | collective-permute-start | bytes 491528 | tf_op jit(solution)/shard_map/ppermute | solution.py:447
  309.2 42.2 %collective-permute-start.52 = (bf16[320,256]{1,0:T(8,128)(2,1)S(1)}, bf16[320,256]{1,0:T(8,128)(2,1)S(1)}, u32[]{:S(2)}, u32[]{:S(2)}) collective-permute-start(bf16[320,256]{1,0:T(8,128)(2,1)S(1)} %add_convert_fusion), channel_id=1, source_target_pairs={{0,16},{4,20},{8,24},{12,28},{16,0},{20,4},{24,8},{28,12},{1,17},{... | collective-permute-start | bytes 491528 | tf_op jit(solution)/shard_map/ppermute | solution.py:447
  309.8 41.6 %collective-permute-start.53 = (bf16[320,256]{1,0:T(8,128)(2,1)S(1)}, bf16[320,256]{1,0:T(8,128)(2,1)S(1)}, u32[]{:S(2)}, u32[]{:S(2)}) collective-permute-start(bf16[320,256]{1,0:T(8,128)(2,1)S(1)} %add_convert_fusion), channel_id=1, source_target_pairs={{0,24},{4,28},{8,16},{12,20},{16,8},{20,12},{24,0},{28,4},{1,25},{... | collective-permute-start | bytes 491528 | tf_op jit(solution)/shard_map/ppermute | solution.py:447
  (61 other events, 747.3 us)
Sparse Core Ops, SparseCore 0:
  22.6 138.8 all-gather.4
  251.1 89.8 all-gather.6

commit v3 on v2

--- a/solution.py
+++ b/solution.py
@@ -153,7 +153,7 @@
 
 
 def combine_kernel(lim_ref, centre_ref, *refs, slabs, cols):
-    halo, (conv_ref, send_ref, stat_ref) = refs[:6], refs[6:]
+    halo, (extra_ref, conv_ref, send_ref, message_ref, local_ref) = refs[:6], refs[6:]
     cells = slabs * cols
     half = cells // 2
     W = centre_ref.shape[1]
@@ -178,36 +178,67 @@
         q = jnp.sum(part * part * mask, axis=0, keepdims=True)
         local = s / own
         send_ref[:, lo : lo + 2 * L] = (part - local).astype(bf16)
-        stat_ref[:, lo : lo + 2 * L] = jnp.concatenate([s, q, local, jnp.zeros((5, 2 * L), f32)], axis=0)
+        message_ref[:8, lo : lo + 2 * L] = extra_ref[:8, lo : lo + 2 * L] + jnp.concatenate(
+            [s, q, jnp.zeros((6, 2 * L), f32)], axis=0
+        )
+        local_ref[:, lo : lo + 2 * L] = jnp.concatenate(
+            [jnp.zeros((2, 2 * L), f32), local, jnp.zeros((5, 2 * L), f32)], axis=0
+        )
+    message_ref[8:] = extra_ref[8:]
+
+
+def norm_of(total, square, n):
+    mean = total / n
+    return mean, lax.rsqrt(square / n - mean * mean + epsilon)
+
+
+def added(parts):
+    a, b, c, d = (r[...] for r in parts)
+    return (a + b) + (c + d)
 
 
 def mix_kernel(
-    lim_ref, conv_ref, c1_ref, c2_ref, c3_ref, stat_ref, gain_ref, wbranch_ref, pool_ref, wpool_ref,
-    mixed_ref, act_ref, sums_ref, scratch, *, slabs, cols, images
+    lim_ref, n_ref, conv_ref, c1_ref, c2_ref, c3_ref, t0, t1, t2, t3, p0, p1, p2, p3,
+    mixed_ref, act_ref, sums_ref, stat_ref, scratch, *, slabs, cols, images
 ):
-    cells = slabs * cols
     per = slabs // images
-    for d, ref in enumerate((conv_ref, c1_ref, c2_ref, c3_ref)):
-        mean, rstd, local = stat_ref[d, 0:1], stat_ref[d, 1:2], stat_ref[d, 2:3]
-        offset = mean if d == 0 else mean - local
-        scale = rstd * gain_ref[d, 0:1]
-        shift = gain_ref[d, 1:2]
+    n = n_ref[0]
+    width = conv_ref.shape[1]
+    L = width // 4
+    cid = lax.broadcasted_iota(jnp.int32, (cols, width), 0)
+    pooled = None
+    for d, (ref, tile_ref, par_ref) in enumerate(
+        ((conv_ref, t0, p0), (c1_ref, t1, p1), (c2_ref, t2, p2), (c3_ref, t3, p3))
+    ):
+        tile = tile_ref[...]
+        par = par_ref[5 * L :].astype(f32)
+        par = par[0:4] + par[4:8] + par[8:12]
+        gain = par[0:1]
+        shift = jnp.concatenate([par[1:2, 2 * L :], par[2:3, : 2 * L]], axis=1)
+        mean, rstd = norm_of(tile[0:1], tile[1:2], n)
+        offset = mean if d == 0 else mean - tile[2:3]
+        scale = rstd * gain
+        if d == 0:
+            stat_ref[...] = jnp.concatenate([mean, rstd, gain, shift, jnp.zeros((4, width), f32)], axis=0)
         dest = act_ref if d == 0 else scratch
-        width = ref.shape[1]
-        cid = lax.broadcasted_iota(jnp.int32, (cols, width), 0)
         for i in range(slabs):
             rows = slice(i * cols, (i + 1) * cols)
             pre = (ref[rows].astype(f32) - offset) * scale + shift
             _, act = silu_parts(pre)
             dest[rows] = jnp.where(cid < lim_ref[i], act, 0.0).astype(bf16)
-        part = dot(dest[...], wbranch_ref[d], NN)
+        part = dot(dest[...], par_ref[:width], NN)
         if d == 0:
             mixed_ref[...] = part
         else:
             mixed_ref[...] += part
-    pooled = dot(pool_ref[0], wpool_ref[0], NN)
-    for d in range(1, 4):
-        pooled += dot(pool_ref[d], wpool_ref[d], NN)
+        projected = tile[4 : 4 + images, :L]
+        pmean, prstd = norm_of(
+            jnp.sum(projected, axis=0, keepdims=True), jnp.sum(projected * projected, axis=0, keepdims=True), images
+        )
+        _, pact = silu_parts(par[1:2, :L] * ((projected - pmean) * prstd) + par[2:3, 2 * L : 3 * L])
+        pact = jnp.concatenate([pact, jnp.zeros((16 - images, L), f32)], axis=0).astype(bf16)
+        part = dot(pact, par_ref[width : width + L], NN)
+        pooled = part if d == 0 else pooled + part
     F = mixed_ref.shape[1]
     cid = lax.broadcasted_iota(jnp.int32, (cols, F), 0)
     s = jnp.zeros((cols, F), f32)
@@ -222,9 +253,26 @@
     sums_ref[...] = column_sums(s, q)
 
 
-def final_kernel(lim_ref, mixed_ref, grad_ref, stat_ref, out_ref, dt_ref, sums_ref, *, slabs, cols):
+def final_kernel(
+    lim_ref, n_ref, own_ref, mixed_ref, grad_ref, p0, p1, p2, p3, s0, s1, s2, s3, out_ref, dt_ref, sums_ref, stat_ref,
+    *, slabs, cols
+):
     F = mixed_ref.shape[1]
-    mean, rstd, gain, shift = (stat_ref[i : i + 1] for i in range(4))
+    total = added((s0, s1, s2, s3))
+    mean, rstd = norm_of(total[0:1], total[1:2], n_ref[0])
+    L = F // 4
+    group = lax.broadcasted_iota(jnp.int32, (8, F), 1) // L
+    gain, shift = jnp.zeros((8, F), f32), jnp.zeros((8, F), f32)
+    for d, ref in enumerate((p0, p1, p2, p3)):
+        par = ref[5 * L :].astype(f32)
+        par = par[0:4] + par[4:8] + par[8:12]
+        here = group == (own_ref[0] ^ d)
+        g = jnp.where(group == 1, jnp.broadcast_to(par[1:2], (8, F)), 0.0)
+        h = jnp.where(group == 3, jnp.broadcast_to(par[2:3], (8, F)), 0.0)
+        gain += jnp.where(here, g + pltpu.roll(g, L, 1) + pltpu.roll(g, 2 * L, 1) + pltpu.roll(g, 3 * L, 1), 0.0)
+        shift += jnp.where(here, h + pltpu.roll(h, L, 1) + pltpu.roll(h, 2 * L, 1) + pltpu.roll(h, 3 * L, 1), 0.0)
+    gain, shift = gain[0:1], shift[0:1]
+    stat_ref[...] = jnp.concatenate([mean, rstd, gain, shift, jnp.zeros((4, F), f32)], axis=0)
     cid = lax.broadcasted_iota(jnp.int32, (cols, F), 0)
     s = jnp.zeros((cols, F), f32)
     q = jnp.zeros((cols, F), f32)
@@ -243,13 +291,15 @@
 
 
 def branch_kernel(
-    lim_ref, mixed_ref, fdt_ref, fstat_ref, conv_ref, act_ref, stat_ref, wbranch_ref,
+    lim_ref, n_ref, mixed_ref, fdt_ref, fstat_ref, conv_ref, act_ref, stat_ref, wbranch_ref, s0, s1, s2, s3,
     dt_ref, gproj_ref, image_ref, sums_ref, grad, *, slabs, cols, images
 ):
     F = mixed_ref.shape[1]
     W = conv_ref.shape[1]
     per = slabs // images
-    mean, rstd, scale, beta, gamma = (fstat_ref[i : i + 1] for i in range(5))
+    mean, rstd, scale = fstat_ref[0:1], fstat_ref[1:2], fstat_ref[1:2] * fstat_ref[2:3]
+    total = added((s0, s1, s2, s3)) / n_ref[0]
+    beta, gamma = total[0:1], total[1:2]
     cid = lax.broadcasted_iota(jnp.int32, (cols, F), 0)
     image_sums = []
     for image in range(images):
@@ -281,16 +331,20 @@
     sums_ref[...] = column_sums(s, q)
 
 
-def grad_kernel(lim_ref, dt_ref, conv_ref, stat_ref, cg_ref, scratch, *, slabs, cols):
+def grad_kernel(lim_ref, n_ref, dt_ref, conv_ref, stat_ref, sums_ref, piece_ref, cg_ref, scratch, *, slabs, cols):
     W = conv_ref.shape[1]
-    mean, rstd, scale, beta, gamma = (stat_ref[i : i + 1] for i in range(5))
+    mean, rstd, scale = stat_ref[0:1], stat_ref[1:2], stat_ref[1:2] * stat_ref[2:3]
+    beta, gamma = sums_ref[0:1] / n_ref[0], sums_ref[1:2] / n_ref[0]
     cid = lax.broadcasted_iota(jnp.int32, (cols, W), 0)
     for i in range(slabs):
         rows = slice(i * cols, (i + 1) * cols)
         normed = (conv_ref[rows] - mean) * rstd
         g = scale * (dt_ref[rows] - beta - normed * gamma)
         scratch[rows] = jnp.where(cid < lim_ref[i], g, 0.0)
-    cg_ref[...] = scratch[...].T.astype(bf16)
+    cg_ref[:W] = scratch[...].T.astype(bf16)
+    F = piece_ref.shape[1]
+    for k in range(piece_ref.shape[0] // 16):
+        cg_ref[W:, k * F : (k + 1) * F] = piece_ref[k * 16 : (k + 1) * 16].astype(bf16)
 
 
 def shifted(f, v, d, col, cols):
@@ -323,7 +377,8 @@
             spot = dest.at[:, pl.ds(pl.multiple_of(place * cells, 128), cells)]
         else:
             spot = dest.at[place]
-        copies.append(pltpu.make_async_copy(ref, spot, sems.at[d]))
+        source = ref if lanes else ref.at[pl.ds(0, dest.shape[1])]
+        copies.append(pltpu.make_async_copy(source, spot, sems.at[d]))
     for c in copies:
         c.start()
     return copies
@@ -367,12 +422,26 @@
 
 
 def wide_kernel(pos_ref, x_ref, *refs):
-    blocks, (acc_ref, point_ref, taps, sems) = refs[:BLOCKS], refs[BLOCKS:]
+    blocks, pieces, (acc_ref, point_ref, proj_ref, taps, sems) = (
+        refs[:BLOCKS],
+        refs[BLOCKS : 2 * BLOCKS],
+        refs[2 * BLOCKS :],
+    )
     L = point_ref.shape[0]
+    F = proj_ref.shape[1]
+    rows = proj_ref.shape[0] // BLOCKS
 
     @pl.when(pl.program_id(0) == 0)
     def _():
-        for c in fetch_blocks(pos_ref[0], blocks, taps, sems, lanes=True):
+        copies = fetch_blocks(pos_ref[0], blocks, taps, sems, lanes=True)
+        for d in range(BLOCKS):
+            p = pos_ref[0] ^ d
+            base = (p % 2 * (BLOCKS // 2) + p // 2) * rows
+            for k in range(0, rows, 16):
+                n = min(16, rows - k)
+                value = pieces[d][:, k // 16 * F : (k // 16 + 1) * F].astype(f32)
+                proj_ref[pl.ds(pl.multiple_of(base + k, 8), n)] = value[:n]
+        for c in copies:
             c.wait()
 
     def store(lo, value):
@@ -393,7 +462,7 @@
 
 
 def input_grad_kernel(pos_ref, lim_ref, col_ref, w_ref, wp_ref, pool_ref, *refs, slabs, cols, rates, images):
-    blocks, (out_ref, cg, lhs, rhs, sems) = refs[:BLOCKS], refs[BLOCKS:]
+    blocks, (keep_ref, give_ref, cg, lhs, rhs, sems) = refs[:BLOCKS], refs[BLOCKS:]
     L = wp_ref.shape[0]
     s = pos_ref[0]
 
@@ -419,14 +488,26 @@
 
     rhs[: 27 * L] = w_ref[...]
     rhs[27 * L :] = wp_ref[...]
-    width = out_ref.shape[2]
+    width = keep_ref.shape[2]
     per = slabs // images
     cid = lax.broadcasted_iota(jnp.int32, (cols, 256), 0)
-    for n in range(0, width, 256):
-        part = dot(lhs[...], rhs[:, n : n + 256], NN)
-        for i in range(slabs):
-            value = part[i * cols : (i + 1) * cols] + pool_ref[i // per : i // per + 1, n : n + 256]
-            out_ref[0, i * cols : (i + 1) * cols, n : n + 256] = jnp.where(cid < lim_ref[i], value, 0.0).astype(bf16)
+
+    def fill(out_ref):
+        for n in range(0, width, 256):
+            part = dot(lhs[...], rhs[:, n : n + 256], NN)
+            for i in range(slabs):
+                value = part[i * cols : (i + 1) * cols] + pool_ref[i // per : i // per + 1, n : n + 256]
+                out_ref[0, i * cols : (i + 1) * cols, n : n + 256] = jnp.where(
+                    cid < lim_ref[i], value, 0.0
+                ).astype(bf16)
+
+    @pl.when(pl.program_id(0) % 2 == 0)
+    def _():
+        fill(keep_ref)
+
+    @pl.when(pl.program_id(0) % 2 == 1)
+    def _():
+        fill(give_ref)
 
 
 def grouped(pairs, size):
@@ -447,10 +528,9 @@
     return lax.ppermute(block, axis, [(i, i ^ bits) for i in range(lax.axis_size(axis))])
 
 
-def sum_over_sp(x):
+def parts_over_sp(x):
     x = x + swap(x, "sp", 1)
-    parts = [swap(x, "sp", b) for b in (2, 4, 6)]
-    return (x + parts[0]) + (parts[1] + parts[2])
+    return [x] + [swap(x, "sp", b) for b in (2, 4, 6)]
 
 
 def swaps_over_sp(x):
@@ -461,20 +541,18 @@
 
 
 def after(x, *others):
-    return lax.optimization_barrier((x,) + others)[0]
+    return lax.optimization_barrier((x, others))[0]
 
 
 def thirds(x):
     hi = lax.reduce_precision(x, 8, 7)
     mid = lax.reduce_precision(x - hi, 8, 7)
-    return jnp.stack([hi, mid, x - hi - mid]).astype(bf16)
-
-
-def sum_over_sp_bf16(x):
-    x = x.astype(bf16)
-    x = (x.astype(f32) + swap(x, "sp", 1).astype(f32)).astype(bf16)
-    parts = [swap(x, "sp", b).astype(f32) for b in (2, 4, 6)]
-    return (x.astype(f32) + parts[0]) + (parts[1] + parts[2])
+    return jnp.concatenate([hi, mid, x - hi - mid], axis=0).astype(bf16)
+
+
+def whole(parts):
+    hi, mid, low = jnp.split(parts.astype(f32), 3, axis=0)
+    return hi + mid + low
 
 
 def plain_from_behind(block, axis, distance):
@@ -746,19 +824,14 @@
     x = features.reshape(cells, C)
     og = out_grad.reshape(cells, F)
 
-    norms = jnp.concatenate([bn_gains, bn_shifts, jnp.zeros((4, L), f32)], axis=0)
+    norms = jnp.concatenate([bn_gains, bn_shifts, jnp.zeros((4, L), f32)], axis=0).reshape(4, W)
     wp = w_proj.reshape(5 * L, F)
-    packed = jnp.concatenate([wp, thirds(norms).reshape(-1, F)], axis=0)
+    packed = jnp.concatenate([wp, thirds(norms), jnp.zeros((4, F), bf16)], axis=0)
     packed_y = swap(packed, "ch", 2)
-    packed_all = jnp.stack([packed, swap(packed, "ch", 1), packed_y, swap(packed_y, "ch", 1)])
-    wp_all = packed_all[:, : 5 * L]
-    norms_all = jnp.sum(packed_all[:, 5 * L :].reshape(4, 3, 16, L).astype(f32), axis=1)
-    wbranch_all, wpool_all = wp_all[:, :W], wp_all[:, W:]
-    natural = (own ^ jnp.arange(4))[:, None] == jnp.arange(4)[None, :]
-    final_par = jnp.sum(
-        jnp.where(natural[:, :, None, None], norms_all[None, :, (5, 11), :], 0.0), axis=1
-    )
-    final_gain, final_shift = final_par[:, 0].reshape(F), final_par[:, 1].reshape(F)
+    packed_core = swap(packed, "ch", 1)
+    packed_all = [packed, packed_core, packed_y, swap(packed_y, "ch", 1)]
+    count = n.reshape(1)
+    own_id = own.astype(jnp.int32).reshape(1)
 
     KT = 512
     steps = C // KT
@@ -787,6 +860,7 @@
             cost_estimate=cost(2 * cells * C * 6 * len(which) * L, 10e6),
             name="side_taps",
         )(lim, jnp.stack([first[j] for j in which]), x, *[atrous_weight] * (2 * len(which)))
+        out = after(tuple(out), packed_y, packed_core)
         moved = []
         for i, j in enumerate(which):
             moved += neighbours(out[2 * i], out[2 * i + 1], "sp", dilation_factors[j])
@@ -804,9 +878,9 @@
     wide_w = (C - narrow) // 4
     own_wide = lax.dynamic_slice_in_dim(x, narrow + own * wide_w, wide_w, 1)
     own_wide = jnp.where(valid, own_wide, jnp.zeros((), bf16))
-    halo, made = side_taps((0, 1, 2), x)
-    x_wide = lax.all_gather(after(own_wide, made), ("sp", "ch"), axis=0).reshape(BLOCKS, 4, cells, wide_w)
-    x_then = after(x, made, mine, own_wide)
+    halo, made = side_taps((0, 1, 2), after(x, packed, own_wide, *sent))
+    x_wide = lax.all_gather(own_wide, ("sp", "ch"), axis=0).reshape(BLOCKS, 4, cells, wide_w)
+    x_then = after(x, made, halo[0], halo[1], mine)
     centre, sums = pl.pallas_call(
         functools.partial(centre_kernel, steps=steps, slabs=slabs, cols=cols, rates=rates, images=images),
         grid=(steps,),
@@ -826,83 +900,76 @@
     own_pooled = sums[:images] / own_count[:, None]
     proj_part = lax.dot_general(own_pooled, w_pool.astype(f32), NT, precision=highest_precision)
 
-    conv, conv_send, stat = pl.pallas_call(
+    extra = jnp.concatenate(
+        [jnp.pad(proj_part, ((4, 4 - images), (0, W - L))), own_pooled.reshape(-1, W)], axis=0
+    )
+    conv, conv_send, message, local = pl.pallas_call(
         functools.partial(combine_kernel, slabs=slabs, cols=cols),
-        in_specs=[SMEM] + [VMEM] * 7,
-        out_specs=[VMEM] * 3,
+        in_specs=[SMEM] + [VMEM] * 8,
+        out_specs=[VMEM] * 4,
         out_shape=[
             jax.ShapeDtypeStruct((cells, W), f32),
             jax.ShapeDtypeStruct((cells, W), bf16),
+            jax.ShapeDtypeStruct(extra.shape, f32),
             jax.ShapeDtypeStruct((8, W), f32),
         ],
         compiler_params=params(20),
         cost_estimate=cost(2e6, 4e6),
         name="combine_taps",
-    )(lim, centre, *halo)
+    )(lim, centre, *halo, extra)
     conv_y = swap(conv_send, "ch", 2)
     conv_core = swap(conv_send, "ch", 1)
-    conv_diag = swap(conv_y, "ch", 1)
-    tile = jnp.concatenate([stat[:4], jnp.pad(proj_part, ((0, 0), (0, W - L)))], axis=0)
-    tile = sum_over_sp(tile)
+    message = parts_over_sp(message)
+    conv_diag = swap(after(conv_y, *message), "ch", 1)
+    tile = ((message[0][:8] + message[1][:8]) + (message[2][:8] + message[3][:8])) + local
     mine = after(mine, tile)
     keep = lax.dynamic_slice_in_dim(mine, (block_id % 2) * cut, cut, 2)
     give = lax.dynamic_slice_in_dim(mine, (1 - block_id % 2) * cut, cut, 2)
     taken = swap(give, "sp", 1)
-    tile = jnp.concatenate([tile[:2], stat[2:3], tile[3:]], axis=0)
-    tiles = jnp.stack([tile] + [swap(tile, "ch", b) for b in (1, 2, 3)])
-    mean = tiles[:, 0] / n
-    rstd = lax.rsqrt(tiles[:, 1] / n - mean * mean + epsilon)
-    branch_stat = jnp.stack([mean, rstd, tiles[:, 2]], axis=1)
-    branch_par = jnp.stack([norms_all[:, :4].reshape(4, W), norms_all[:, 6:10].reshape(4, W)], axis=1)
-    projected = tiles[:, 4 : 4 + images, :L]
-    pool_mean = jnp.mean(projected, axis=1, keepdims=True)
-    pool_rstd = lax.rsqrt(
-        jnp.mean(projected * projected, axis=1, keepdims=True) - pool_mean * pool_mean + epsilon
-    )
+    tiles = [tile] + [swap(tile, "ch", b) for b in (1, 2, 3)]
+    projected = tile[4 : 4 + images, :L]
+    pool_mean = jnp.mean(projected, axis=0)
+    pool_rstd = lax.rsqrt(jnp.mean(projected * projected, axis=0) - pool_mean * pool_mean + epsilon)
     pool_normed = (projected - pool_mean) * pool_rstd
-    pool_pre = norms_all[:, 4:5] * pool_normed + norms_all[:, 10:11]
+    pool_pre = bn_gains[4] * pool_normed + bn_shifts[4]
     pool_act = jax.nn.silu(pool_pre).astype(bf16)
-    pool_in = jnp.pad(pool_act, ((0, 0), (0, 8 - images), (0, 0)))
-
-    mixed, act, mixed_stat = pl.pallas_call(
+
+    mixed, act, mixed_stat, own_stat = pl.pallas_call(
         functools.partial(mix_kernel, slabs=slabs, cols=cols, images=images),
-        in_specs=[SMEM] + [VMEM] * 9,
-        out_specs=[VMEM] * 3,
+        in_specs=[SMEM] * 2 + [VMEM] * 12,
+        out_specs=[VMEM] * 4,
         out_shape=[
             jax.ShapeDtypeStruct((cells, F), f32),
             jax.ShapeDtypeStruct((cells, W), bf16),
             jax.ShapeDtypeStruct((8, F), f32),
+            jax.ShapeDtypeStruct((8, W), f32),
         ],
         scratch_shapes=[pltpu.VMEM((cells, W), bf16)],
         compiler_params=params(20),
         cost_estimate=cost(2 * cells * 4 * W * F, 6e6),
         name="mix_branches",
-    )(lim, conv, conv_core, conv_y, conv_diag, branch_stat, branch_par, wbranch_all, pool_in, wpool_all)
-    total = sum_over_sp(mixed_stat)
-    fmean = total[0] / n
-    frstd = lax.rsqrt(total[1] / n - fmean * fmean + epsilon)
-    final_stat = jnp.stack([fmean, frstd, final_gain, final_shift])
-    out_all, fdt, fsums = pl.pallas_call(
+    )(lim, count, conv, conv_core, conv_y, conv_diag, *tiles, *packed_all)
+    total = parts_over_sp(mixed_stat)
+    out_all, fdt, fsums, fstat = pl.pallas_call(
         functools.partial(final_kernel, slabs=slabs, cols=cols),
-        in_specs=[SMEM] + [VMEM] * 3,
-        out_specs=[VMEM] * 3,
+        in_specs=[SMEM] * 3 + [VMEM] * 10,
+        out_specs=[VMEM] * 4,
         out_shape=[
             jax.ShapeDtypeStruct((cells, F), bf16),
             jax.ShapeDtypeStruct((cells, F), f32),
+            jax.ShapeDtypeStruct((8, F), f32),
             jax.ShapeDtypeStruct((8, F), f32),
         ],
         compiler_params=params(20),
         cost_estimate=cost(2e6, 4e6),
         name="final_norm",
-    )(lim, mixed, og, final_stat)
-    ftotal = sum_over_sp(fsums)
-    final_beta, final_gamma = ftotal[0], ftotal[1]
-    fgrad_stat = jnp.stack([fmean, frstd, frstd * final_gain, final_beta / n, final_gamma / n])
-    own_gain, own_shift = branch_par[0, 0], branch_par[0, 1]
-    own_mean, own_rstd = branch_stat[0, 0], branch_stat[0, 1]
+    )(lim, count, own_id, mixed, og, *packed_all, *total)
+    ftotal = parts_over_sp(fsums)
+    final_sums = (ftotal[0] + ftotal[1]) + (ftotal[2] + ftotal[3])
+    final_beta, final_gamma = final_sums[0], final_sums[1]
     dt, gproj, image_sums, bsums = pl.pallas_call(
         functools.partial(branch_kernel, slabs=slabs, cols=cols, images=images),
-        in_specs=[SMEM] + [VMEM] * 7,
+        in_specs=[SMEM] * 2 + [VMEM] * 11,
         out_specs=[VMEM] * 4,
         out_shape=[
             jax.ShapeDtypeStruct((cells, W), f32),
@@ -915,31 +982,56 @@
         cost_estimate=cost(4 * cells * W * F, 8e6),
         name="branch_grads",
     )(
-        lim, mixed, fdt, fgrad_stat, conv, act,
-        jnp.stack([own_mean, own_rstd, own_gain, own_shift]), wp[:W],
+        lim, count, mixed, fdt, fstat, conv, act, own_stat, wp[:W], *ftotal
     )
     image_sums = image_sums[:images]
     pool_part = lax.dot_general(image_sums, w_proj[4].astype(f32), NT, precision=highest_precision)
-    gproj_pool = lax.dot_general(pool_act[0].astype(f32), image_sums, TN, precision=highest_precision)
-    btile = sum_over_sp(
-        jnp.concatenate([bsums[:4], jnp.pad(pool_part, ((0, 0), (0, W - L)))], axis=0)
-    )
+    gproj_pool = lax.dot_general(pool_act.astype(f32), image_sums, TN, precision=highest_precision)
+    gp = jnp.concatenate([gproj, gproj_pool], axis=0)
+    across, along = block_id % 2, block_id // 2
+    gp_half, gp_piece = gp.shape[0] // 2, gp.shape[0] // BLOCKS
+    bown = jnp.concatenate([bsums[:4], jnp.pad(pool_part, ((0, 0), (0, W - L)))], axis=0)
+    got = swap(
+        jnp.concatenate(
+            [thirds(bown), lax.dynamic_slice_in_dim(gp, (1 - across) * gp_half, gp_half).astype(bf16)], axis=0
+        ),
+        "sp",
+        1,
+    )
+    bown = bown + whole(got[:24])
+    gp = lax.dynamic_slice_in_dim(gp, across * gp_half, gp_half) + got[24:].astype(f32)
+    mine_thirds = thirds(bown)
+    got = [
+        swap(
+            jnp.concatenate(
+                [mine_thirds, lax.dynamic_slice_in_dim(gp, (along ^ dz) * gp_piece, gp_piece).astype(bf16)],
+                axis=0,
+            ),
+            "sp",
+            2 * dz,
+        )
+        for dz in (1, 2, 3)
+    ]
+    btile = (bown + whole(got[0][:24])) + (whole(got[1][:24]) + whole(got[2][:24]))
+    gp = lax.dynamic_slice_in_dim(gp, along * gp_piece, gp_piece)
+    gp = (gp + got[0][24:].astype(f32)) + (got[1][24:].astype(f32) + got[2][24:].astype(f32))
+    gp = jnp.pad(gp, ((0, -gp_piece % 16), (0, 0)))
     branch_beta, branch_gamma = btile[0], btile[1]
     cgt = pl.pallas_call(
         functools.partial(grad_kernel, slabs=slabs, cols=cols),
-        in_specs=[SMEM] + [VMEM] * 3,
+        in_specs=[SMEM] * 2 + [VMEM] * 5,
         out_specs=VMEM,
-        out_shape=jax.ShapeDtypeStruct((W, cells), bf16),
+        out_shape=jax.ShapeDtypeStruct((W + 16, cells), bf16),
         scratch_shapes=[pltpu.VMEM((cells, W), f32)],
         compiler_params=params(20),
         cost_estimate=cost(2e6, 4e6),
         name="conv_grads",
-    )(lim, dt, conv, jnp.stack([own_mean, own_rstd, own_rstd * own_gain, branch_beta / n, branch_gamma / n]))
-    pool_dt = btile[4 : 4 + images, :L] * silu_slope(pool_pre[0])
+    )(lim, count, dt, conv, own_stat, btile, gp)
+    pool_dt = btile[4 : 4 + images, :L] * silu_slope(pool_pre)
     pool_beta = jnp.sum(pool_dt, axis=0)
-    pool_gamma = jnp.sum(pool_dt * pool_normed[0], axis=0)
+    pool_gamma = jnp.sum(pool_dt * pool_normed, axis=0)
     proj_grad = (
-        pool_rstd[0] * bn_gains[4] * (pool_dt - pool_beta / images - pool_normed[0] * pool_gamma / images)
+        pool_rstd * bn_gains[4] * (pool_dt - pool_beta / images - pool_normed * pool_gamma / images)
     )
     g_gains = jnp.concatenate([branch_gamma.reshape(4, L), pool_gamma[None],
         lax.dynamic_slice_in_dim(final_gamma, own * L, L)[None]], axis=0)
@@ -965,17 +1057,20 @@
             name="column_taps",
         )(col_row, block)
 
-    near = [swap(cgt, "sp", b) for b in (2, 4, 6)]
+    near = [swap(cgt, "sp", b) for b in (2, 4)]
+    near.append(swap(after(cgt, near[1]), "sp", 6))
     pair = swap(cgt, "sp", 1)
     taps = [column_taps(cgt), column_taps(pair), column_taps(near[0])]
     near_pair = swap(near[0], "sp", 1)
     taps.append(column_taps(near_pair))
-    x_slices = after(jnp.stack([keep, taken], axis=1).reshape(1, BLOCKS, part, cut), near[0])
+    message = after(tuple(message), pair)
+    pooled = ((message[0][8:] + message[1][8:]) + (message[2][8:] + message[3][8:])).reshape(images, C)
+    x_slices = after(jnp.stack([keep, taken], axis=1).reshape(1, BLOCKS, part, cut), pair)
     x_slices = jnp.concatenate([x_slices, swap(x_slices, "ch", 2)], axis=0)
     x_core = swap(x_slices, "ch", 1)
     x_slices = jnp.stack([x_slices[0], x_core[0], x_slices[1], x_core[1]])
-    pooled = sum_over_sp(after(own_pooled, near[0]))
-    far = [after(near[1], *taps[:3]), after(near[2], *taps, x_slices, pooled)]
+    g_pool = jnp.einsum("kf,kc->fc", proj_grad, pooled, precision=highest_precision)
+    far = [after(near[1], *taps[:2], output, g_pool, g_gains, g_shifts, pooled_grad), after(near[2], *taps)]
     far_pairs = [swap(t, "sp", 1) for t in far]
     blocks = [cgt, pair, near[0], near_pair, far[0], far_pairs[0], far[1], far_pairs[1]]
     taps += [column_taps(t) for t in blocks[4:]]
@@ -1000,7 +1095,7 @@
     gw_all = lax.all_gather(gw, "sp", axis=0)
     pos, gw = lax.optimization_barrier((pos, gw))
     group = C // 4
-    ig = pl.pallas_call(
+    ig_keep, ig_give = pl.pallas_call(
         functools.partial(input_grad_kernel, slabs=slabs, cols=cols, rates=rates, images=images),
         grid_spec=pltpu.PrefetchScalarGridSpec(
             num_scalar_prefetch=2,
@@ -1012,7 +1107,7 @@
                 pl.BlockSpec((8, group), lambda i, p, l: (0, p[2] ^ i)),
             ]
             + [ANY] * BLOCKS,
-            out_specs=pl.BlockSpec((1, cells, group), lambda i, p, l: (i, 0, 0)),
+            out_specs=[pl.BlockSpec((1, cells, group), lambda i, p, l: (i // 2, 0, 0))] * 2,
             scratch_shapes=[
                 pltpu.VMEM((BLOCKS, W, cells), bf16),
                 pltpu.VMEM((cells, 28 * L), bf16),
@@ -1020,48 +1115,48 @@
                 pltpu.SemaphoreType.DMA((BLOCKS,)),
             ],
         ),
-        out_shape=jax.ShapeDtypeStruct((4, cells, group), bf16),
+        out_shape=[jax.ShapeDtypeStruct((2, cells, group), bf16)] * 2,
         compiler_params=params(),
         cost_estimate=cost(1e6, 1e6),
         name="input_grads",
     )(pos, lim, col_row, atrous_weight.reshape(27 * L, C), w_point,
       jnp.pad(pooled_grad, ((0, 8 - images), (0, 0))), *blocks)
-    gp = after(jnp.concatenate([gproj, gproj_pool], axis=0).astype(bf16), gw)
-    gp = (gp.astype(f32) + swap(gp, "sp", 1).astype(f32)).astype(bf16)
-    gp_parts = [swap(gp, "sp", b) for b in (2, 4, 6)]
-    g_pool = jnp.einsum("kf,kc->fc", proj_grad, pooled, precision=highest_precision)
-    from_core = swap(jnp.concatenate([ig[1], ig[3]], axis=1), "ch", 1)
+    from_core = swap(ig_give, "ch", 1)
+
     from_core = from_core.astype(f32)
-    keep = ig[0].astype(f32) + from_core[:, :group]
-    give = (ig[2].astype(f32) + from_core[:, group:]).astype(bf16)
+    keep = ig_keep[0].astype(f32) + from_core[0]
+    give = (ig_keep[1].astype(f32) + from_core[1]).astype(bf16)
     given = swap(give, "ch", 2)
     pos = after(pos, give)
-    if wide_w:
-        g_wide, p_wide = pl.pallas_call(
-            wide_kernel,
-            grid=(4,),
-            in_specs=[SMEM, pl.BlockSpec((BLOCKS, 1, cells, wide_w), lambda i: (0, i, 0, 0))] + [ANY] * BLOCKS,
-            out_specs=[
-                pl.BlockSpec((27 * L, wide_w), lambda i: (0, narrow // wide_w + i)),
-                pl.BlockSpec((L, wide_w), lambda i: (0, narrow // wide_w + i)),
-            ],
-            out_shape=[jax.ShapeDtypeStruct((27 * L, C), f32), jax.ShapeDtypeStruct((L, C), f32)],
-            scratch_shapes=[tap_scratch, pltpu.SemaphoreType.DMA((BLOCKS,))],
-            compiler_params=params(),
-            cost_estimate=cost(1e6, 1e6),
-            name="wide_weight_grads",
-        )(pos, x_wide, *taps)
-    else:
-        g_wide, p_wide = jnp.zeros((27 * L, C), f32), jnp.zeros((L, C), f32)
-    gp, *gp_parts = (t.astype(f32) for t in lax.optimization_barrier((gp, *gp_parts, p_wide))[:4])
-    g_proj = ((gp + gp_parts[0]) + (gp_parts[1] + gp_parts[2])).reshape(5, L, F)
+    g_wide, p_wide, g_proj = pl.pallas_call(
+        wide_kernel,
+        grid=(4,),
+        in_specs=[SMEM, pl.BlockSpec((BLOCKS, 1, cells, wide_w), lambda i: (0, i, 0, 0))]
+        + [ANY] * BLOCKS
+        + [pl.BlockSpec((16, cells), lambda i: (W // 16, 0))] * BLOCKS,
+        out_specs=[
+            pl.BlockSpec((27 * L, wide_w), lambda i: (0, narrow // wide_w + i)),
+            pl.BlockSpec((L, wide_w), lambda i: (0, narrow // wide_w + i)),
+            pl.BlockSpec((5 * L, F), lambda i: (0, 0)),
+        ],
+        out_shape=[
+            jax.ShapeDtypeStruct((27 * L, C), f32),
+            jax.ShapeDtypeStruct((L, C), f32),
+            jax.ShapeDtypeStruct((5 * L, F), f32),
+        ],
+        scratch_shapes=[tap_scratch, pltpu.SemaphoreType.DMA((BLOCKS,))],
+        compiler_params=params(),
+        cost_estimate=cost(1e6, 1e6),
+        name="wide_weight_grads",
+    )(pos, x_wide, *taps, *blocks)
+    g_proj = g_proj.reshape(5, L, F)
     in_grad = (keep + after(given, p_wide).astype(f32)).astype(bf16)
     in_grad = in_grad.reshape(images, rows_dev, cols, group)
 
-    step = 3 * L
+    step = 9 * L
     g_atrous, g_point = pl.pallas_call(
         widen_kernel,
-        grid=(9,),
+        grid=(3,),
         in_specs=[
             pl.BlockSpec((BLOCKS, step, eighth), lambda i: (0, i, 0)),
             pl.BlockSpec((BLOCKS, L, eighth), lambda i: (0, 27, 0)),

time: 378 us -> 341 us (0.902)
  starting transfers between devices: 90.5 us -> 75.6 us
  local copies, waits for them, and re-layouts: 24.8 us -> 12.2 us
  other arithmetic: 35.2 us -> 24.6 us
    ppermute x48 -> x40, starting transfers between devices: 71.4 us -> 53.5 us  [swap(): lax.ppermute(block, axis, [(i, i ^ bits) for i in range(lax.axis_size(axi...]
    unnamed x106 -> x46, local copies, waits for them, and re-layouts: 13.6 us -> 4.48 us
    ppermute x48 -> x40, waiting for transfers between devices: 73 us -> 73.9 us  [swap(): lax.ppermute(block, axis, [(i, i ^ bits) for i in range(lax.axis_size(axi...]
  transfers between devices with their start and end apart: 56 -> 48, of which waited for: 28 -> 18; matrix products, arithmetic and copies ran while one was open for 12% -> 9% of each run, Pallas kernels for 29% -> 37%
where the time goes in v3:
time: 341 us; the launch traced here: 334 us
  Pallas kernels  130 us (38%)
  starting transfers between devices  75.6 us (22%)
  waiting for transfers between devices  73.9 us (22%)
  other arithmetic  24.6 us (7%)
  between operations  15.2 us (4%)
  local copies, waits for them, and re-layouts  12.2 us (4%)
    ppermute x40, waiting for transfers between devices, swap(): lax.ppermute(block, axis, [(i, i ^ bits) for i in range(lax.axis_size(axi...  73.9 us
    ppermute x40, starting transfers between devices, swap(): lax.ppermute(block, axis, [(i, i ^ bits) for i in range(lax.axis_size(axi...  53.5 us
    pallas_call x1, Pallas kernels, body(): pl.pallas_call(wide_kernel, grid=(4,), in_specs=[SMEM, pl.BlockSpec((BLOC...  38.7 us
    ppermute x6, starting transfers between devices, neighbours(): rounds.append(lax.ppermute(block, axis, grouped(pairs, size)))  22 us
    pallas_call x8, Pallas kernels, column_taps(): pl.pallas_call(functools.partial(expand_kernel, cols=cols, rates=rates),...  20.5 us
    pallas_call x1, Pallas kernels, body(): pl.pallas_call(functools.partial(input_grad_kernel, slabs=slabs, cols=col...  18.3 us
    pallas_call x1, Pallas kernels, body(): pl.pallas_call(functools.partial(narrow_kernel, parts=images), in_specs=[...  14.4 us
    pallas_call x1, Pallas kernels, side_taps(): pl.pallas_call(functools.partial(side_kernel, steps=steps, slabs=slabs, c...  11.3 us
  transfers between devices with their start and end apart: 48, of which 18 were waited for; matrix products, arithmetic and copies ran while one was open for 9% of the time, Pallas kernels for 37%

profile of v3, /device:TPU:0, one launch (start us, length us, event | category | flops | bytes accessed | tf_op | source)
XLA Modules:
  0.0 334.3 jit_solution(4313780184008733394)
XLA Ops:
  8.3 2.1 dynamic-slice_select_fusion.1
  12.4 3.0 collective-permute-start
  18.6 2.6 collective-permute-start.5
  22.0 11.3 %side_taps.1 = (bf16[576,128]{1,0:T(8,128)(2,1)}, bf16[576,128]{1,0:T(8,128)(2,1)}, bf16[576,128]{1,0:T(8,128)(2,1)}, bf16[576,128]{1,0:T(8,128)(2,1)}, bf16[576...) custom-call(s32[24]{0:T(128)} %copy-done.5, s32[3]{0:T(128)} %pad_add_fusion.low_ref, bf16[1152,2048]{1,0:T(8,128)(2,1)} %bitcast.64, ...), custom_call_target="tpu_custom_call" | custom-call | flops 5435817984 | bytes 10000000 | tf_op jit(solution)/shard_map/side_taps/pallas_call | solution.py:842
  38.1 8.3 %collective-permute-start.7 = (bf16[576,128]{1,0:T(8,128)(2,1)}, bf16[576,128]{1,0:T(8,128)(2,1)S(1)}, u32[]{:S(2)}, u32[]{:S(2)}) collective-permute-start(bf16[576,128]{1,0:T(8,128)(2,1)} %get-tuple-element.71), channel_id=1, source_target_pairs={{0,8},{4,12},{16,24},{20,28},{8,0},{12,4},{24,16},{28,20},{1,9},{5... | collective-permute-start | bytes 442376 | tf_op jit(solution)/shard_map/ppermute | solution.py:523
  47.0 10.1 %collective-permute-start.9 = (bf16[576,128]{1,0:T(8,128)(2,1)}, bf16[576,128]{1,0:T(8,128)(2,1)S(1)}, u32[]{:S(2)}, u32[]{:S(2)}) collective-permute-start(bf16[576,128]{1,0:T(8,128)(2,1)} %get-tuple-element.73), channel_id=1, source_target_pairs={{0,12},{4,16},{8,20},{12,0},{16,4},{20,8},{1,13},{5,17},{9,21},{13... | collective-permute-start | bytes 442376 | tf_op jit(solution)/shard_map/ppermute | solution.py:523
  57.2 9.1 %centre_taps.1 = (f32[1152,256]{1,0:T(8,128)}, f32[8,2048]{1,0:T(8,128)}) custom-call(s32[24]{0:T(128)} %copy-done.5, bf16[1152,2048]{1,0:T(8,128)(2,1)} %bitcast.65, bf16[3,3,3,64,2048]{4,3,2,1,0:T(8,128)(2,1)} %wc_ref.1, bf16[64,2048]{1,0:T(8,128)(2,1)} %wp_ref.1), custom_call_target="tpu_custom_call" | custom-call | flops 3019898880 | bytes 8000000 | tf_op jit(solution)/shard_map/centre_taps/pallas_call | solution.py:884
  68.9 2.0 combine_taps.1
  71.4 2.8 collective-permute-start.13
  74.2 2.0 collective-permute-done.13
  78.4 2.2 collective-permute-start.16
  81.8 3.6 %collective-permute-done.15 = f32[40,256]{1,0:T(8,128)} collective-permute-done((f32[40,256]{1,0:T(8,128)S(1)}, f32[40,256]{1,0:T(8,128)}, u32[]{:S(2)}, u32[]{:S(2)}) %collective-permute-start.15) | collective-permute-done | bytes 40992 | tf_op jit(solution)/shard_map/ppermute | solution.py:528
  93.6 4.2 %mix_branches.1 = (f32[1152,256]{1,0:T(8,128)S(1)}, bf16[1152,256]{1,0:T(8,128)(2,1)S(1)}, f32[8,256]{1,0:T(8,128)S(1)}, f32[8,256]{1,0:T(8,128)S(1)}) custom-call(s32[24]{0:T(128)S(1)} %copy-done.6, f32[1]{0:T(128)} %bitcast.2.n_ref, f32[1152,256]{1,0:T(8,128)S(1)} %get-tuple-element.76.conv_ref, bf16[1152,256]{1,0:T(8,128)(2,1)S(1)} %collective-permute-done.11.c1_ref, ...), custom_call_target="tpu_custom_call" | custom-call | flops 603979776 | bytes 6000000 | tf_op jit(solution)/shard_map/mix_branches/pallas_call | solution.py:937
  100.7 4.0 %collective-permute-done.22 = f32[8,256]{1,0:T(8,128)S(1)} collective-permute-done((f32[8,256]{1,0:T(8,128)S(1)}, f32[8,256]{1,0:T(8,128)S(1)}, u32[]{:S(2)}, u32[]{:S(2)}) %collective-permute-start.22) | collective-permute-done | bytes 8224 | tf_op jit(solution)/shard_map/ppermute | solution.py:528
  104.7 4.4 %collective-permute-start.23 = (f32[8,256]{1,0:T(8,128)S(1)}, f32[8,256]{1,0:T(8,128)S(1)}, u32[]{:S(2)}, u32[]{:S(2)}) collective-permute-start(f32[8,256]{1,0:T(8,128)S(1)} %add.269.s0), channel_id=1, source_target_pairs={{0,8},{4,12},{8,0},{12,4},{16,24},{20,28},{24,16},{28,20},{1,9},{5... | collective-permute-start | bytes 24584 | tf_op jit(solution)/shard_map/ppermute | solution.py:528
  111.5 2.4 collective-permute-done.24.s2
  115.4 2.2 final_norm.1
  117.6 2.2 collective-permute-start.26
  121.9 3.0 collective-permute-start.28
  126.8 3.6 %collective-permute-done.29.s3 = f32[8,256]{1,0:T(8,128)S(1)} collective-permute-done((f32[8,256]{1,0:T(8,128)S(1)}, f32[8,256]{1,0:T(8,128)S(1)}, u32[]{:S(2)}, u32[]{:S(2)}) %collective-permute-start.29) | collective-permute-done | bytes 8224 | tf_op jit(solution)/shard_map/ppermute | solution.py:528
  130.4 2.4 branch_grads.1
  135.2 2.8 collective-permute-done.30
  139.8 2.8 collective-permute-start.33
  142.7 2.0 collective-permute-done.31
  144.7 2.7 collective-permute-done.32
  150.1 3.1 collective-permute-start.37
  154.6 4.9 %collective-permute-done.34.cg_ref.refs_1_.refs_9_ = bf16[272,1152]{1,0:T(8,128)(2,1)S(1)} collective-permute-done((bf16[272,1152]{1,0:T(8,128)(2,1)S(1)}, bf16[272,1152]{1,0:T(8,128)(2,1)S(1)}, u32[]{:S(2)}, u32[]{:S(2)}) %collective-permute-start.34) | collective-permute-done | bytes 626720 | tf_op jit(solution)/shard_map/ppermute | solution.py:528
  161.7 2.6 column_taps.8.refs_0_
  165.2 19.6 %collective-permute-done.37.cg_ref.refs_4_.refs_12_ = bf16[272,1152]{1,0:T(8,128)(2,1)S(1)} collective-permute-done((bf16[272,1152]{1,0:T(8,128)(2,1)S(1)}, bf16[272,1152]{1,0:T(8,128)(2,1)S(1)}, u32[]{:S(2)}, u32[]{:S(2)}) %collective-permute-start.37) | collective-permute-done | bytes 626720 | tf_op jit(solution)/shard_map/ppermute | solution.py:528
  189.1 2.2 pad_maximum_fusion.1
  191.2 2.5 column_taps.9.refs_1_
  195.6 2.6 column_taps.10.refs_2_
  198.2 5.7 %collective-permute-done.36.cg_ref.refs_3_.refs_11_ = bf16[272,1152]{1,0:T(8,128)(2,1)S(1)} collective-permute-done((bf16[272,1152]{1,0:T(8,128)(2,1)}, bf16[272,1152]{1,0:T(8,128)(2,1)S(1)}, u32[]{:S(2)}, u32[]{:S(2)}) %collective-permute-start.36) | collective-permute-done | bytes 626720 | tf_op jit(solution)/shard_map/ppermute | solution.py:528
  204.7 2.6 column_taps.11.refs_3_
  209.6 2.8 column_taps.12.refs_4_
  212.3 2.5 column_taps.14.refs_6_
  214.8 2.5 collective-permute-done.38.cg_ref.refs_5_.refs_13_
  218.2 2.5 column_taps.13.refs_5_
  220.7 8.0 %collective-permute-done.40.cg_ref.refs_7_.refs_15_ = bf16[272,1152]{1,0:T(8,128)(2,1)S(1)} collective-permute-done((bf16[272,1152]{1,0:T(8,128)(2,1)}, bf16[272,1152]{1,0:T(8,128)(2,1)S(1)}, u32[]{:S(2)}, u32[]{:S(2)}) %collective-permute-start.40) | collective-permute-done | bytes 626720 | tf_op jit(solution)/shard_map/ppermute | solution.py:528
  229.6 2.5 column_taps.15.refs_7_
  233.4 2.8 pad_maximum_fusion.refs_8_
  236.2 14.4 %narrow_weight_grads.1 = bf16[1792,128]{1,0:T(8,128)(2,1)} custom-call(s32[3]{0:T(128)} %pad_add_fusion.1.pos_ref, bf16[640,1152]{1,0:T(8,128)(2,1)} %column_taps.8.refs_0_, bf16[640,1152]{1,0:T(8,128)(2,1)} %column_taps.9.refs_1_, bf16[640,1152]{1,0:T(8,128)(2,1)} %column_taps.10.refs_2_, bf16[640,1152]{1,0:T(8,128)(2,1)} %column_taps.11.refs_3_, ...), custom_call_target="tpu_custom_call" | custom-call | flops 4227858432 | bytes 12000000 | tf_op jit(solution)/shard_map/narrow_weight_grads/pallas_call | solution.py:1079
  251.3 18.3 %input_grads.1 = (bf16[2,1152,512]{2,1,0:T(8,128)(2,1)}, bf16[2,1152,512]{2,1,0:T(8,128)(2,1)}) custom-call(s32[3]{0:T(128)} %pad_add_fusion.1.pos_ref, s32[24]{0:T(128)} %copy-done.5, s32[8,1152]{1,0:T(8,128)} %broadcast_in_dim.93.col_ref, bf16[1728,2048]{1,0:T(8,128)(2,1)} %bitcast.61, bf16[64,2048]{1,0:T(8,128)(2,1)} %wp_ref.1, f32[8,2048]{1,0:T(8,128)} %pad.19.pool_ref, ...), custom_call_target="tpu_custom_call" | custom-call | flops 1000000 | bytes 1000000 | tf_op jit(solution)/shard_map/input_grads/pallas_call | solution.py:1098
  269.6 4.7 %collective-permute-done.44 = bf16[2,1152,512]{2,1,0:T(8,128)(2,1)S(1)} collective-permute-done((bf16[2,1152,512]{2,1,0:T(8,128)(2,1)}, bf16[2,1152,512]{2,1,0:T(8,128)(2,1)S(1)}, u32[]{:S(2)}, u32[]{:S(2)}) %collective-permute-start.44) | collective-permute-done | bytes 2359328 | tf_op jit(solution)/shard_map/ppermute | solution.py:528
  275.0 1.9 fusion.4
  279.2 38.7 %wide_weight_grads.1 = (f32[1728,2048]{1,0:T(8,128)}, f32[64,2048]{1,0:T(8,128)}, f32[320,256]{1,0:T(8,128)}) custom-call(s32[3]{0:T(128)} %pad_add_fusion.1.pos_ref, bf16[8,4,1152,256]{3,2,1,0:T(8,128)(2,1)} %bitcast.66, bf16[640,1152]{1,0:T(8,128)(2,1)} %column_taps.8.refs_0_, bf16[640,1152]{1,0:T(8,128)(2,1)} %column_taps.9.refs_1_, ...), custom_call_target="tpu_custom_call" | custom-call | flops 1000000 | bytes 1000000 | tf_op jit(solution)/shard_map/wide_weight_grads/pallas_call | solution.py:1131
  317.9 3.5 %fusion.3 = bf16[1152,512]{1,0:T(8,128)(2,1)} fusion(f32[2,1152,512]{2,1,0:T(8,128)} %copy-done.7, bf16[1152,512]{1,0:T(8,128)(2,1)} %collective-permute-done.45, bf16[2,1152,512]{2,1,0:T(8,128)(2,1)S(1)} %copy-done.13), kind=kLoop, calls=%fused_computation.5 | loop fusion | flops 2949120 | bytes 5898240 | tf_op jit(solution)/shard_map/convert_element_type | solution.py:1153
  321.4 5.7 %widen.1 = (f32[1728,2048]{1,0:T(8,128)}, f32[64,2048]{1,0:T(8,128)}) custom-call(bf16[8,1792,128]{2,1,0:T(8,128)(2,1)} %bitcast.67, bf16[8,1792,128]{2,1,0:T(8,128)(2,1)} %bitcast.68, f32[1728,2048]{1,0:T(8,128)} %get-tuple-element.108.keep_ref, f32[64,2048]{1,0:T(8,128)} %get-tuple-element.106.pkeep_ref), custom_call_target="tpu_custom_call", output_to_operand_aliasing={{0}: (2, {}), {1}: (3, {})} | custom-call | flops 1000000 | bytes 20000000 | tf_op jit(solution)/shard_map/widen/pallas_call | solution.py:1157
  (195 shorter events, 64.7 us)
Async XLA Ops:
  7.2 272.0 %all-gather.5.cloned.1.call-start = ((), (), s32[]{:S(2)}) async-start(), calls=%async_computation | async-start | bytes 19464192 | tf_op jit(solution)/shard_map/all_gather | solution.py:882
  10.4 310.9 %all-gather.7.cloned.1.call-start = ((), (), s32[]{:S(2)}) async-start(), calls=%async_computation.1 | async-start | bytes 4128768 | tf_op jit(solution)/shard_map/all_gather | solution.py:1095
  12.4 21.0 %collective-permute-start = (bf16[336,256]{1,0:T(8,128)(2,1)S(1)}, bf16[336,256]{1,0:T(8,128)(2,1)S(1)}, u32[]{:S(2)}, u32[]{:S(2)}) collective-permute-start(bf16[336,256]{1,0:T(8,128)(2,1)S(1)} %concatenate.48.p0), channel_id=1, source_target_pairs={{0,2},{1,3},{2,0},{3,1},{4,6},{5,7},{6,4},{7,5},{8,10},{9,11},{10,... | collective-permute-start | bytes 516104 | tf_op jit(solution)/shard_map/ppermute | solution.py:528
  15.4 17.9 %collective-permute-start.1 = (bf16[336,256]{1,0:T(8,128)(2,1)S(1)}, bf16[336,256]{1,0:T(8,128)(2,1)S(1)}, u32[]{:S(2)}, u32[]{:S(2)}) collective-permute-start(bf16[336,256]{1,0:T(8,128)(2,1)S(1)} %concatenate.48.p0), channel_id=1, source_target_pairs={{0,1},{1,0},{2,3},{3,2},{4,5},{5,4},{6,7},{7,6},{8,9},{9,8},{10,11... | collective-permute-start | bytes 516104 | tf_op jit(solution)/shard_map/ppermute | solution.py:528
  17.0 18.7 %collective-permute-start.4 = (bf16[288,256]{1,0:T(8,128)(2,1)S(1)}, bf16[288,256]{1,0:T(8,128)(2,1)S(1)}, u32[]{:S(2)}, u32[]{:S(2)}) collective-permute-start(bf16[288,256]{1,0:T(8,128)(2,1)S(1)} %get-tuple-element.129), channel_id=1, source_target_pairs={{0,8},{4,12},{8,0},{12,4},{16,24},{20,28},{24,16},{28,20},{1,9},{5... | collective-permute-start | bytes 442376 | tf_op jit(solution)/shard_map/ppermute | solution.py:528
  18.6 17.0 %collective-permute-start.5 = (bf16[288,256]{1,0:T(8,128)(2,1)S(1)}, bf16[288,256]{1,0:T(8,128)(2,1)S(1)}, u32[]{:S(2)}, u32[]{:S(2)}) collective-permute-start(bf16[288,256]{1,0:T(8,128)(2,1)S(1)} %get-tuple-element.128), channel_id=1, source_target_pairs={{0,16},{4,20},{8,24},{12,28},{16,0},{20,4},{24,8},{28,12},{1,17},{... | collective-permute-start | bytes 442376 | tf_op jit(solution)/shard_map/ppermute | solution.py:528
  21.2 15.2 %collective-permute-start.6 = (bf16[288,256]{1,0:T(8,128)(2,1)S(1)}, bf16[288,256]{1,0:T(8,128)(2,1)S(1)}, u32[]{:S(2)}, u32[]{:S(2)}) collective-permute-start(bf16[288,256]{1,0:T(8,128)(2,1)S(1)} %get-tuple-element.127), channel_id=1, source_target_pairs={{0,24},{4,28},{8,16},{12,20},{16,8},{20,12},{24,0},{28,4},{1,25},{... | collective-permute-start | bytes 442376 | tf_op jit(solution)/shard_map/ppermute | solution.py:528
  33.4 13.7 %collective-permute-start.2 = (bf16[576,128]{1,0:T(8,128)(2,1)}, bf16[576,128]{1,0:T(8,128)(2,1)S(1)}, u32[]{:S(2)}, u32[]{:S(2)}) collective-permute-start(bf16[576,128]{1,0:T(8,128)(2,1)} %get-tuple-element.67), channel_id=1, source_target_pairs={{0,4},{8,12},{16,20},{24,28},{4,0},{12,8},{20,16},{28,24},{1,5},{9... | collective-permute-start | bytes 442376 | tf_op jit(solution)/shard_map/ppermute | solution.py:523
  34.9 22.2 %collective-permute-start.3 = (bf16[576,128]{1,0:T(8,128)(2,1)}, bf16[576,128]{1,0:T(8,128)(2,1)S(1)}, u32[]{:S(2)}, u32[]{:S(2)}) collective-permute-start(bf16[576,128]{1,0:T(8,128)(2,1)} %get-tuple-element.68), channel_id=1, source_target_pairs={{4,8},{12,16},{20,24},{8,4},{16,12},{24,20},{5,9},{13,17},{21,25},... | collective-permute-start | bytes 442376 | tf_op jit(solution)/shard_map/ppermute | solution.py:523
  37.3 30.3 %collective-permute-start.10 = (bf16[576,128]{1,0:T(8,128)(2,1)}, bf16[576,128]{1,0:T(8,128)(2,1)S(1)}, u32[]{:S(2)}, u32[]{:S(2)}) collective-permute-start(bf16[576,128]{1,0:T(8,128)(2,1)} %get-tuple-element.74), channel_id=1, source_target_pairs={{12,24},{16,28},{24,12},{28,16},{13,25},{17,29},{25,13},{29,17},{1... | collective-permute-start | bytes 442376 | tf_op jit(solution)/shard_map/ppermute | solution.py:523
  38.1 29.5 %collective-permute-start.7 = (bf16[576,128]{1,0:T(8,128)(2,1)}, bf16[576,128]{1,0:T(8,128)(2,1)S(1)}, u32[]{:S(2)}, u32[]{:S(2)}) collective-permute-start(bf16[576,128]{1,0:T(8,128)(2,1)} %get-tuple-element.71), channel_id=1, source_target_pairs={{0,8},{4,12},{16,24},{20,28},{8,0},{12,4},{24,16},{28,20},{1,9},{5... | collective-permute-start | bytes 442376 | tf_op jit(solution)/shard_map/ppermute | solution.py:523
  46.4 21.2 %collective-permute-start.8 = (bf16[576,128]{1,0:T(8,128)(2,1)}, bf16[576,128]{1,0:T(8,128)(2,1)S(1)}, u32[]{:S(2)}, u32[]{:S(2)}) collective-permute-start(bf16[576,128]{1,0:T(8,128)(2,1)} %get-tuple-element.72), channel_id=1, source_target_pairs={{8,16},{12,20},{16,8},{20,12},{9,17},{13,21},{17,9},{21,13},{10,18... | collective-permute-start | bytes 442376 | tf_op jit(solution)/shard_map/ppermute | solution.py:523
  47.0 20.6 %collective-permute-start.9 = (bf16[576,128]{1,0:T(8,128)(2,1)}, bf16[576,128]{1,0:T(8,128)(2,1)S(1)}, u32[]{:S(2)}, u32[]{:S(2)}) collective-permute-start(bf16[576,128]{1,0:T(8,128)(2,1)} %get-tuple-element.73), channel_id=1, source_target_pairs={{0,12},{4,16},{8,20},{12,0},{16,4},{20,8},{1,13},{5,17},{9,21},{13... | collective-permute-start | bytes 442376 | tf_op jit(solution)/shard_map/ppermute | solution.py:523
  70.9 14.6 %collective-permute-start.12 = (bf16[1152,256]{1,0:T(8,128)(2,1)}, bf16[1152,256]{1,0:T(8,128)(2,1)S(1)}, u32[]{:S(2)}, u32[]{:S(2)}) collective-permute-start(bf16[1152,256]{1,0:T(8,128)(2,1)} %get-tuple-element.77), channel_id=1, source_target_pairs={{0,2},{1,3},{2,0},{3,1},{4,6},{5,7},{6,4},{7,5},{8,10},{9,11},{10,... | collective-permute-start | bytes 1769480 | tf_op jit(solution)/shard_map/ppermute | solution.py:528
  71.4 4.8 %collective-permute-start.13 = (f32[40,256]{1,0:T(8,128)S(1)}, f32[40,256]{1,0:T(8,128)S(1)}, u32[]{:S(2)}, u32[]{:S(2)}) collective-permute-start(f32[40,256]{1,0:T(8,128)S(1)} %get-tuple-element.78), channel_id=1, source_target_pairs={{0,4},{4,0},{8,12},{12,8},{16,20},{20,16},{24,28},{28,24},{1,5},{5... | collective-permute-start | bytes 122888 | tf_op jit(solution)/shard_map/ppermute | solution.py:528
  76.2 5.6 %collective-permute-start.14 = (f32[40,256]{1,0:T(8,128)S(1)}, f32[40,256]{1,0:T(8,128)S(1)}, u32[]{:S(2)}, u32[]{:S(2)}) collective-permute-start(f32[40,256]{1,0:T(8,128)S(1)} %add.264), channel_id=1, source_target_pairs={{0,8},{4,12},{8,0},{12,4},{16,24},{20,28},{24,16},{28,20},{1,9},{5... | collective-permute-start | bytes 122888 | tf_op jit(solution)/shard_map/ppermute | solution.py:528
  77.6 7.8 %collective-permute-start.15 = (f32[40,256]{1,0:T(8,128)S(1)}, f32[40,256]{1,0:T(8,128)}, u32[]{:S(2)}, u32[]{:S(2)}) collective-permute-start(f32[40,256]{1,0:T(8,128)S(1)} %add.264), channel_id=1, source_target_pairs={{0,16},{4,20},{8,24},{12,28},{16,0},{20,4},{24,8},{28,12},{1,17},{... | collective-permute-start | bytes 122888 | tf_op jit(solution)/shard_map/ppermute | solution.py:528
  78.4 7.0 %collective-permute-start.16 = (f32[40,256]{1,0:T(8,128)S(1)}, f32[40,256]{1,0:T(8,128)S(1)}, u32[]{:S(2)}, u32[]{:S(2)}) collective-permute-start(f32[40,256]{1,0:T(8,128)S(1)} %add.264), channel_id=1, source_target_pairs={{0,24},{4,28},{8,16},{12,20},{16,8},{20,12},{24,0},{28,4},{1,25},{... | collective-permute-start | bytes 122888 | tf_op jit(solution)/shard_map/ppermute | solution.py:528
  81.8 11.8 %collective-permute-start.11 = (bf16[1152,256]{1,0:T(8,128)(2,1)}, bf16[1152,256]{1,0:T(8,128)(2,1)S(1)}, u32[]{:S(2)}, u32[]{:S(2)}) collective-permute-start(bf16[1152,256]{1,0:T(8,128)(2,1)} %get-tuple-element.77), channel_id=1, source_target_pairs={{0,1},{1,0},{2,3},{3,2},{4,5},{5,4},{6,7},{7,6},{8,9},{9,8},{10,11... | collective-permute-start | bytes 1769480 | tf_op jit(solution)/shard_map/ppermute | solution.py:528
  85.5 8.1 %collective-permute-start.17 = (bf16[1152,256]{1,0:T(8,128)(2,1)S(1)}, bf16[1152,256]{1,0:T(8,128)(2,1)}, u32[]{:S(2)}, u32[]{:S(2)}) collective-permute-start(bf16[1152,256]{1,0:T(8,128)(2,1)S(1)} %collective-permute-done.12.c2_ref), channel_id=1, source_target_pairs={{0,1},{1,0},{2,3},{3,2},{4,5},{5,4},{6,7},{7,6},{8,9},{9,8},{10,11... | collective-permute-start | bytes 1769480 | tf_op jit(solution)/shard_map/ppermute | solution.py:528
  86.2 4.2 %collective-permute-start.21 = (bf16[336,256]{1,0:T(8,128)(2,1)S(1)}, bf16[336,256]{1,0:T(8,128)(2,1)S(1)}, u32[]{:S(2)}, u32[]{:S(2)}) collective-permute-start(bf16[336,256]{1,0:T(8,128)(2,1)S(1)} %collective-permute-done.p2), channel_id=1, source_target_pairs={{0,1},{1,0},{2,3},{3,2},{4,5},{5,4},{6,7},{7,6},{8,9},{9,8},{10,11... | collective-permute-start | bytes 516104 | tf_op jit(solution)/shard_map/ppermute | solution.py:528
  87.5 3.2 collective-permute-start.18
  87.6 4.6 %collective-permute-start.19 = (f32[8,256]{1,0:T(8,128)S(1)}, f32[8,256]{1,0:T(8,128)S(1)}, u32[]{:S(2)}, u32[]{:S(2)}) collective-permute-start(f32[8,256]{1,0:T(8,128)S(1)} %fusion.19.t0), channel_id=1, source_target_pairs={{0,2},{1,3},{2,0},{3,1},{4,6},{5,7},{6,4},{7,5},{8,10},{9,11},{10,... | collective-permute-start | bytes 24584 | tf_op jit(solution)/shard_map/ppermute | solution.py:528
  90.5 3.1 collective-permute-start.20
  90.7 29.1 %collective-permute-start.41 = (bf16[4,288,128]{2,1,0:T(8,128)(2,1)S(1)}, bf16[4,288,128]{2,1,0:T(8,128)(2,1)S(1)}, u32[]{:S(2)}, u32[]{:S(2)}) collective-permute-start(bf16[4,288,128]{2,1,0:T(8,128)(2,1)S(1)} %get-tuple-element.126), channel_id=1, source_target_pairs={{0,4},{4,0},{8,12},{12,8},{16,20},{20,16},{24,28},{28,24},{1,5},{5... | collective-permute-start | bytes 884744 | tf_op jit(solution)/shard_map/ppermute | solution.py:528
  97.8 6.9 %collective-permute-start.22 = (f32[8,256]{1,0:T(8,128)S(1)}, f32[8,256]{1,0:T(8,128)S(1)}, u32[]{:S(2)}, u32[]{:S(2)}) collective-permute-start(f32[8,256]{1,0:T(8,128)S(1)} %get-tuple-element.82), channel_id=1, source_target_pairs={{0,4},{4,0},{8,12},{12,8},{16,20},{20,16},{24,28},{28,24},{1,5},{5... | collective-permute-start | bytes 24584 | tf_op jit(solution)/shard_map/ppermute | solution.py:528
  104.7 6.8 %collective-permute-start.23 = (f32[8,256]{1,0:T(8,128)S(1)}, f32[8,256]{1,0:T(8,128)S(1)}, u32[]{:S(2)}, u32[]{:S(2)}) collective-permute-start(f32[8,256]{1,0:T(8,128)S(1)} %add.269.s0), channel_id=1, source_target_pairs={{0,8},{4,12},{8,0},{12,4},{16,24},{20,28},{24,16},{28,20},{1,9},{5... | collective-permute-start | bytes 24584 | tf_op jit(solution)/shard_map/ppermute | solution.py:528
  109.1 4.8 %collective-permute-start.24 = (f32[8,256]{1,0:T(8,128)S(1)}, f32[8,256]{1,0:T(8,128)S(1)}, u32[]{:S(2)}, u32[]{:S(2)}) collective-permute-start(f32[8,256]{1,0:T(8,128)S(1)} %add.269.s0), channel_id=1, source_target_pairs={{0,16},{4,20},{8,24},{12,28},{16,0},{20,4},{24,8},{28,12},{1,17},{... | collective-permute-start | bytes 24584 | tf_op jit(solution)/shard_map/ppermute | solution.py:528
  109.8 5.6 %collective-permute-start.25 = (f32[8,256]{1,0:T(8,128)S(1)}, f32[8,256]{1,0:T(8,128)S(1)}, u32[]{:S(2)}, u32[]{:S(2)}) collective-permute-start(f32[8,256]{1,0:T(8,128)S(1)} %add.269.s0), channel_id=1, source_target_pairs={{0,24},{4,28},{8,16},{12,20},{16,8},{20,12},{24,0},{28,4},{1,25},{... | collective-permute-start | bytes 24584 | tf_op jit(solution)/shard_map/ppermute | solution.py:528
  117.6 3.9 %collective-permute-start.26 = (f32[8,256]{1,0:T(8,128)S(1)}, f32[8,256]{1,0:T(8,128)S(1)}, u32[]{:S(2)}, u32[]{:S(2)}) collective-permute-start(f32[8,256]{1,0:T(8,128)S(1)} %get-tuple-element.88), channel_id=1, source_target_pairs={{0,4},{4,0},{8,12},{12,8},{16,20},{20,16},{24,28},{28,24},{1,5},{5... | collective-permute-start | bytes 24584 | tf_op jit(solution)/shard_map/ppermute | solution.py:528
  121.6 5.3 %collective-permute-start.27 = (f32[8,256]{1,0:T(8,128)S(1)}, f32[8,256]{1,0:T(8,128)S(1)}, u32[]{:S(2)}, u32[]{:S(2)}) collective-permute-start(f32[8,256]{1,0:T(8,128)S(1)} %add.273.s0), channel_id=1, source_target_pairs={{0,8},{4,12},{8,0},{12,4},{16,24},{20,28},{24,16},{28,20},{1,9},{5... | collective-permute-start | bytes 24584 | tf_op jit(solution)/shard_map/ppermute | solution.py:528
  121.9 4.9 %collective-permute-start.28 = (f32[8,256]{1,0:T(8,128)S(1)}, f32[8,256]{1,0:T(8,128)S(1)}, u32[]{:S(2)}, u32[]{:S(2)}) collective-permute-start(f32[8,256]{1,0:T(8,128)S(1)} %add.273.s0), channel_id=1, source_target_pairs={{0,16},{4,20},{8,24},{12,28},{16,0},{20,4},{24,8},{28,12},{1,17},{... | collective-permute-start | bytes 24584 | tf_op jit(solution)/shard_map/ppermute | solution.py:528
  124.9 5.6 %collective-permute-start.29 = (f32[8,256]{1,0:T(8,128)S(1)}, f32[8,256]{1,0:T(8,128)S(1)}, u32[]{:S(2)}, u32[]{:S(2)}) collective-permute-start(f32[8,256]{1,0:T(8,128)S(1)} %add.273.s0), channel_id=1, source_target_pairs={{0,24},{4,28},{8,16},{12,20},{16,8},{20,12},{24,0},{28,4},{1,25},{... | collective-permute-start | bytes 24584 | tf_op jit(solution)/shard_map/ppermute | solution.py:528
  133.4 4.6 %collective-permute-start.30 = (bf16[184,256]{1,0:T(8,128)(2,1)S(1)}, bf16[184,256]{1,0:T(8,128)(2,1)S(1)}, u32[]{:S(2)}, u32[]{:S(2)}) collective-permute-start(bf16[184,256]{1,0:T(8,128)(2,1)S(1)} %pad_maximum_fusion.4), channel_id=1, source_target_pairs={{0,4},{4,0},{8,12},{12,8},{16,20},{20,16},{24,28},{28,24},{1,5},{5... | collective-permute-start | bytes 282632 | tf_op jit(solution)/shard_map/ppermute | solution.py:528
  138.2 6.5 %collective-permute-start.31 = (bf16[64,256]{1,0:T(8,128)(2,1)S(1)}, bf16[64,256]{1,0:T(8,128)(2,1)S(1)}, u32[]{:S(2)}, u32[]{:S(2)}) collective-permute-start(bf16[64,256]{1,0:T(8,128)(2,1)S(1)} %get-tuple-element.134), channel_id=1, source_target_pairs={{0,8},{4,12},{8,0},{12,4},{16,24},{20,28},{24,16},{28,20},{1,9},{5... | collective-permute-start | bytes 98312 | tf_op jit(solution)/shard_map/ppermute | solution.py:528
  139.0 8.4 %collective-permute-start.32 = (bf16[64,256]{1,0:T(8,128)(2,1)S(1)}, bf16[64,256]{1,0:T(8,128)(2,1)S(1)}, u32[]{:S(2)}, u32[]{:S(2)}) collective-permute-start(bf16[64,256]{1,0:T(8,128)(2,1)S(1)} %get-tuple-element.135), channel_id=1, source_target_pairs={{0,16},{4,20},{8,24},{12,28},{16,0},{20,4},{24,8},{28,12},{1,17},{... | collective-permute-start | bytes 98312 | tf_op jit(solution)/shard_map/ppermute | solution.py:528
  139.8 7.6 %collective-permute-start.33 = (bf16[64,256]{1,0:T(8,128)(2,1)S(1)}, bf16[64,256]{1,0:T(8,128)(2,1)S(1)}, u32[]{:S(2)}, u32[]{:S(2)}) collective-permute-start(bf16[64,256]{1,0:T(8,128)(2,1)S(1)} %get-tuple-element.136), channel_id=1, source_target_pairs={{0,24},{4,28},{8,16},{12,20},{16,8},{20,12},{24,0},{28,4},{1,25},{... | collective-permute-start | bytes 98312 | tf_op jit(solution)/shard_map/ppermute | solution.py:528
  149.2 10.3 %collective-permute-start.34 = (bf16[272,1152]{1,0:T(8,128)(2,1)S(1)}, bf16[272,1152]{1,0:T(8,128)(2,1)S(1)}, u32[]{:S(2)}, u32[]{:S(2)}) collective-permute-start(bf16[272,1152]{1,0:T(8,128)(2,1)S(1)} %conv_grads.1.cg_ref.refs_0_.refs_8_), channel_id=1, source_target_pairs={{0,4},{4,0},{8,12},{12,8},{16,20},{20,16},{24,28},{28,24},{1,5},{5... | collective-permute-start | bytes 1880072 | tf_op jit(solution)/shard_map/ppermute | solution.py:528
  150.1 34.7 %collective-permute-start.37 = (bf16[272,1152]{1,0:T(8,128)(2,1)S(1)}, bf16[272,1152]{1,0:T(8,128)(2,1)S(1)}, u32[]{:S(2)}, u32[]{:S(2)}) collective-permute-start(bf16[272,1152]{1,0:T(8,128)(2,1)S(1)} %conv_grads.1.cg_ref.refs_0_.refs_8_), channel_id=1, source_target_pairs={{0,16},{4,20},{8,24},{12,28},{16,0},{20,4},{24,8},{28,12},{1,17},{... | collective-permute-start | bytes 1880072 | tf_op jit(solution)/shard_map/ppermute | solution.py:528
  153.2 33.4 %collective-permute-start.35 = (bf16[272,1152]{1,0:T(8,128)(2,1)S(1)}, bf16[272,1152]{1,0:T(8,128)(2,1)}, u32[]{:S(2)}, u32[]{:S(2)}) collective-permute-start(bf16[272,1152]{1,0:T(8,128)(2,1)S(1)} %conv_grads.1.cg_ref.refs_0_.refs_8_), channel_id=1, source_target_pairs={{0,8},{4,12},{8,0},{12,4},{16,24},{20,28},{24,16},{28,20},{1,9},{5... | collective-permute-start | bytes 1880072 | tf_op jit(solution)/shard_map/ppermute | solution.py:528
  159.5 29.5 %collective-permute-start.42 = (bf16[1,8,288,128]{3,2,1,0:T(8,128)(2,1)S(1)}, bf16[1,8,288,128]{3,2,1,0:T(8,128)(2,1)}, u32[]{:S(2)}, u32[]{:S(2)}) collective-permute-start(bf16[1,8,288,128]{3,2,1,0:T(8,128)(2,1)S(1)} %bitcast.70), channel_id=1, source_target_pairs={{0,2},{1,3},{2,0},{3,1},{4,6},{5,7},{6,4},{7,5},{8,10},{9,11},{10,... | collective-permute-start | bytes 1769480 | tf_op jit(solution)/shard_map/ppermute | solution.py:528
  184.8 22.5 %collective-permute-start.39 = (bf16[272,1152]{1,0:T(8,128)(2,1)}, bf16[272,1152]{1,0:T(8,128)(2,1)}, u32[]{:S(2)}, u32[]{:S(2)}) collective-permute-start(bf16[272,1152]{1,0:T(8,128)(2,1)} %copy-done.2), channel_id=1, source_target_pairs={{0,24},{4,28},{8,16},{12,20},{16,8},{20,12},{24,0},{28,4},{1,25},{... | collective-permute-start | bytes 1880072 | tf_op jit(solution)/shard_map/ppermute | solution.py:528
  186.6 17.3 %collective-permute-start.36 = (bf16[272,1152]{1,0:T(8,128)(2,1)}, bf16[272,1152]{1,0:T(8,128)(2,1)S(1)}, u32[]{:S(2)}, u32[]{:S(2)}) collective-permute-start(bf16[272,1152]{1,0:T(8,128)(2,1)} %collective-permute-done.35.cg_ref.refs_2_.refs_10_), channel_id=1, source_target_pairs={{0,4},{4,0},{8,12},{12,8},{16,20},{20,16},{24,28},{28,24},{1,5},{5... | collective-permute-start | bytes 1880072 | tf_op jit(solution)/shard_map/ppermute | solution.py:528
  191.2 40.8 %collective-permute-start.43 = (bf16[2,8,288,128]{3,2,1,0:T(8,128)(2,1)}, bf16[2,8,288,128]{3,2,1,0:T(8,128)(2,1)}, u32[]{:S(2)}, u32[]{:S(2)}) collective-permute-start(bf16[2,8,288,128]{3,2,1,0:T(8,128)(2,1)} %pad_maximum_fusion.1), channel_id=1, source_target_pairs={{0,1},{1,0},{2,3},{3,2},{4,5},{5,4},{6,7},{7,6},{8,9},{9,8},{10,11... | collective-permute-start | bytes 3538952 | tf_op jit(solution)/shard_map/ppermute | solution.py:528
  195.2 22.1 %collective-permute-start.38 = (bf16[272,1152]{1,0:T(8,128)(2,1)S(1)}, bf16[272,1152]{1,0:T(8,128)(2,1)S(1)}, u32[]{:S(2)}, u32[]{:S(2)}) collective-permute-start(bf16[272,1152]{1,0:T(8,128)(2,1)S(1)} %collective-permute-done.37.cg_ref.refs_4_.refs_12_), channel_id=1, source_target_pairs={{0,4},{4,0},{8,12},{12,8},{16,20},{20,16},{24,28},{28,24},{1,5},{5... | collective-permute-start | bytes 1880072 | tf_op jit(solution)/shard_map/ppermute | solution.py:528
  207.3 21.5 %collective-permute-start.40 = (bf16[272,1152]{1,0:T(8,128)(2,1)}, bf16[272,1152]{1,0:T(8,128)(2,1)S(1)}, u32[]{:S(2)}, u32[]{:S(2)}) collective-permute-start(bf16[272,1152]{1,0:T(8,128)(2,1)} %collective-permute-done.39.cg_ref.refs_6_.refs_14_), channel_id=1, source_target_pairs={{0,4},{4,0},{8,12},{12,8},{16,20},{20,16},{24,28},{28,24},{1,5},{5... | collective-permute-start | bytes 1880072 | tf_op jit(solution)/shard_map/ppermute | solution.py:528
  269.5 4.8 %collective-permute-start.44 = (bf16[2,1152,512]{2,1,0:T(8,128)(2,1)}, bf16[2,1152,512]{2,1,0:T(8,128)(2,1)S(1)}, u32[]{:S(2)}, u32[]{:S(2)}) collective-permute-start(bf16[2,1152,512]{2,1,0:T(8,128)(2,1)} %get-tuple-element.104), channel_id=1, source_target_pairs={{0,1},{1,0},{2,3},{3,2},{4,5},{5,4},{6,7},{7,6},{8,9},{9,8},{10,11... | collective-permute-start | bytes 7077896 | tf_op jit(solution)/shard_map/ppermute | solution.py:528
  277.6 40.3 %collective-permute-start.45 = (bf16[1152,512]{1,0:T(8,128)(2,1)}, bf16[1152,512]{1,0:T(8,128)(2,1)}, u32[]{:S(2)}, u32[]{:S(2)}) collective-permute-start(bf16[1152,512]{1,0:T(8,128)(2,1)} %fusion.4), channel_id=1, source_target_pairs={{0,2},{1,3},{2,0},{3,1},{4,6},{5,7},{6,4},{7,5},{8,10},{9,11},{10,... | collective-permute-start | bytes 3538952 | tf_op jit(solution)/shard_map/ppermute | solution.py:528
  (23 other events, 360.1 us)
Sparse Core Ops, SparseCore 0:
  10.9 167.7 all-gather.4
  250.7 66.4 all-gather.6

commit v4 on v3

--- a/solution.py
+++ b/solution.py
@@ -400,16 +400,17 @@
 
 
 def narrow_kernel(pos_ref, *refs, parts):
-    blocks, (x_ref, out_ref, taps, x, sems, xsems) = refs[:BLOCKS], refs[BLOCKS:]
+    blocks, (xown_ref, xcore_ref, out_ref, taps, x, sems, xsems) = refs[:BLOCKS], refs[BLOCKS:]
     pos, ch = pos_ref[0], pos_ref[2]
     L = taps.shape[0] // 10
     cells = taps.shape[1] // BLOCKS
-    rows = x_ref.shape[2]
+    rows = xown_ref.shape[2]
     copies = fetch_blocks(pos, blocks, taps, sems, lanes=True)
     for e in range(parts):
         for d in range(BLOCKS):
             place = pl.ds(pl.multiple_of((pos ^ d) * cells + (ch ^ e) * rows, 16), rows)
-            c = pltpu.make_async_copy(x_ref.at[e, d], x.at[place], xsems.at[e, d])
+            source = (xown_ref, xcore_ref)[e % 2].at[e // 2, d]
+            c = pltpu.make_async_copy(source, x.at[place], xsems.at[e, d])
             c.start()
             copies.append(c)
     for c in copies:
@@ -1058,7 +1059,7 @@
         )(col_row, block)
 
     near = [swap(cgt, "sp", b) for b in (2, 4)]
-    near.append(swap(after(cgt, near[1]), "sp", 6))
+    near.append(swap(after(cgt, near[0]), "sp", 6))
     pair = swap(cgt, "sp", 1)
     taps = [column_taps(cgt), column_taps(pair), column_taps(near[0])]
     near_pair = swap(near[0], "sp", 1)
@@ -1068,7 +1069,6 @@
     x_slices = after(jnp.stack([keep, taken], axis=1).reshape(1, BLOCKS, part, cut), pair)
     x_slices = jnp.concatenate([x_slices, swap(x_slices, "ch", 2)], axis=0)
     x_core = swap(x_slices, "ch", 1)
-    x_slices = jnp.stack([x_slices[0], x_core[0], x_slices[1], x_core[1]])
     g_pool = jnp.einsum("kf,kc->fc", proj_grad, pooled, precision=highest_precision)
     far = [after(near[1], *taps[:2], output, g_pool, g_gains, g_shifts, pooled_grad), after(near[2], *taps)]
     far_pairs = [swap(t, "sp", 1) for t in far]
@@ -1078,7 +1078,7 @@
     tap_scratch = pltpu.VMEM((10 * L, BLOCKS * cells), bf16)
     gw = pl.pallas_call(
         functools.partial(narrow_kernel, parts=images),
-        in_specs=[SMEM] + [ANY] * (BLOCKS + 1),
+        in_specs=[SMEM] + [ANY] * (BLOCKS + 2),
         out_specs=pl.BlockSpec((28 * L, eighth), lambda i: (0, 0)),
         grid=(1,),
         out_shape=jax.ShapeDtypeStruct((28 * L, eighth), bf16),
@@ -1091,7 +1091,7 @@
         compiler_params=params(),
         cost_estimate=cost(2 * cells * BLOCKS * 28 * L * eighth, 12e6),
         name="narrow_weight_grads",
-    )(pos, *taps, x_slices)
+    )(pos, *taps, x_slices, x_core)
     gw_all = lax.all_gather(gw, "sp", axis=0)
     pos, gw = lax.optimization_barrier((pos, gw))
     group = C // 4

time: 341 us -> 336 us (0.985)
  other arithmetic: 24.6 us -> 16.8 us
  transfers between devices with their start and end apart: 48 -> 48, of which waited for: 18 -> 18; matrix products, arithmetic and copies ran while one was open for 9% -> 8% of each run, Pallas kernels for 37% -> 38%
where the time goes in v4:
time: 336 us; the launch traced here: 330 us
  Pallas kernels  131 us (39%)
  starting transfers between devices  77.5 us (23%)
  waiting for transfers between devices  74 us (22%)
  other arithmetic  16.8 us (5%)
  between operations  15.2 us (5%)
  local copies, waits for them, and re-layouts  13.2 us (4%)
    ppermute x40, waiting for transfers between devices, swap(): lax.ppermute(block, axis, [(i, i ^ bits) for i in range(lax.axis_size(axi...  73.9 us
    ppermute x40, starting transfers between devices, swap(): lax.ppermute(block, axis, [(i, i ^ bits) for i in range(lax.axis_size(axi...  54.7 us
    pallas_call x1, Pallas kernels, body(): pl.pallas_call(wide_kernel, grid=(4,), in_specs=[SMEM, pl.BlockSpec((BLOC...  38.8 us
    ppermute x6, starting transfers between devices, neighbours(): rounds.append(lax.ppermute(block, axis, grouped(pairs, size)))  22.7 us
    pallas_call x8, Pallas kernels, column_taps(): pl.pallas_call(functools.partial(expand_kernel, cols=cols, rates=rates),...  20.6 us
    pallas_call x1, Pallas kernels, body(): pl.pallas_call(functools.partial(input_grad_kernel, slabs=slabs, cols=col...  18.3 us
    pallas_call x1, Pallas kernels, body(): pl.pallas_call(functools.partial(narrow_kernel, parts=images), in_specs=[...  14.5 us
    pallas_call x1, Pallas kernels, side_taps(): pl.pallas_call(functools.partial(side_kernel, steps=steps, slabs=slabs, c...  11.4 us
  transfers between devices with their start and end apart: 48, of which 18 were waited for; matrix products, arithmetic and copies ran while one was open for 8% of the time, Pallas kernels for 38%

profile of v4, /device:TPU:0, one launch (start us, length us, event | category | flops | bytes accessed | tf_op | source)
XLA Modules:
  0.0 330.0 jit_solution(1356870611772413160)
XLA Ops:
  8.3 2.1 dynamic-slice_select_fusion.1
  10.9 3.0 collective-permute-start
  17.1 2.6 collective-permute-start.5
  20.5 11.4 %side_taps.1 = (bf16[576,128]{1,0:T(8,128)(2,1)}, bf16[576,128]{1,0:T(8,128)(2,1)}, bf16[576,128]{1,0:T(8,128)(2,1)}, bf16[576,128]{1,0:T(8,128)(2,1)}, bf16[576...) custom-call(s32[24]{0:T(128)} %copy-done.5, s32[3]{0:T(128)} %pad_add_fusion.low_ref, bf16[1152,2048]{1,0:T(8,128)(2,1)} %bitcast.64, ...), custom_call_target="tpu_custom_call" | custom-call | flops 5435817984 | bytes 10000000 | tf_op jit(solution)/shard_map/side_taps/pallas_call | solution.py:843
  35.9 9.2 %collective-permute-start.7 = (bf16[576,128]{1,0:T(8,128)(2,1)}, bf16[576,128]{1,0:T(8,128)(2,1)S(1)}, u32[]{:S(2)}, u32[]{:S(2)}) collective-permute-start(bf16[576,128]{1,0:T(8,128)(2,1)} %get-tuple-element.71), channel_id=1, source_target_pairs={{0,8},{4,12},{16,24},{20,28},{8,0},{12,4},{24,16},{28,20},{1,9},{5... | collective-permute-start | bytes 442376 | tf_op jit(solution)/shard_map/ppermute | solution.py:524
  45.8 9.8 %collective-permute-start.9 = (bf16[576,128]{1,0:T(8,128)(2,1)}, bf16[576,128]{1,0:T(8,128)(2,1)S(1)}, u32[]{:S(2)}, u32[]{:S(2)}) collective-permute-start(bf16[576,128]{1,0:T(8,128)(2,1)} %get-tuple-element.73), channel_id=1, source_target_pairs={{0,12},{4,16},{8,20},{12,0},{16,4},{20,8},{1,13},{5,17},{9,21},{13... | collective-permute-start | bytes 442376 | tf_op jit(solution)/shard_map/ppermute | solution.py:524
  55.7 9.1 %centre_taps.1 = (f32[1152,256]{1,0:T(8,128)}, f32[8,2048]{1,0:T(8,128)}) custom-call(s32[24]{0:T(128)} %copy-done.5, bf16[1152,2048]{1,0:T(8,128)(2,1)} %bitcast.65, bf16[3,3,3,64,2048]{4,3,2,1,0:T(8,128)(2,1)} %wc_ref.1, bf16[64,2048]{1,0:T(8,128)(2,1)} %wp_ref.1), custom_call_target="tpu_custom_call" | custom-call | flops 3019898880 | bytes 8000000 | tf_op jit(solution)/shard_map/centre_taps/pallas_call | solution.py:885
  67.4 2.0 combine_taps.1
  69.9 2.9 collective-permute-start.13
  72.7 2.0 collective-permute-done.13
  76.9 2.2 collective-permute-start.16
  80.0 3.9 %collective-permute-done.15 = f32[40,256]{1,0:T(8,128)S(1)} collective-permute-done((f32[40,256]{1,0:T(8,128)S(1)}, f32[40,256]{1,0:T(8,128)S(1)}, u32[]{:S(2)}, u32[]{:S(2)}) %collective-permute-start.15) | collective-permute-done | bytes 40992 | tf_op jit(solution)/shard_map/ppermute | solution.py:529
  92.0 4.3 %mix_branches.1 = (f32[1152,256]{1,0:T(8,128)S(1)}, bf16[1152,256]{1,0:T(8,128)(2,1)S(1)}, f32[8,256]{1,0:T(8,128)S(1)}, f32[8,256]{1,0:T(8,128)S(1)}) custom-call(s32[24]{0:T(128)S(1)} %copy-done.6, f32[1]{0:T(128)} %bitcast.2.n_ref, f32[1152,256]{1,0:T(8,128)S(1)} %get-tuple-element.76.conv_ref, bf16[1152,256]{1,0:T(8,128)(2,1)S(1)} %collective-permute-done.11.c1_ref, ...), custom_call_target="tpu_custom_call" | custom-call | flops 603979776 | bytes 6000000 | tf_op jit(solution)/shard_map/mix_branches/pallas_call | solution.py:938
  98.5 4.6 %collective-permute-done.22 = f32[8,256]{1,0:T(8,128)S(1)} collective-permute-done((f32[8,256]{1,0:T(8,128)S(1)}, f32[8,256]{1,0:T(8,128)S(1)}, u32[]{:S(2)}, u32[]{:S(2)}) %collective-permute-start.22) | collective-permute-done | bytes 8224 | tf_op jit(solution)/shard_map/ppermute | solution.py:529
  103.1 4.5 %collective-permute-start.23 = (f32[8,256]{1,0:T(8,128)S(1)}, f32[8,256]{1,0:T(8,128)S(1)}, u32[]{:S(2)}, u32[]{:S(2)}) collective-permute-start(f32[8,256]{1,0:T(8,128)S(1)} %add.269.s0), channel_id=1, source_target_pairs={{0,8},{4,12},{8,0},{12,4},{16,24},{20,28},{24,16},{28,20},{1,9},{5... | collective-permute-start | bytes 24584 | tf_op jit(solution)/shard_map/ppermute | solution.py:529
  109.9 2.4 collective-permute-done.24.s2
  113.7 2.2 final_norm.1
  116.0 2.2 collective-permute-start.26
  120.3 2.7 collective-permute-start.28
  125.2 3.3 collective-permute-done.29.s3
  128.5 2.5 branch_grads.1
  131.4 2.2 collective-permute-start.30
  133.6 2.5 collective-permute-done.30
  138.2 2.6 collective-permute-start.33
  142.7 3.1 collective-permute-done.32
  153.1 4.8 %collective-permute-done.34.cg_ref.refs_1_.refs_9_ = bf16[272,1152]{1,0:T(8,128)(2,1)S(1)} collective-permute-done((bf16[272,1152]{1,0:T(8,128)(2,1)S(1)}, bf16[272,1152]{1,0:T(8,128)(2,1)S(1)}, u32[]{:S(2)}, u32[]{:S(2)}) %collective-permute-start.34) | collective-permute-done | bytes 626720 | tf_op jit(solution)/shard_map/ppermute | solution.py:529
  160.2 2.6 column_taps.8.refs_0_
  163.1 20.8 %collective-permute-done.35.cg_ref.refs_2_.refs_10_ = bf16[272,1152]{1,0:T(8,128)(2,1)S(1)} collective-permute-done((bf16[272,1152]{1,0:T(8,128)(2,1)S(1)}, bf16[272,1152]{1,0:T(8,128)(2,1)S(1)}, u32[]{:S(2)}, u32[]{:S(2)}) %collective-permute-start.35) | collective-permute-done | bytes 626720 | tf_op jit(solution)/shard_map/ppermute | solution.py:529
  184.0 2.1 collective-permute-start.39
  187.7 1.9 constant_dynamic-update-slice_fusion.1
  189.7 1.9 constant_dynamic-update-slice_fusion.refs_8_
  191.6 2.5 column_taps.9.refs_1_
  196.0 2.6 column_taps.10.refs_2_
  198.6 4.7 %collective-permute-done.36.cg_ref.refs_3_.refs_11_ = bf16[272,1152]{1,0:T(8,128)(2,1)} collective-permute-done((bf16[272,1152]{1,0:T(8,128)(2,1)S(1)}, bf16[272,1152]{1,0:T(8,128)(2,1)}, u32[]{:S(2)}, u32[]{:S(2)}) %collective-permute-start.36) | collective-permute-done | bytes 626720 | tf_op jit(solution)/shard_map/ppermute | solution.py:529
  203.3 2.5 column_taps.11.refs_3_
  208.1 2.7 column_taps.12.refs_4_
  210.8 2.5 column_taps.14.refs_6_
  213.4 3.3 collective-permute-done.38.cg_ref.refs_5_.refs_13_
  217.5 2.6 column_taps.13.refs_5_
  220.1 8.1 %collective-permute-done.40.cg_ref.refs_7_.refs_15_ = bf16[272,1152]{1,0:T(8,128)(2,1)S(1)} collective-permute-done((bf16[272,1152]{1,0:T(8,128)(2,1)S(1)}, bf16[272,1152]{1,0:T(8,128)(2,1)S(1)}, u32[]{:S(2)}, u32[]{:S(2)}) %collective-permute-start.40) | collective-permute-done | bytes 626720 | tf_op jit(solution)/shard_map/ppermute | solution.py:529
  229.0 2.5 column_taps.15.refs_7_
  231.5 14.5 %narrow_weight_grads.1 = bf16[1792,128]{1,0:T(8,128)(2,1)} custom-call(s32[3]{0:T(128)} %pad_add_fusion.1.pos_ref, bf16[640,1152]{1,0:T(8,128)(2,1)} %column_taps.8.refs_0_, bf16[640,1152]{1,0:T(8,128)(2,1)} %column_taps.9.refs_1_, bf16[640,1152]{1,0:T(8,128)(2,1)} %column_taps.10.refs_2_, bf16[640,1152]{1,0:T(8,128)(2,1)} %column_taps.11.refs_3_, ...), custom_call_target="tpu_custom_call" | custom-call | flops 4227858432 | bytes 12000000 | tf_op jit(solution)/shard_map/narrow_weight_grads/pallas_call | solution.py:1079
  246.6 18.3 %input_grads.1 = (bf16[2,1152,512]{2,1,0:T(8,128)(2,1)}, bf16[2,1152,512]{2,1,0:T(8,128)(2,1)}) custom-call(s32[3]{0:T(128)} %pad_add_fusion.1.pos_ref, s32[24]{0:T(128)} %copy-done.5, s32[8,1152]{1,0:T(8,128)} %broadcast_in_dim.93.col_ref, bf16[1728,2048]{1,0:T(8,128)(2,1)} %bitcast.61, bf16[64,2048]{1,0:T(8,128)(2,1)} %wp_ref.1, f32[8,2048]{1,0:T(8,128)} %pad.19.pool_ref, ...), custom_call_target="tpu_custom_call" | custom-call | flops 1000000 | bytes 1000000 | tf_op jit(solution)/shard_map/input_grads/pallas_call | solution.py:1098
  265.0 4.7 %collective-permute-done.44 = bf16[2,1152,512]{2,1,0:T(8,128)(2,1)S(1)} collective-permute-done((bf16[2,1152,512]{2,1,0:T(8,128)(2,1)}, bf16[2,1152,512]{2,1,0:T(8,128)(2,1)S(1)}, u32[]{:S(2)}, u32[]{:S(2)}) %collective-permute-start.44) | collective-permute-done | bytes 2359328 | tf_op jit(solution)/shard_map/ppermute | solution.py:529
  270.5 1.9 fusion.4
  274.7 38.8 %wide_weight_grads.1 = (f32[1728,2048]{1,0:T(8,128)}, f32[64,2048]{1,0:T(8,128)}, f32[320,256]{1,0:T(8,128)}) custom-call(s32[3]{0:T(128)} %pad_add_fusion.1.pos_ref, bf16[8,4,1152,256]{3,2,1,0:T(8,128)(2,1)} %bitcast.66, bf16[640,1152]{1,0:T(8,128)(2,1)} %column_taps.8.refs_0_, bf16[640,1152]{1,0:T(8,128)(2,1)} %column_taps.9.refs_1_, ...), custom_call_target="tpu_custom_call" | custom-call | flops 1000000 | bytes 1000000 | tf_op jit(solution)/shard_map/wide_weight_grads/pallas_call | solution.py:1131
  313.5 3.5 %fusion.3 = bf16[1152,512]{1,0:T(8,128)(2,1)} fusion(f32[2,1152,512]{2,1,0:T(8,128)} %copy-done.7, bf16[1152,512]{1,0:T(8,128)(2,1)} %collective-permute-done.45, bf16[2,1152,512]{2,1,0:T(8,128)(2,1)S(1)} %copy-done.14), kind=kLoop, calls=%fused_computation.5 | loop fusion | flops 2949120 | bytes 5898240 | tf_op jit(solution)/shard_map/convert_element_type | solution.py:1153
  317.0 5.7 %widen.1 = (f32[1728,2048]{1,0:T(8,128)}, f32[64,2048]{1,0:T(8,128)}) custom-call(bf16[8,1792,128]{2,1,0:T(8,128)(2,1)} %bitcast.67, bf16[8,1792,128]{2,1,0:T(8,128)(2,1)} %bitcast.68, f32[1728,2048]{1,0:T(8,128)} %get-tuple-element.108.keep_ref, f32[64,2048]{1,0:T(8,128)} %get-tuple-element.106.pkeep_ref), custom_call_target="tpu_custom_call", output_to_operand_aliasing={{0}: (2, {}), {1}: (3, {})} | custom-call | flops 1000000 | bytes 20000000 | tf_op jit(solution)/shard_map/widen/pallas_call | solution.py:1157
  (206 shorter events, 59.8 us)
Async XLA Ops:
  7.2 267.5 %all-gather.5.cloned.1.call-start = ((), (), s32[]{:S(2)}) async-start(), calls=%async_computation | async-start | bytes 19464192 | tf_op jit(solution)/shard_map/all_gather | solution.py:883
  10.5 306.6 %all-gather.7.cloned.1.call-start = ((), (), s32[]{:S(2)}) async-start(), calls=%async_computation.1 | async-start | bytes 4128768 | tf_op jit(solution)/shard_map/all_gather | solution.py:1095
  10.9 21.0 %collective-permute-start = (bf16[336,256]{1,0:T(8,128)(2,1)S(1)}, bf16[336,256]{1,0:T(8,128)(2,1)S(1)}, u32[]{:S(2)}, u32[]{:S(2)}) collective-permute-start(bf16[336,256]{1,0:T(8,128)(2,1)S(1)} %concatenate.48.p0), channel_id=1, source_target_pairs={{0,2},{1,3},{2,0},{3,1},{4,6},{5,7},{6,4},{7,5},{8,10},{9,11},{10,... | collective-permute-start | bytes 516104 | tf_op jit(solution)/shard_map/ppermute | solution.py:529
  13.9 18.0 %collective-permute-start.1 = (bf16[336,256]{1,0:T(8,128)(2,1)S(1)}, bf16[336,256]{1,0:T(8,128)(2,1)S(1)}, u32[]{:S(2)}, u32[]{:S(2)}) collective-permute-start(bf16[336,256]{1,0:T(8,128)(2,1)S(1)} %concatenate.48.p0), channel_id=1, source_target_pairs={{0,1},{1,0},{2,3},{3,2},{4,5},{5,4},{6,7},{7,6},{8,9},{9,8},{10,11... | collective-permute-start | bytes 516104 | tf_op jit(solution)/shard_map/ppermute | solution.py:529
  15.5 18.7 %collective-permute-start.4 = (bf16[288,256]{1,0:T(8,128)(2,1)S(1)}, bf16[288,256]{1,0:T(8,128)(2,1)S(1)}, u32[]{:S(2)}, u32[]{:S(2)}) collective-permute-start(bf16[288,256]{1,0:T(8,128)(2,1)S(1)} %get-tuple-element.127), channel_id=1, source_target_pairs={{0,8},{4,12},{8,0},{12,4},{16,24},{20,28},{24,16},{28,20},{1,9},{5... | collective-permute-start | bytes 442376 | tf_op jit(solution)/shard_map/ppermute | solution.py:529
  17.1 17.1 %collective-permute-start.5 = (bf16[288,256]{1,0:T(8,128)(2,1)S(1)}, bf16[288,256]{1,0:T(8,128)(2,1)S(1)}, u32[]{:S(2)}, u32[]{:S(2)}) collective-permute-start(bf16[288,256]{1,0:T(8,128)(2,1)S(1)} %get-tuple-element.126), channel_id=1, source_target_pairs={{0,16},{4,20},{8,24},{12,28},{16,0},{20,4},{24,8},{28,12},{1,17},{... | collective-permute-start | bytes 442376 | tf_op jit(solution)/shard_map/ppermute | solution.py:529
  19.7 14.5 %collective-permute-start.6 = (bf16[288,256]{1,0:T(8,128)(2,1)S(1)}, bf16[288,256]{1,0:T(8,128)(2,1)S(1)}, u32[]{:S(2)}, u32[]{:S(2)}) collective-permute-start(bf16[288,256]{1,0:T(8,128)(2,1)S(1)} %get-tuple-element.125), channel_id=1, source_target_pairs={{0,24},{4,28},{8,16},{12,20},{16,8},{20,12},{24,0},{28,4},{1,25},{... | collective-permute-start | bytes 442376 | tf_op jit(solution)/shard_map/ppermute | solution.py:529
  32.0 13.9 %collective-permute-start.2 = (bf16[576,128]{1,0:T(8,128)(2,1)}, bf16[576,128]{1,0:T(8,128)(2,1)S(1)}, u32[]{:S(2)}, u32[]{:S(2)}) collective-permute-start(bf16[576,128]{1,0:T(8,128)(2,1)} %get-tuple-element.67), channel_id=1, source_target_pairs={{0,4},{8,12},{16,20},{24,28},{4,0},{12,8},{20,16},{28,24},{1,5},{9... | collective-permute-start | bytes 442376 | tf_op jit(solution)/shard_map/ppermute | solution.py:524
  33.5 22.2 %collective-permute-start.3 = (bf16[576,128]{1,0:T(8,128)(2,1)}, bf16[576,128]{1,0:T(8,128)(2,1)S(1)}, u32[]{:S(2)}, u32[]{:S(2)}) collective-permute-start(bf16[576,128]{1,0:T(8,128)(2,1)} %get-tuple-element.68), channel_id=1, source_target_pairs={{4,8},{12,16},{20,24},{8,4},{16,12},{24,20},{5,9},{13,17},{21,25},... | collective-permute-start | bytes 442376 | tf_op jit(solution)/shard_map/ppermute | solution.py:524
  35.1 30.9 %collective-permute-start.10 = (bf16[576,128]{1,0:T(8,128)(2,1)}, bf16[576,128]{1,0:T(8,128)(2,1)S(1)}, u32[]{:S(2)}, u32[]{:S(2)}) collective-permute-start(bf16[576,128]{1,0:T(8,128)(2,1)} %get-tuple-element.74), channel_id=1, source_target_pairs={{12,24},{16,28},{24,12},{28,16},{13,25},{17,29},{25,13},{29,17},{1... | collective-permute-start | bytes 442376 | tf_op jit(solution)/shard_map/ppermute | solution.py:524
  35.9 30.1 %collective-permute-start.7 = (bf16[576,128]{1,0:T(8,128)(2,1)}, bf16[576,128]{1,0:T(8,128)(2,1)S(1)}, u32[]{:S(2)}, u32[]{:S(2)}) collective-permute-start(bf16[576,128]{1,0:T(8,128)(2,1)} %get-tuple-element.71), channel_id=1, source_target_pairs={{0,8},{4,12},{16,24},{20,28},{8,0},{12,4},{24,16},{28,20},{1,9},{5... | collective-permute-start | bytes 442376 | tf_op jit(solution)/shard_map/ppermute | solution.py:524
  45.2 20.9 %collective-permute-start.8 = (bf16[576,128]{1,0:T(8,128)(2,1)}, bf16[576,128]{1,0:T(8,128)(2,1)S(1)}, u32[]{:S(2)}, u32[]{:S(2)}) collective-permute-start(bf16[576,128]{1,0:T(8,128)(2,1)} %get-tuple-element.72), channel_id=1, source_target_pairs={{8,16},{12,20},{16,8},{20,12},{9,17},{13,21},{17,9},{21,13},{10,18... | collective-permute-start | bytes 442376 | tf_op jit(solution)/shard_map/ppermute | solution.py:524
  45.8 20.3 %collective-permute-start.9 = (bf16[576,128]{1,0:T(8,128)(2,1)}, bf16[576,128]{1,0:T(8,128)(2,1)S(1)}, u32[]{:S(2)}, u32[]{:S(2)}) collective-permute-start(bf16[576,128]{1,0:T(8,128)(2,1)} %get-tuple-element.73), channel_id=1, source_target_pairs={{0,12},{4,16},{8,20},{12,0},{16,4},{20,8},{1,13},{5,17},{9,21},{13... | collective-permute-start | bytes 442376 | tf_op jit(solution)/shard_map/ppermute | solution.py:524
  69.4 14.5 %collective-permute-start.12 = (bf16[1152,256]{1,0:T(8,128)(2,1)}, bf16[1152,256]{1,0:T(8,128)(2,1)S(1)}, u32[]{:S(2)}, u32[]{:S(2)}) collective-permute-start(bf16[1152,256]{1,0:T(8,128)(2,1)} %get-tuple-element.77), channel_id=1, source_target_pairs={{0,2},{1,3},{2,0},{3,1},{4,6},{5,7},{6,4},{7,5},{8,10},{9,11},{10,... | collective-permute-start | bytes 1769480 | tf_op jit(solution)/shard_map/ppermute | solution.py:529
  69.9 4.9 %collective-permute-start.13 = (f32[40,256]{1,0:T(8,128)S(1)}, f32[40,256]{1,0:T(8,128)S(1)}, u32[]{:S(2)}, u32[]{:S(2)}) collective-permute-start(f32[40,256]{1,0:T(8,128)S(1)} %get-tuple-element.78), channel_id=1, source_target_pairs={{0,4},{4,0},{8,12},{12,8},{16,20},{20,16},{24,28},{28,24},{1,5},{5... | collective-permute-start | bytes 122888 | tf_op jit(solution)/shard_map/ppermute | solution.py:529
  74.7 5.3 %collective-permute-start.14 = (f32[40,256]{1,0:T(8,128)S(1)}, f32[40,256]{1,0:T(8,128)S(1)}, u32[]{:S(2)}, u32[]{:S(2)}) collective-permute-start(f32[40,256]{1,0:T(8,128)S(1)} %add.264), channel_id=1, source_target_pairs={{0,8},{4,12},{8,0},{12,4},{16,24},{20,28},{24,16},{28,20},{1,9},{5... | collective-permute-start | bytes 122888 | tf_op jit(solution)/shard_map/ppermute | solution.py:529
  76.2 7.7 %collective-permute-start.15 = (f32[40,256]{1,0:T(8,128)S(1)}, f32[40,256]{1,0:T(8,128)S(1)}, u32[]{:S(2)}, u32[]{:S(2)}) collective-permute-start(f32[40,256]{1,0:T(8,128)S(1)} %add.264), channel_id=1, source_target_pairs={{0,16},{4,20},{8,24},{12,28},{16,0},{20,4},{24,8},{28,12},{1,17},{... | collective-permute-start | bytes 122888 | tf_op jit(solution)/shard_map/ppermute | solution.py:529
  76.9 7.0 %collective-permute-start.16 = (f32[40,256]{1,0:T(8,128)S(1)}, f32[40,256]{1,0:T(8,128)S(1)}, u32[]{:S(2)}, u32[]{:S(2)}) collective-permute-start(f32[40,256]{1,0:T(8,128)S(1)} %add.264), channel_id=1, source_target_pairs={{0,24},{4,28},{8,16},{12,20},{16,8},{20,12},{24,0},{28,4},{1,25},{... | collective-permute-start | bytes 122888 | tf_op jit(solution)/shard_map/ppermute | solution.py:529
  79.6 12.3 %collective-permute-start.11 = (bf16[1152,256]{1,0:T(8,128)(2,1)}, bf16[1152,256]{1,0:T(8,128)(2,1)S(1)}, u32[]{:S(2)}, u32[]{:S(2)}) collective-permute-start(bf16[1152,256]{1,0:T(8,128)(2,1)} %get-tuple-element.77), channel_id=1, source_target_pairs={{0,1},{1,0},{2,3},{3,2},{4,5},{5,4},{6,7},{7,6},{8,9},{9,8},{10,11... | collective-permute-start | bytes 1769480 | tf_op jit(solution)/shard_map/ppermute | solution.py:529
  83.9 8.0 %collective-permute-start.17 = (bf16[1152,256]{1,0:T(8,128)(2,1)S(1)}, bf16[1152,256]{1,0:T(8,128)(2,1)}, u32[]{:S(2)}, u32[]{:S(2)}) collective-permute-start(bf16[1152,256]{1,0:T(8,128)(2,1)S(1)} %collective-permute-done.12.c2_ref), channel_id=1, source_target_pairs={{0,1},{1,0},{2,3},{3,2},{4,5},{5,4},{6,7},{7,6},{8,9},{9,8},{10,11... | collective-permute-start | bytes 1769480 | tf_op jit(solution)/shard_map/ppermute | solution.py:529
  84.7 4.1 %collective-permute-start.21 = (bf16[336,256]{1,0:T(8,128)(2,1)S(1)}, bf16[336,256]{1,0:T(8,128)(2,1)S(1)}, u32[]{:S(2)}, u32[]{:S(2)}) collective-permute-start(bf16[336,256]{1,0:T(8,128)(2,1)S(1)} %collective-permute-done.p2), channel_id=1, source_target_pairs={{0,1},{1,0},{2,3},{3,2},{4,5},{5,4},{6,7},{7,6},{8,9},{9,8},{10,11... | collective-permute-start | bytes 516104 | tf_op jit(solution)/shard_map/ppermute | solution.py:529
  86.0 3.1 collective-permute-start.18
  86.0 4.7 %collective-permute-start.19 = (f32[8,256]{1,0:T(8,128)S(1)}, f32[8,256]{1,0:T(8,128)S(1)}, u32[]{:S(2)}, u32[]{:S(2)}) collective-permute-start(f32[8,256]{1,0:T(8,128)S(1)} %fusion.19.t0), channel_id=1, source_target_pairs={{0,2},{1,3},{2,0},{3,1},{4,6},{5,7},{6,4},{7,5},{8,10},{9,11},{10,... | collective-permute-start | bytes 24584 | tf_op jit(solution)/shard_map/ppermute | solution.py:529
  88.8 3.1 collective-permute-start.20
  89.0 29.1 %collective-permute-start.41 = (bf16[4,288,128]{2,1,0:T(8,128)(2,1)S(1)}, bf16[4,288,128]{2,1,0:T(8,128)(2,1)S(1)}, u32[]{:S(2)}, u32[]{:S(2)}) collective-permute-start(bf16[4,288,128]{2,1,0:T(8,128)(2,1)S(1)} %get-tuple-element.124), channel_id=1, source_target_pairs={{0,4},{4,0},{8,12},{12,8},{16,20},{20,16},{24,28},{28,24},{1,5},{5... | collective-permute-start | bytes 884744 | tf_op jit(solution)/shard_map/ppermute | solution.py:529
  96.2 6.8 %collective-permute-start.22 = (f32[8,256]{1,0:T(8,128)S(1)}, f32[8,256]{1,0:T(8,128)S(1)}, u32[]{:S(2)}, u32[]{:S(2)}) collective-permute-start(f32[8,256]{1,0:T(8,128)S(1)} %get-tuple-element.82), channel_id=1, source_target_pairs={{0,4},{4,0},{8,12},{12,8},{16,20},{20,16},{24,28},{28,24},{1,5},{5... | collective-permute-start | bytes 24584 | tf_op jit(solution)/shard_map/ppermute | solution.py:529
  103.1 6.9 %collective-permute-start.23 = (f32[8,256]{1,0:T(8,128)S(1)}, f32[8,256]{1,0:T(8,128)S(1)}, u32[]{:S(2)}, u32[]{:S(2)}) collective-permute-start(f32[8,256]{1,0:T(8,128)S(1)} %add.269.s0), channel_id=1, source_target_pairs={{0,8},{4,12},{8,0},{12,4},{16,24},{20,28},{24,16},{28,20},{1,9},{5... | collective-permute-start | bytes 24584 | tf_op jit(solution)/shard_map/ppermute | solution.py:529
  107.6 4.8 %collective-permute-start.24 = (f32[8,256]{1,0:T(8,128)S(1)}, f32[8,256]{1,0:T(8,128)S(1)}, u32[]{:S(2)}, u32[]{:S(2)}) collective-permute-start(f32[8,256]{1,0:T(8,128)S(1)} %add.269.s0), channel_id=1, source_target_pairs={{0,16},{4,20},{8,24},{12,28},{16,0},{20,4},{24,8},{28,12},{1,17},{... | collective-permute-start | bytes 24584 | tf_op jit(solution)/shard_map/ppermute | solution.py:529
  108.1 5.6 %collective-permute-start.25 = (f32[8,256]{1,0:T(8,128)S(1)}, f32[8,256]{1,0:T(8,128)S(1)}, u32[]{:S(2)}, u32[]{:S(2)}) collective-permute-start(f32[8,256]{1,0:T(8,128)S(1)} %add.269.s0), channel_id=1, source_target_pairs={{0,24},{4,28},{8,16},{12,20},{16,8},{20,12},{24,0},{28,4},{1,25},{... | collective-permute-start | bytes 24584 | tf_op jit(solution)/shard_map/ppermute | solution.py:529
  116.0 4.0 %collective-permute-start.26 = (f32[8,256]{1,0:T(8,128)S(1)}, f32[8,256]{1,0:T(8,128)S(1)}, u32[]{:S(2)}, u32[]{:S(2)}) collective-permute-start(f32[8,256]{1,0:T(8,128)S(1)} %get-tuple-element.88), channel_id=1, source_target_pairs={{0,4},{4,0},{8,12},{12,8},{16,20},{20,16},{24,28},{28,24},{1,5},{5... | collective-permute-start | bytes 24584 | tf_op jit(solution)/shard_map/ppermute | solution.py:529
  119.9 5.3 %collective-permute-start.27 = (f32[8,256]{1,0:T(8,128)S(1)}, f32[8,256]{1,0:T(8,128)S(1)}, u32[]{:S(2)}, u32[]{:S(2)}) collective-permute-start(f32[8,256]{1,0:T(8,128)S(1)} %add.273.s0), channel_id=1, source_target_pairs={{0,8},{4,12},{8,0},{12,4},{16,24},{20,28},{24,16},{28,20},{1,9},{5... | collective-permute-start | bytes 24584 | tf_op jit(solution)/shard_map/ppermute | solution.py:529
  120.3 4.9 %collective-permute-start.28 = (f32[8,256]{1,0:T(8,128)S(1)}, f32[8,256]{1,0:T(8,128)S(1)}, u32[]{:S(2)}, u32[]{:S(2)}) collective-permute-start(f32[8,256]{1,0:T(8,128)S(1)} %add.273.s0), channel_id=1, source_target_pairs={{0,16},{4,20},{8,24},{12,28},{16,0},{20,4},{24,8},{28,12},{1,17},{... | collective-permute-start | bytes 24584 | tf_op jit(solution)/shard_map/ppermute | solution.py:529
  123.0 5.5 %collective-permute-start.29 = (f32[8,256]{1,0:T(8,128)S(1)}, f32[8,256]{1,0:T(8,128)S(1)}, u32[]{:S(2)}, u32[]{:S(2)}) collective-permute-start(f32[8,256]{1,0:T(8,128)S(1)} %add.273.s0), channel_id=1, source_target_pairs={{0,24},{4,28},{8,16},{12,20},{16,8},{20,12},{24,0},{28,4},{1,25},{... | collective-permute-start | bytes 24584 | tf_op jit(solution)/shard_map/ppermute | solution.py:529
  131.4 4.7 %collective-permute-start.30 = (bf16[184,256]{1,0:T(8,128)(2,1)S(1)}, bf16[184,256]{1,0:T(8,128)(2,1)S(1)}, u32[]{:S(2)}, u32[]{:S(2)}) collective-permute-start(bf16[184,256]{1,0:T(8,128)(2,1)S(1)} %pad_maximum_fusion.2), channel_id=1, source_target_pairs={{0,4},{4,0},{8,12},{12,8},{16,20},{20,16},{24,28},{28,24},{1,5},{5... | collective-permute-start | bytes 282632 | tf_op jit(solution)/shard_map/ppermute | solution.py:529
  136.3 6.3 %collective-permute-start.31 = (bf16[64,256]{1,0:T(8,128)(2,1)S(1)}, bf16[64,256]{1,0:T(8,128)(2,1)S(1)}, u32[]{:S(2)}, u32[]{:S(2)}) collective-permute-start(bf16[64,256]{1,0:T(8,128)(2,1)S(1)} %get-tuple-element.132), channel_id=1, source_target_pairs={{0,8},{4,12},{8,0},{12,4},{16,24},{20,28},{24,16},{28,20},{1,9},{5... | collective-permute-start | bytes 98312 | tf_op jit(solution)/shard_map/ppermute | solution.py:529
  137.5 8.2 %collective-permute-start.32 = (bf16[64,256]{1,0:T(8,128)(2,1)S(1)}, bf16[64,256]{1,0:T(8,128)(2,1)S(1)}, u32[]{:S(2)}, u32[]{:S(2)}) collective-permute-start(bf16[64,256]{1,0:T(8,128)(2,1)S(1)} %get-tuple-element.133), channel_id=1, source_target_pairs={{0,16},{4,20},{8,24},{12,28},{16,0},{20,4},{24,8},{28,12},{1,17},{... | collective-permute-start | bytes 98312 | tf_op jit(solution)/shard_map/ppermute | solution.py:529
  138.2 7.6 %collective-permute-start.33 = (bf16[64,256]{1,0:T(8,128)(2,1)S(1)}, bf16[64,256]{1,0:T(8,128)(2,1)S(1)}, u32[]{:S(2)}, u32[]{:S(2)}) collective-permute-start(bf16[64,256]{1,0:T(8,128)(2,1)S(1)} %get-tuple-element.134), channel_id=1, source_target_pairs={{0,24},{4,28},{8,16},{12,20},{16,8},{20,12},{24,0},{28,4},{1,25},{... | collective-permute-start | bytes 98312 | tf_op jit(solution)/shard_map/ppermute | solution.py:529
  147.5 10.3 %collective-permute-start.34 = (bf16[272,1152]{1,0:T(8,128)(2,1)S(1)}, bf16[272,1152]{1,0:T(8,128)(2,1)S(1)}, u32[]{:S(2)}, u32[]{:S(2)}) collective-permute-start(bf16[272,1152]{1,0:T(8,128)(2,1)S(1)} %conv_grads.1.cg_ref.refs_0_.refs_8_), channel_id=1, source_target_pairs={{0,4},{4,0},{8,12},{12,8},{16,20},{20,16},{24,28},{28,24},{1,5},{5... | collective-permute-start | bytes 1880072 | tf_op jit(solution)/shard_map/ppermute | solution.py:529
  148.4 35.6 %collective-permute-start.35 = (bf16[272,1152]{1,0:T(8,128)(2,1)S(1)}, bf16[272,1152]{1,0:T(8,128)(2,1)S(1)}, u32[]{:S(2)}, u32[]{:S(2)}) collective-permute-start(bf16[272,1152]{1,0:T(8,128)(2,1)S(1)} %conv_grads.1.cg_ref.refs_0_.refs_8_), channel_id=1, source_target_pairs={{0,8},{4,12},{8,0},{12,4},{16,24},{20,28},{24,16},{28,20},{1,9},{5... | collective-permute-start | bytes 1880072 | tf_op jit(solution)/shard_map/ppermute | solution.py:529
  150.1 45.5 %collective-permute-start.37 = (bf16[272,1152]{1,0:T(8,128)(2,1)S(1)}, bf16[272,1152]{1,0:T(8,128)(2,1)S(1)}, u32[]{:S(2)}, u32[]{:S(2)}) collective-permute-start(bf16[272,1152]{1,0:T(8,128)(2,1)S(1)} %conv_grads.1.cg_ref.refs_0_.refs_8_), channel_id=1, source_target_pairs={{0,16},{4,20},{8,24},{12,28},{16,0},{20,4},{24,8},{28,12},{1,17},{... | collective-permute-start | bytes 1880072 | tf_op jit(solution)/shard_map/ppermute | solution.py:529
  157.9 31.8 %collective-permute-start.42 = (bf16[1,8,288,128]{3,2,1,0:T(8,128)(2,1)}, bf16[1,8,288,128]{3,2,1,0:T(8,128)(2,1)}, u32[]{:S(2)}, u32[]{:S(2)}) collective-permute-start(bf16[1,8,288,128]{3,2,1,0:T(8,128)(2,1)} %bitcast.70), channel_id=1, source_target_pairs={{0,2},{1,3},{2,0},{3,1},{4,6},{5,7},{6,4},{7,5},{8,10},{9,11},{10,... | collective-permute-start | bytes 1769480 | tf_op jit(solution)/shard_map/ppermute | solution.py:529
  184.0 21.9 %collective-permute-start.39 = (bf16[272,1152]{1,0:T(8,128)(2,1)}, bf16[272,1152]{1,0:T(8,128)(2,1)S(1)}, u32[]{:S(2)}, u32[]{:S(2)}) collective-permute-start(bf16[272,1152]{1,0:T(8,128)(2,1)} %copy-done.2), channel_id=1, source_target_pairs={{0,24},{4,28},{8,16},{12,20},{16,8},{20,12},{24,0},{28,4},{1,25},{... | collective-permute-start | bytes 1880072 | tf_op jit(solution)/shard_map/ppermute | solution.py:529
  186.1 17.2 %collective-permute-start.36 = (bf16[272,1152]{1,0:T(8,128)(2,1)S(1)}, bf16[272,1152]{1,0:T(8,128)(2,1)}, u32[]{:S(2)}, u32[]{:S(2)}) collective-permute-start(bf16[272,1152]{1,0:T(8,128)(2,1)S(1)} %collective-permute-done.35.cg_ref.refs_2_.refs_10_), channel_id=1, source_target_pairs={{0,4},{4,0},{8,12},{12,8},{16,20},{20,16},{24,28},{28,24},{1,5},{5... | collective-permute-start | bytes 1880072 | tf_op jit(solution)/shard_map/ppermute | solution.py:529
  191.6 39.9 %collective-permute-start.43 = (bf16[2,8,288,128]{3,2,1,0:T(8,128)(2,1)}, bf16[2,8,288,128]{3,2,1,0:T(8,128)(2,1)}, u32[]{:S(2)}, u32[]{:S(2)}) collective-permute-start(bf16[2,8,288,128]{3,2,1,0:T(8,128)(2,1)} %constant_dynamic-update-slice_fusion.refs_8_), channel_id=1, source_target_pairs={{0,1},{1,0},{2,3},{3,2},{4,5},{5,4},{6,7},{7,6},{8,9},{9,8},{10,11... | collective-permute-start | bytes 3538952 | tf_op jit(solution)/shard_map/ppermute | solution.py:529
  195.6 21.1 %collective-permute-start.38 = (bf16[272,1152]{1,0:T(8,128)(2,1)S(1)}, bf16[272,1152]{1,0:T(8,128)(2,1)S(1)}, u32[]{:S(2)}, u32[]{:S(2)}) collective-permute-start(bf16[272,1152]{1,0:T(8,128)(2,1)S(1)} %collective-permute-done.37.cg_ref.refs_4_.refs_12_), channel_id=1, source_target_pairs={{0,4},{4,0},{8,12},{12,8},{16,20},{20,16},{24,28},{28,24},{1,5},{5... | collective-permute-start | bytes 1880072 | tf_op jit(solution)/shard_map/ppermute | solution.py:529
  205.9 22.3 %collective-permute-start.40 = (bf16[272,1152]{1,0:T(8,128)(2,1)S(1)}, bf16[272,1152]{1,0:T(8,128)(2,1)S(1)}, u32[]{:S(2)}, u32[]{:S(2)}) collective-permute-start(bf16[272,1152]{1,0:T(8,128)(2,1)S(1)} %collective-permute-done.39.cg_ref.refs_6_.refs_14_), channel_id=1, source_target_pairs={{0,4},{4,0},{8,12},{12,8},{16,20},{20,16},{24,28},{28,24},{1,5},{5... | collective-permute-start | bytes 1880072 | tf_op jit(solution)/shard_map/ppermute | solution.py:529
  265.0 4.8 %collective-permute-start.44 = (bf16[2,1152,512]{2,1,0:T(8,128)(2,1)}, bf16[2,1152,512]{2,1,0:T(8,128)(2,1)S(1)}, u32[]{:S(2)}, u32[]{:S(2)}) collective-permute-start(bf16[2,1152,512]{2,1,0:T(8,128)(2,1)} %get-tuple-element.104), channel_id=1, source_target_pairs={{0,1},{1,0},{2,3},{3,2},{4,5},{5,4},{6,7},{7,6},{8,9},{9,8},{10,11... | collective-permute-start | bytes 7077896 | tf_op jit(solution)/shard_map/ppermute | solution.py:529
  273.0 40.6 %collective-permute-start.45 = (bf16[1152,512]{1,0:T(8,128)(2,1)}, bf16[1152,512]{1,0:T(8,128)(2,1)}, u32[]{:S(2)}, u32[]{:S(2)}) collective-permute-start(bf16[1152,512]{1,0:T(8,128)(2,1)} %fusion.4), channel_id=1, source_target_pairs={{0,2},{1,3},{2,0},{3,1},{4,6},{5,7},{6,4},{7,5},{8,10},{9,11},{10,... | collective-permute-start | bytes 3538952 | tf_op jit(solution)/shard_map/ppermute | solution.py:529
  (29 other events, 306.3 us)
Sparse Core Ops, SparseCore 0:
  11.0 166.7 all-gather.4
  246.1 65.0 all-gather.6

commit v5 on v4

--- a/solution.py
+++ b/solution.py
@@ -875,13 +875,15 @@
     image = jnp.where(lax.dynamic_slice_in_dim(valid, own * part, part), image, jnp.zeros((), bf16))
     column = block_id // 2
     sent = [lax.dynamic_slice_in_dim(image, (column ^ dz) * 2 * cut, 2 * cut, 1) for dz in range(4)]
-    mine = jnp.stack([sent[0]] + [swap(sent[dz], "sp", 2 * dz) for dz in (1, 2, 3)])
+    pieces = sent
+    sent = [sent[0]] + [swap(sent[dz], "sp", 2 * dz) for dz in (1, 2, 3)]
+    mine = jnp.stack(sent)
     wide_w = (C - narrow) // 4
     own_wide = lax.dynamic_slice_in_dim(x, narrow + own * wide_w, wide_w, 1)
     own_wide = jnp.where(valid, own_wide, jnp.zeros((), bf16))
-    halo, made = side_taps((0, 1, 2), after(x, packed, own_wide, *sent))
+    halo, made = side_taps((0, 1, 2), after(x, packed, own_wide, *pieces))
     x_wide = lax.all_gather(own_wide, ("sp", "ch"), axis=0).reshape(BLOCKS, 4, cells, wide_w)
-    x_then = after(x, made, halo[0], halo[1], mine)
+    x_then = after(x, made, halo[0], halo[1], *sent)
     centre, sums = pl.pallas_call(
         functools.partial(centre_kernel, steps=steps, slabs=slabs, cols=cols, rates=rates, images=images),
         grid=(steps,),

time: 336 us -> 334 us (level)
    ppermute x6, starting transfers between devices: 22.7 us -> 18.7 us  [neighbours(): rounds.append(lax.ppermute(block, axis, grouped(pairs, size)))]
  transfers between devices with their start and end apart: 48 -> 48, of which waited for: 18 -> 19; matrix products, arithmetic and copies ran while one was open for 8% -> 8% of each run, Pallas kernels for 38% -> 38%
where the time goes in v5:
time: 334 us; the launch traced here: 328 us
  Pallas kernels  131 us (39%)
  starting transfers between devices  76.3 us (23%)
  waiting for transfers between devices  74.3 us (22%)
  other arithmetic  17.2 us (5%)
  between operations  15.2 us (5%)
  local copies, waits for them, and re-layouts  12.4 us (4%)
    ppermute x40, waiting for transfers between devices, swap(): lax.ppermute(block, axis, [(i, i ^ bits) for i in range(lax.axis_size(axi...  74.2 us
    ppermute x40, starting transfers between devices, swap(): lax.ppermute(block, axis, [(i, i ^ bits) for i in range(lax.axis_size(axi...  57.5 us
    pallas_call x1, Pallas kernels, body(): pl.pallas_call(wide_kernel, grid=(4,), in_specs=[SMEM, pl.BlockSpec((BLOC...  38.8 us
    pallas_call x8, Pallas kernels, column_taps(): pl.pallas_call(functools.partial(expand_kernel, cols=cols, rates=rates),...  20.4 us
    ppermute x6, starting transfers between devices, neighbours(): rounds.append(lax.ppermute(block, axis, grouped(pairs, size)))  18.7 us
    pallas_call x1, Pallas kernels, body(): pl.pallas_call(functools.partial(input_grad_kernel, slabs=slabs, cols=col...  18.3 us
    pallas_call x1, Pallas kernels, body(): pl.pallas_call(functools.partial(narrow_kernel, parts=images), in_specs=[...  14.4 us
    pallas_call x1, Pallas kernels, side_taps(): pl.pallas_call(functools.partial(side_kernel, steps=steps, slabs=slabs, c...  11.4 us
  transfers between devices with their start and end apart: 48, of which 19 were waited for; matrix products, arithmetic and copies ran while one was open for 8% of the time, Pallas kernels for 38%

profile of v5, /device:TPU:0, one launch (start us, length us, event | category | flops | bytes accessed | tf_op | source)
XLA Modules:
  0.0 328.3 jit_solution(11364890764873526182)
XLA Ops:
  8.3 2.1 dynamic-slice_select_fusion.1
  10.9 3.0 collective-permute-start
  17.7 2.6 collective-permute-start.5
  21.1 11.4 %side_taps.1 = (bf16[576,128]{1,0:T(8,128)(2,1)}, bf16[576,128]{1,0:T(8,128)(2,1)}, bf16[576,128]{1,0:T(8,128)(2,1)}, bf16[576,128]{1,0:T(8,128)(2,1)}, bf16[576...) custom-call(s32[24]{0:T(128)} %copy-done.5, s32[3]{0:T(128)} %pad_add_fusion.low_ref, bf16[1152,2048]{1,0:T(8,128)(2,1)} %bitcast.64, ...), custom_call_target="tpu_custom_call" | custom-call | flops 5435817984 | bytes 10000000 | tf_op jit(solution)/shard_map/side_taps/pallas_call | solution.py:843
  35.6 3.3 %collective-permute-start.7 = (bf16[576,128]{1,0:T(8,128)(2,1)}, bf16[576,128]{1,0:T(8,128)(2,1)S(1)}, u32[]{:S(2)}, u32[]{:S(2)}) collective-permute-start(bf16[576,128]{1,0:T(8,128)(2,1)} %get-tuple-element.71), channel_id=1, source_target_pairs={{0,8},{4,12},{16,24},{20,28},{8,0},{12,4},{24,16},{28,20},{1,9},{5... | collective-permute-start | bytes 442376 | tf_op jit(solution)/shard_map/ppermute | solution.py:524
  39.6 11.9 %collective-permute-start.9 = (bf16[576,128]{1,0:T(8,128)(2,1)}, bf16[576,128]{1,0:T(8,128)(2,1)S(1)}, u32[]{:S(2)}, u32[]{:S(2)}) collective-permute-start(bf16[576,128]{1,0:T(8,128)(2,1)} %get-tuple-element.73), channel_id=1, source_target_pairs={{0,12},{4,16},{8,20},{12,0},{16,4},{20,8},{1,13},{5,17},{9,21},{13... | collective-permute-start | bytes 442376 | tf_op jit(solution)/shard_map/ppermute | solution.py:524
  51.4 9.2 %centre_taps.1 = (f32[1152,256]{1,0:T(8,128)}, f32[8,2048]{1,0:T(8,128)}) custom-call(s32[24]{0:T(128)} %copy-done.5, bf16[1152,2048]{1,0:T(8,128)(2,1)} %bitcast.65, bf16[3,3,3,64,2048]{4,3,2,1,0:T(8,128)(2,1)} %wc_ref.1, bf16[64,2048]{1,0:T(8,128)(2,1)} %wp_ref.1), custom_call_target="tpu_custom_call" | custom-call | flops 3019898880 | bytes 8000000 | tf_op jit(solution)/shard_map/centre_taps/pallas_call | solution.py:887
  65.7 3.0 collective-permute-start.13
  68.7 2.8 collective-permute-done.13
  71.5 2.5 collective-permute-start.14
  85.3 2.1 collective-permute-start.19
  87.6 2.3 collective-permute-start.41
  90.6 4.1 %mix_branches.1 = (f32[1152,256]{1,0:T(8,128)S(1)}, bf16[1152,256]{1,0:T(8,128)(2,1)S(1)}, f32[8,256]{1,0:T(8,128)S(1)}, f32[8,256]{1,0:T(8,128)S(1)}) custom-call(s32[24]{0:T(128)S(1)} %copy-done.6, f32[1]{0:T(128)} %bitcast.2.n_ref, f32[1152,256]{1,0:T(8,128)S(1)} %get-tuple-element.76.conv_ref, bf16[1152,256]{1,0:T(8,128)(2,1)S(1)} %collective-permute-done.11.c1_ref, ...), custom_call_target="tpu_custom_call" | custom-call | flops 603979776 | bytes 6000000 | tf_op jit(solution)/shard_map/mix_branches/pallas_call | solution.py:940
  94.7 2.2 collective-permute-start.22
  97.0 3.0 collective-permute-done.22
  100.0 5.1 %collective-permute-start.23 = (f32[8,256]{1,0:T(8,128)S(1)}, f32[8,256]{1,0:T(8,128)S(1)}, u32[]{:S(2)}, u32[]{:S(2)}) collective-permute-start(f32[8,256]{1,0:T(8,128)S(1)} %add.269.s0), channel_id=1, source_target_pairs={{0,8},{4,12},{8,0},{12,4},{16,24},{20,28},{24,16},{28,20},{1,9},{5... | collective-permute-start | bytes 24584 | tf_op jit(solution)/shard_map/ppermute | solution.py:529
  107.5 2.4 collective-permute-done.24.s2
  111.2 2.2 final_norm.1
  113.5 2.6 collective-permute-start.26
  117.9 2.0 collective-permute-start.27
  123.1 3.4 %collective-permute-done.28.s2 = f32[8,256]{1,0:T(8,128)S(1)} collective-permute-done((f32[8,256]{1,0:T(8,128)S(1)}, f32[8,256]{1,0:T(8,128)S(1)}, u32[]{:S(2)}, u32[]{:S(2)}) %collective-permute-start.28) | collective-permute-done | bytes 8224 | tf_op jit(solution)/shard_map/ppermute | solution.py:529
  126.6 2.4 branch_grads.1
  129.5 2.0 collective-permute-start.30
  131.6 2.6 collective-permute-done.30
  134.3 2.8 collective-permute-start.31
  137.1 2.4 collective-permute-start.33
  141.7 3.7 %collective-permute-done.32 = bf16[64,256]{1,0:T(8,128)(2,1)S(1)} collective-permute-done((bf16[64,256]{1,0:T(8,128)(2,1)S(1)}, bf16[64,256]{1,0:T(8,128)(2,1)S(1)}, u32[]{:S(2)}, u32[]{:S(2)}) %collective-permute-start.32) | collective-permute-done | bytes 32800 | tf_op jit(solution)/shard_map/ppermute | solution.py:529
  152.0 5.4 %collective-permute-done.34.cg_ref.refs_1_.refs_9_ = bf16[272,1152]{1,0:T(8,128)(2,1)S(1)} collective-permute-done((bf16[272,1152]{1,0:T(8,128)(2,1)S(1)}, bf16[272,1152]{1,0:T(8,128)(2,1)S(1)}, u32[]{:S(2)}, u32[]{:S(2)}) %collective-permute-start.34) | collective-permute-done | bytes 626720 | tf_op jit(solution)/shard_map/ppermute | solution.py:529
  158.1 2.6 column_taps.8.refs_0_
  160.9 22.1 %collective-permute-done.35.cg_ref.refs_2_.refs_10_ = bf16[272,1152]{1,0:T(8,128)(2,1)S(1)} collective-permute-done((bf16[272,1152]{1,0:T(8,128)(2,1)S(1)}, bf16[272,1152]{1,0:T(8,128)(2,1)S(1)}, u32[]{:S(2)}, u32[]{:S(2)}) %collective-permute-start.35) | collective-permute-done | bytes 626720 | tf_op jit(solution)/shard_map/ppermute | solution.py:529
  190.5 2.5 column_taps.9.refs_1_
  194.8 2.6 column_taps.10.refs_2_
  197.4 3.1 collective-permute-done.36.cg_ref.refs_3_.refs_11_
  200.5 2.5 column_taps.11.refs_3_
  203.1 2.8 collective-permute-start.40
  206.5 2.5 column_taps.12.refs_4_
  209.0 2.5 column_taps.14.refs_6_
  211.5 2.5 collective-permute-done.38.cg_ref.refs_5_.refs_13_
  214.8 2.6 column_taps.13.refs_5_
  217.4 8.5 %collective-permute-done.40.cg_ref.refs_7_.refs_15_ = bf16[272,1152]{1,0:T(8,128)(2,1)S(1)} collective-permute-done((bf16[272,1152]{1,0:T(8,128)(2,1)S(1)}, bf16[272,1152]{1,0:T(8,128)(2,1)S(1)}, u32[]{:S(2)}, u32[]{:S(2)}) %collective-permute-start.40) | collective-permute-done | bytes 626720 | tf_op jit(solution)/shard_map/ppermute | solution.py:529
  226.8 2.5 column_taps.15.refs_7_
  229.3 14.4 %narrow_weight_grads.1 = bf16[1792,128]{1,0:T(8,128)(2,1)} custom-call(s32[3]{0:T(128)} %pad_add_fusion.1.pos_ref, bf16[640,1152]{1,0:T(8,128)(2,1)} %column_taps.8.refs_0_, bf16[640,1152]{1,0:T(8,128)(2,1)} %column_taps.9.refs_1_, bf16[640,1152]{1,0:T(8,128)(2,1)} %column_taps.10.refs_2_, bf16[640,1152]{1,0:T(8,128)(2,1)} %column_taps.11.refs_3_, ...), custom_call_target="tpu_custom_call" | custom-call | flops 4227858432 | bytes 12000000 | tf_op jit(solution)/shard_map/narrow_weight_grads/pallas_call | solution.py:1081
  244.4 18.3 %input_grads.1 = (bf16[2,1152,512]{2,1,0:T(8,128)(2,1)}, bf16[2,1152,512]{2,1,0:T(8,128)(2,1)}) custom-call(s32[3]{0:T(128)} %pad_add_fusion.1.pos_ref, s32[24]{0:T(128)} %copy-done.5, s32[8,1152]{1,0:T(8,128)} %broadcast_in_dim.93.col_ref, bf16[1728,2048]{1,0:T(8,128)(2,1)} %bitcast.61, bf16[64,2048]{1,0:T(8,128)(2,1)} %wp_ref.1, f32[8,2048]{1,0:T(8,128)} %pad.19.pool_ref, ...), custom_call_target="tpu_custom_call" | custom-call | flops 1000000 | bytes 1000000 | tf_op jit(solution)/shard_map/input_grads/pallas_call | solution.py:1100
  262.8 4.7 %collective-permute-done.44 = bf16[2,1152,512]{2,1,0:T(8,128)(2,1)S(1)} collective-permute-done((bf16[2,1152,512]{2,1,0:T(8,128)(2,1)}, bf16[2,1152,512]{2,1,0:T(8,128)(2,1)S(1)}, u32[]{:S(2)}, u32[]{:S(2)}) %collective-permute-start.44) | collective-permute-done | bytes 2359328 | tf_op jit(solution)/shard_map/ppermute | solution.py:529
  270.7 2.2 collective-permute-start.45
  273.0 38.8 %wide_weight_grads.1 = (f32[1728,2048]{1,0:T(8,128)}, f32[64,2048]{1,0:T(8,128)}, f32[320,256]{1,0:T(8,128)}) custom-call(s32[3]{0:T(128)} %pad_add_fusion.1.pos_ref, bf16[8,4,1152,256]{3,2,1,0:T(8,128)(2,1)} %bitcast.66, bf16[640,1152]{1,0:T(8,128)(2,1)} %column_taps.8.refs_0_, bf16[640,1152]{1,0:T(8,128)(2,1)} %column_taps.9.refs_1_, ...), custom_call_target="tpu_custom_call" | custom-call | flops 1000000 | bytes 1000000 | tf_op jit(solution)/shard_map/wide_weight_grads/pallas_call | solution.py:1133
  311.8 3.5 %fusion.3 = bf16[1152,512]{1,0:T(8,128)(2,1)} fusion(f32[2,1152,512]{2,1,0:T(8,128)} %copy-done.7, bf16[1152,512]{1,0:T(8,128)(2,1)} %collective-permute-done.45, bf16[2,1152,512]{2,1,0:T(8,128)(2,1)S(1)} %copy-done.14), kind=kLoop, calls=%fused_computation.5 | loop fusion | flops 2949120 | bytes 5898240 | tf_op jit(solution)/shard_map/convert_element_type | solution.py:1155
  315.3 5.7 %widen.1 = (f32[1728,2048]{1,0:T(8,128)}, f32[64,2048]{1,0:T(8,128)}) custom-call(bf16[8,1792,128]{2,1,0:T(8,128)(2,1)} %bitcast.67, bf16[8,1792,128]{2,1,0:T(8,128)(2,1)} %bitcast.68, f32[1728,2048]{1,0:T(8,128)} %get-tuple-element.108.keep_ref, f32[64,2048]{1,0:T(8,128)} %get-tuple-element.106.pkeep_ref), custom_call_target="tpu_custom_call", output_to_operand_aliasing={{0}: (2, {}), {1}: (3, {})} | custom-call | flops 1000000 | bytes 20000000 | tf_op jit(solution)/shard_map/widen/pallas_call | solution.py:1159
  (210 shorter events, 61.4 us)
Async XLA Ops:
  7.2 265.8 %all-gather.5.cloned.1.call-start = ((), (), s32[]{:S(2)}) async-start(), calls=%async_computation | async-start | bytes 19464192 | tf_op jit(solution)/shard_map/all_gather | solution.py:885
  10.5 304.9 %all-gather.7.cloned.1.call-start = ((), (), s32[]{:S(2)}) async-start(), calls=%async_computation.1 | async-start | bytes 4128768 | tf_op jit(solution)/shard_map/all_gather | solution.py:1097
  10.9 21.7 %collective-permute-start = (bf16[336,256]{1,0:T(8,128)(2,1)S(1)}, bf16[336,256]{1,0:T(8,128)(2,1)S(1)}, u32[]{:S(2)}, u32[]{:S(2)}) collective-permute-start(bf16[336,256]{1,0:T(8,128)(2,1)S(1)} %concatenate.48.p0), channel_id=1, source_target_pairs={{0,2},{1,3},{2,0},{3,1},{4,6},{5,7},{6,4},{7,5},{8,10},{9,11},{10,... | collective-permute-start | bytes 516104 | tf_op jit(solution)/shard_map/ppermute | solution.py:529
  13.9 18.7 %collective-permute-start.1 = (bf16[336,256]{1,0:T(8,128)(2,1)S(1)}, bf16[336,256]{1,0:T(8,128)(2,1)S(1)}, u32[]{:S(2)}, u32[]{:S(2)}) collective-permute-start(bf16[336,256]{1,0:T(8,128)(2,1)S(1)} %concatenate.48.p0), channel_id=1, source_target_pairs={{0,1},{1,0},{2,3},{3,2},{4,5},{5,4},{6,7},{7,6},{8,9},{9,8},{10,11... | collective-permute-start | bytes 516104 | tf_op jit(solution)/shard_map/ppermute | solution.py:529
  16.2 18.7 %collective-permute-start.4 = (bf16[288,256]{1,0:T(8,128)(2,1)S(1)}, bf16[288,256]{1,0:T(8,128)(2,1)S(1)}, u32[]{:S(2)}, u32[]{:S(2)}) collective-permute-start(bf16[288,256]{1,0:T(8,128)(2,1)S(1)} %get-tuple-element.127), channel_id=1, source_target_pairs={{0,8},{4,12},{8,0},{12,4},{16,24},{20,28},{24,16},{28,20},{1,9},{5... | collective-permute-start | bytes 442376 | tf_op jit(solution)/shard_map/ppermute | solution.py:529
  17.7 17.8 %collective-permute-start.5 = (bf16[288,256]{1,0:T(8,128)(2,1)S(1)}, bf16[288,256]{1,0:T(8,128)(2,1)S(1)}, u32[]{:S(2)}, u32[]{:S(2)}) collective-permute-start(bf16[288,256]{1,0:T(8,128)(2,1)S(1)} %get-tuple-element.126), channel_id=1, source_target_pairs={{0,16},{4,20},{8,24},{12,28},{16,0},{20,4},{24,8},{28,12},{1,17},{... | collective-permute-start | bytes 442376 | tf_op jit(solution)/shard_map/ppermute | solution.py:529
  20.3 18.6 %collective-permute-start.6 = (bf16[288,256]{1,0:T(8,128)(2,1)S(1)}, bf16[288,256]{1,0:T(8,128)(2,1)S(1)}, u32[]{:S(2)}, u32[]{:S(2)}) collective-permute-start(bf16[288,256]{1,0:T(8,128)(2,1)S(1)} %get-tuple-element.125), channel_id=1, source_target_pairs={{0,24},{4,28},{8,16},{12,20},{16,8},{20,12},{24,0},{28,4},{1,25},{... | collective-permute-start | bytes 442376 | tf_op jit(solution)/shard_map/ppermute | solution.py:529
  32.6 7.0 %collective-permute-start.2 = (bf16[576,128]{1,0:T(8,128)(2,1)}, bf16[576,128]{1,0:T(8,128)(2,1)S(1)}, u32[]{:S(2)}, u32[]{:S(2)}) collective-permute-start(bf16[576,128]{1,0:T(8,128)(2,1)} %get-tuple-element.67), channel_id=1, source_target_pairs={{0,4},{8,12},{16,20},{24,28},{4,0},{12,8},{20,16},{28,24},{1,5},{9... | collective-permute-start | bytes 442376 | tf_op jit(solution)/shard_map/ppermute | solution.py:524
  34.2 17.3 %collective-permute-start.3 = (bf16[576,128]{1,0:T(8,128)(2,1)}, bf16[576,128]{1,0:T(8,128)(2,1)S(1)}, u32[]{:S(2)}, u32[]{:S(2)}) collective-permute-start(bf16[576,128]{1,0:T(8,128)(2,1)} %get-tuple-element.68), channel_id=1, source_target_pairs={{4,8},{12,16},{20,24},{8,4},{16,12},{24,20},{5,9},{13,17},{21,25},... | collective-permute-start | bytes 442376 | tf_op jit(solution)/shard_map/ppermute | solution.py:524
  34.9 27.0 %collective-permute-start.10 = (bf16[576,128]{1,0:T(8,128)(2,1)}, bf16[576,128]{1,0:T(8,128)(2,1)S(1)}, u32[]{:S(2)}, u32[]{:S(2)}) collective-permute-start(bf16[576,128]{1,0:T(8,128)(2,1)} %get-tuple-element.74), channel_id=1, source_target_pairs={{12,24},{16,28},{24,12},{28,16},{13,25},{17,29},{25,13},{29,17},{1... | collective-permute-start | bytes 442376 | tf_op jit(solution)/shard_map/ppermute | solution.py:524
  35.6 26.4 %collective-permute-start.7 = (bf16[576,128]{1,0:T(8,128)(2,1)}, bf16[576,128]{1,0:T(8,128)(2,1)S(1)}, u32[]{:S(2)}, u32[]{:S(2)}) collective-permute-start(bf16[576,128]{1,0:T(8,128)(2,1)} %get-tuple-element.71), channel_id=1, source_target_pairs={{0,8},{4,12},{16,24},{20,28},{8,0},{12,4},{24,16},{28,20},{1,9},{5... | collective-permute-start | bytes 442376 | tf_op jit(solution)/shard_map/ppermute | solution.py:524
  38.9 23.1 %collective-permute-start.8 = (bf16[576,128]{1,0:T(8,128)(2,1)}, bf16[576,128]{1,0:T(8,128)(2,1)S(1)}, u32[]{:S(2)}, u32[]{:S(2)}) collective-permute-start(bf16[576,128]{1,0:T(8,128)(2,1)} %get-tuple-element.72), channel_id=1, source_target_pairs={{8,16},{12,20},{16,8},{20,12},{9,17},{13,21},{17,9},{21,13},{10,18... | collective-permute-start | bytes 442376 | tf_op jit(solution)/shard_map/ppermute | solution.py:524
  39.6 22.4 %collective-permute-start.9 = (bf16[576,128]{1,0:T(8,128)(2,1)}, bf16[576,128]{1,0:T(8,128)(2,1)S(1)}, u32[]{:S(2)}, u32[]{:S(2)}) collective-permute-start(bf16[576,128]{1,0:T(8,128)(2,1)} %get-tuple-element.73), channel_id=1, source_target_pairs={{0,12},{4,16},{8,20},{12,0},{16,4},{20,8},{1,13},{5,17},{9,21},{13... | collective-permute-start | bytes 442376 | tf_op jit(solution)/shard_map/ppermute | solution.py:524
  65.2 16.2 %collective-permute-start.12 = (bf16[1152,256]{1,0:T(8,128)(2,1)}, bf16[1152,256]{1,0:T(8,128)(2,1)S(1)}, u32[]{:S(2)}, u32[]{:S(2)}) collective-permute-start(bf16[1152,256]{1,0:T(8,128)(2,1)} %get-tuple-element.77), channel_id=1, source_target_pairs={{0,2},{1,3},{2,0},{3,1},{4,6},{5,7},{6,4},{7,5},{8,10},{9,11},{10,... | collective-permute-start | bytes 1769480 | tf_op jit(solution)/shard_map/ppermute | solution.py:529
  65.7 5.8 %collective-permute-start.13 = (f32[40,256]{1,0:T(8,128)S(1)}, f32[40,256]{1,0:T(8,128)S(1)}, u32[]{:S(2)}, u32[]{:S(2)}) collective-permute-start(f32[40,256]{1,0:T(8,128)S(1)} %get-tuple-element.78), channel_id=1, source_target_pairs={{0,4},{4,0},{8,12},{12,8},{16,20},{20,16},{24,28},{28,24},{1,5},{5... | collective-permute-start | bytes 122888 | tf_op jit(solution)/shard_map/ppermute | solution.py:529
  71.5 6.7 %collective-permute-start.14 = (f32[40,256]{1,0:T(8,128)S(1)}, f32[40,256]{1,0:T(8,128)S(1)}, u32[]{:S(2)}, u32[]{:S(2)}) collective-permute-start(f32[40,256]{1,0:T(8,128)S(1)} %add.264), channel_id=1, source_target_pairs={{0,8},{4,12},{8,0},{12,4},{16,24},{20,28},{24,16},{28,20},{1,9},{5... | collective-permute-start | bytes 122888 | tf_op jit(solution)/shard_map/ppermute | solution.py:529
  74.0 5.7 %collective-permute-start.15 = (f32[40,256]{1,0:T(8,128)S(1)}, f32[40,256]{1,0:T(8,128)S(1)}, u32[]{:S(2)}, u32[]{:S(2)}) collective-permute-start(f32[40,256]{1,0:T(8,128)S(1)} %add.264), channel_id=1, source_target_pairs={{0,16},{4,20},{8,24},{12,28},{16,0},{20,4},{24,8},{28,12},{1,17},{... | collective-permute-start | bytes 122888 | tf_op jit(solution)/shard_map/ppermute | solution.py:529
  74.9 6.5 %collective-permute-start.16 = (f32[40,256]{1,0:T(8,128)S(1)}, f32[40,256]{1,0:T(8,128)S(1)}, u32[]{:S(2)}, u32[]{:S(2)}) collective-permute-start(f32[40,256]{1,0:T(8,128)S(1)} %add.264), channel_id=1, source_target_pairs={{0,24},{4,28},{8,16},{12,20},{16,8},{20,12},{24,0},{28,4},{1,25},{... | collective-permute-start | bytes 122888 | tf_op jit(solution)/shard_map/ppermute | solution.py:529
  76.4 14.2 %collective-permute-start.11 = (bf16[1152,256]{1,0:T(8,128)(2,1)}, bf16[1152,256]{1,0:T(8,128)(2,1)S(1)}, u32[]{:S(2)}, u32[]{:S(2)}) collective-permute-start(bf16[1152,256]{1,0:T(8,128)(2,1)} %get-tuple-element.77), channel_id=1, source_target_pairs={{0,1},{1,0},{2,3},{3,2},{4,5},{5,4},{6,7},{7,6},{8,9},{9,8},{10,11... | collective-permute-start | bytes 1769480 | tf_op jit(solution)/shard_map/ppermute | solution.py:529
  81.4 9.2 %collective-permute-start.17 = (bf16[1152,256]{1,0:T(8,128)(2,1)S(1)}, bf16[1152,256]{1,0:T(8,128)(2,1)}, u32[]{:S(2)}, u32[]{:S(2)}) collective-permute-start(bf16[1152,256]{1,0:T(8,128)(2,1)S(1)} %collective-permute-done.12.c2_ref), channel_id=1, source_target_pairs={{0,1},{1,0},{2,3},{3,2},{4,5},{5,4},{6,7},{7,6},{8,9},{9,8},{10,11... | collective-permute-start | bytes 1769480 | tf_op jit(solution)/shard_map/ppermute | solution.py:529
  84.0 3.5 %collective-permute-start.21 = (bf16[336,256]{1,0:T(8,128)(2,1)S(1)}, bf16[336,256]{1,0:T(8,128)(2,1)S(1)}, u32[]{:S(2)}, u32[]{:S(2)}) collective-permute-start(bf16[336,256]{1,0:T(8,128)(2,1)S(1)} %collective-permute-done.p2), channel_id=1, source_target_pairs={{0,1},{1,0},{2,3},{3,2},{4,5},{5,4},{6,7},{7,6},{8,9},{9,8},{10,11... | collective-permute-start | bytes 516104 | tf_op jit(solution)/shard_map/ppermute | solution.py:529
  85.3 2.4 collective-permute-start.18
  85.3 4.6 %collective-permute-start.19 = (f32[8,256]{1,0:T(8,128)S(1)}, f32[8,256]{1,0:T(8,128)S(1)}, u32[]{:S(2)}, u32[]{:S(2)}) collective-permute-start(f32[8,256]{1,0:T(8,128)S(1)} %fusion.19.t0), channel_id=1, source_target_pairs={{0,2},{1,3},{2,0},{3,1},{4,6},{5,7},{6,4},{7,5},{8,10},{9,11},{10,... | collective-permute-start | bytes 24584 | tf_op jit(solution)/shard_map/ppermute | solution.py:529
  87.5 3.1 collective-permute-start.20
  87.6 28.5 %collective-permute-start.41 = (bf16[4,288,128]{2,1,0:T(8,128)(2,1)S(1)}, bf16[4,288,128]{2,1,0:T(8,128)(2,1)S(1)}, u32[]{:S(2)}, u32[]{:S(2)}) collective-permute-start(bf16[4,288,128]{2,1,0:T(8,128)(2,1)S(1)} %get-tuple-element.124), channel_id=1, source_target_pairs={{0,4},{4,0},{8,12},{12,8},{16,20},{20,16},{24,28},{28,24},{1,5},{5... | collective-permute-start | bytes 884744 | tf_op jit(solution)/shard_map/ppermute | solution.py:529
  94.7 5.2 %collective-permute-start.22 = (f32[8,256]{1,0:T(8,128)S(1)}, f32[8,256]{1,0:T(8,128)S(1)}, u32[]{:S(2)}, u32[]{:S(2)}) collective-permute-start(f32[8,256]{1,0:T(8,128)S(1)} %get-tuple-element.82), channel_id=1, source_target_pairs={{0,4},{4,0},{8,12},{12,8},{16,20},{20,16},{24,28},{28,24},{1,5},{5... | collective-permute-start | bytes 24584 | tf_op jit(solution)/shard_map/ppermute | solution.py:529
  100.0 7.5 %collective-permute-start.23 = (f32[8,256]{1,0:T(8,128)S(1)}, f32[8,256]{1,0:T(8,128)S(1)}, u32[]{:S(2)}, u32[]{:S(2)}) collective-permute-start(f32[8,256]{1,0:T(8,128)S(1)} %add.269.s0), channel_id=1, source_target_pairs={{0,8},{4,12},{8,0},{12,4},{16,24},{20,28},{24,16},{28,20},{1,9},{5... | collective-permute-start | bytes 24584 | tf_op jit(solution)/shard_map/ppermute | solution.py:529
  105.1 4.7 %collective-permute-start.24 = (f32[8,256]{1,0:T(8,128)S(1)}, f32[8,256]{1,0:T(8,128)S(1)}, u32[]{:S(2)}, u32[]{:S(2)}) collective-permute-start(f32[8,256]{1,0:T(8,128)S(1)} %add.269.s0), channel_id=1, source_target_pairs={{0,16},{4,20},{8,24},{12,28},{16,0},{20,4},{24,8},{28,12},{1,17},{... | collective-permute-start | bytes 24584 | tf_op jit(solution)/shard_map/ppermute | solution.py:529
  105.6 5.6 %collective-permute-start.25 = (f32[8,256]{1,0:T(8,128)S(1)}, f32[8,256]{1,0:T(8,128)S(1)}, u32[]{:S(2)}, u32[]{:S(2)}) collective-permute-start(f32[8,256]{1,0:T(8,128)S(1)} %add.269.s0), channel_id=1, source_target_pairs={{0,24},{4,28},{8,16},{12,20},{16,8},{20,12},{24,0},{28,4},{1,25},{... | collective-permute-start | bytes 24584 | tf_op jit(solution)/shard_map/ppermute | solution.py:529
  113.5 4.4 %collective-permute-start.26 = (f32[8,256]{1,0:T(8,128)S(1)}, f32[8,256]{1,0:T(8,128)S(1)}, u32[]{:S(2)}, u32[]{:S(2)}) collective-permute-start(f32[8,256]{1,0:T(8,128)S(1)} %get-tuple-element.88), channel_id=1, source_target_pairs={{0,4},{4,0},{8,12},{12,8},{16,20},{20,16},{24,28},{28,24},{1,5},{5... | collective-permute-start | bytes 24584 | tf_op jit(solution)/shard_map/ppermute | solution.py:529
  117.9 5.3 %collective-permute-start.27 = (f32[8,256]{1,0:T(8,128)S(1)}, f32[8,256]{1,0:T(8,128)S(1)}, u32[]{:S(2)}, u32[]{:S(2)}) collective-permute-start(f32[8,256]{1,0:T(8,128)S(1)} %add.273.s0), channel_id=1, source_target_pairs={{0,8},{4,12},{8,0},{12,4},{16,24},{20,28},{24,16},{28,20},{1,9},{5... | collective-permute-start | bytes 24584 | tf_op jit(solution)/shard_map/ppermute | solution.py:529
  119.9 6.7 %collective-permute-start.28 = (f32[8,256]{1,0:T(8,128)S(1)}, f32[8,256]{1,0:T(8,128)S(1)}, u32[]{:S(2)}, u32[]{:S(2)}) collective-permute-start(f32[8,256]{1,0:T(8,128)S(1)} %add.273.s0), channel_id=1, source_target_pairs={{0,16},{4,20},{8,24},{12,28},{16,0},{20,4},{24,8},{28,12},{1,17},{... | collective-permute-start | bytes 24584 | tf_op jit(solution)/shard_map/ppermute | solution.py:529
  120.7 5.9 %collective-permute-start.29 = (f32[8,256]{1,0:T(8,128)S(1)}, f32[8,256]{1,0:T(8,128)S(1)}, u32[]{:S(2)}, u32[]{:S(2)}) collective-permute-start(f32[8,256]{1,0:T(8,128)S(1)} %add.273.s0), channel_id=1, source_target_pairs={{0,24},{4,28},{8,16},{12,20},{16,8},{20,12},{24,0},{28,4},{1,25},{... | collective-permute-start | bytes 24584 | tf_op jit(solution)/shard_map/ppermute | solution.py:529
  129.5 4.6 %collective-permute-start.30 = (bf16[184,256]{1,0:T(8,128)(2,1)S(1)}, bf16[184,256]{1,0:T(8,128)(2,1)S(1)}, u32[]{:S(2)}, u32[]{:S(2)}) collective-permute-start(bf16[184,256]{1,0:T(8,128)(2,1)S(1)} %pad_maximum_fusion.2), channel_id=1, source_target_pairs={{0,4},{4,0},{8,12},{12,8},{16,20},{20,16},{24,28},{28,24},{1,5},{5... | collective-permute-start | bytes 282632 | tf_op jit(solution)/shard_map/ppermute | solution.py:529
  134.3 7.4 %collective-permute-start.31 = (bf16[64,256]{1,0:T(8,128)(2,1)S(1)}, bf16[64,256]{1,0:T(8,128)(2,1)S(1)}, u32[]{:S(2)}, u32[]{:S(2)}) collective-permute-start(bf16[64,256]{1,0:T(8,128)(2,1)S(1)} %get-tuple-element.132), channel_id=1, source_target_pairs={{0,8},{4,12},{8,0},{12,4},{16,24},{20,28},{24,16},{28,20},{1,9},{5... | collective-permute-start | bytes 98312 | tf_op jit(solution)/shard_map/ppermute | solution.py:529
  137.1 8.2 %collective-permute-start.32 = (bf16[64,256]{1,0:T(8,128)(2,1)S(1)}, bf16[64,256]{1,0:T(8,128)(2,1)S(1)}, u32[]{:S(2)}, u32[]{:S(2)}) collective-permute-start(bf16[64,256]{1,0:T(8,128)(2,1)S(1)} %get-tuple-element.133), channel_id=1, source_target_pairs={{0,16},{4,20},{8,24},{12,28},{16,0},{20,4},{24,8},{28,12},{1,17},{... | collective-permute-start | bytes 98312 | tf_op jit(solution)/shard_map/ppermute | solution.py:529
  137.1 8.2 %collective-permute-start.33 = (bf16[64,256]{1,0:T(8,128)(2,1)S(1)}, bf16[64,256]{1,0:T(8,128)(2,1)S(1)}, u32[]{:S(2)}, u32[]{:S(2)}) collective-permute-start(bf16[64,256]{1,0:T(8,128)(2,1)S(1)} %get-tuple-element.134), channel_id=1, source_target_pairs={{0,24},{4,28},{8,16},{12,20},{16,8},{20,12},{24,0},{28,4},{1,25},{... | collective-permute-start | bytes 98312 | tf_op jit(solution)/shard_map/ppermute | solution.py:529
  147.1 10.3 %collective-permute-start.34 = (bf16[272,1152]{1,0:T(8,128)(2,1)S(1)}, bf16[272,1152]{1,0:T(8,128)(2,1)S(1)}, u32[]{:S(2)}, u32[]{:S(2)}) collective-permute-start(bf16[272,1152]{1,0:T(8,128)(2,1)S(1)} %conv_grads.1.cg_ref.refs_0_.refs_8_), channel_id=1, source_target_pairs={{0,4},{4,0},{8,12},{12,8},{16,20},{20,16},{24,28},{28,24},{1,5},{5... | collective-permute-start | bytes 1880072 | tf_op jit(solution)/shard_map/ppermute | solution.py:529
  148.6 34.4 %collective-permute-start.35 = (bf16[272,1152]{1,0:T(8,128)(2,1)S(1)}, bf16[272,1152]{1,0:T(8,128)(2,1)S(1)}, u32[]{:S(2)}, u32[]{:S(2)}) collective-permute-start(bf16[272,1152]{1,0:T(8,128)(2,1)S(1)} %conv_grads.1.cg_ref.refs_0_.refs_8_), channel_id=1, source_target_pairs={{0,8},{4,12},{8,0},{12,4},{16,24},{20,28},{24,16},{28,20},{1,9},{5... | collective-permute-start | bytes 1880072 | tf_op jit(solution)/shard_map/ppermute | solution.py:529
  150.6 43.9 %collective-permute-start.37 = (bf16[272,1152]{1,0:T(8,128)(2,1)S(1)}, bf16[272,1152]{1,0:T(8,128)(2,1)S(1)}, u32[]{:S(2)}, u32[]{:S(2)}) collective-permute-start(bf16[272,1152]{1,0:T(8,128)(2,1)S(1)} %conv_grads.1.cg_ref.refs_0_.refs_8_), channel_id=1, source_target_pairs={{0,16},{4,20},{8,24},{12,28},{16,0},{20,4},{24,8},{28,12},{1,17},{... | collective-permute-start | bytes 1880072 | tf_op jit(solution)/shard_map/ppermute | solution.py:529
  157.4 31.2 %collective-permute-start.42 = (bf16[1,8,288,128]{3,2,1,0:T(8,128)(2,1)}, bf16[1,8,288,128]{3,2,1,0:T(8,128)(2,1)}, u32[]{:S(2)}, u32[]{:S(2)}) collective-permute-start(bf16[1,8,288,128]{3,2,1,0:T(8,128)(2,1)} %bitcast.70), channel_id=1, source_target_pairs={{0,2},{1,3},{2,0},{3,1},{4,6},{5,7},{6,4},{7,5},{8,10},{9,11},{10,... | collective-permute-start | bytes 1769480 | tf_op jit(solution)/shard_map/ppermute | solution.py:529
  183.0 20.1 %collective-permute-start.39 = (bf16[272,1152]{1,0:T(8,128)(2,1)}, bf16[272,1152]{1,0:T(8,128)(2,1)S(1)}, u32[]{:S(2)}, u32[]{:S(2)}) collective-permute-start(bf16[272,1152]{1,0:T(8,128)(2,1)} %copy-done.2), channel_id=1, source_target_pairs={{0,24},{4,28},{8,16},{12,20},{16,8},{20,12},{24,0},{28,4},{1,25},{... | collective-permute-start | bytes 1880072 | tf_op jit(solution)/shard_map/ppermute | solution.py:529
  184.9 15.6 %collective-permute-start.36 = (bf16[272,1152]{1,0:T(8,128)(2,1)S(1)}, bf16[272,1152]{1,0:T(8,128)(2,1)}, u32[]{:S(2)}, u32[]{:S(2)}) collective-permute-start(bf16[272,1152]{1,0:T(8,128)(2,1)S(1)} %collective-permute-done.35.cg_ref.refs_2_.refs_10_), channel_id=1, source_target_pairs={{0,4},{4,0},{8,12},{12,8},{16,20},{20,16},{24,28},{28,24},{1,5},{5... | collective-permute-start | bytes 1880072 | tf_op jit(solution)/shard_map/ppermute | solution.py:529
  190.5 38.8 %collective-permute-start.43 = (bf16[2,8,288,128]{3,2,1,0:T(8,128)(2,1)}, bf16[2,8,288,128]{3,2,1,0:T(8,128)(2,1)}, u32[]{:S(2)}, u32[]{:S(2)}) collective-permute-start(bf16[2,8,288,128]{3,2,1,0:T(8,128)(2,1)} %constant_dynamic-update-slice_fusion.refs_8_), channel_id=1, source_target_pairs={{0,1},{1,0},{2,3},{3,2},{4,5},{5,4},{6,7},{7,6},{8,9},{9,8},{10,11... | collective-permute-start | bytes 3538952 | tf_op jit(solution)/shard_map/ppermute | solution.py:529
  194.5 19.4 %collective-permute-start.38 = (bf16[272,1152]{1,0:T(8,128)(2,1)S(1)}, bf16[272,1152]{1,0:T(8,128)(2,1)S(1)}, u32[]{:S(2)}, u32[]{:S(2)}) collective-permute-start(bf16[272,1152]{1,0:T(8,128)(2,1)S(1)} %collective-permute-done.37.cg_ref.refs_4_.refs_12_), channel_id=1, source_target_pairs={{0,4},{4,0},{8,12},{12,8},{16,20},{20,16},{24,28},{28,24},{1,5},{5... | collective-permute-start | bytes 1880072 | tf_op jit(solution)/shard_map/ppermute | solution.py:529
  203.1 22.8 %collective-permute-start.40 = (bf16[272,1152]{1,0:T(8,128)(2,1)S(1)}, bf16[272,1152]{1,0:T(8,128)(2,1)S(1)}, u32[]{:S(2)}, u32[]{:S(2)}) collective-permute-start(bf16[272,1152]{1,0:T(8,128)(2,1)S(1)} %collective-permute-done.39.cg_ref.refs_6_.refs_14_), channel_id=1, source_target_pairs={{0,4},{4,0},{8,12},{12,8},{16,20},{20,16},{24,28},{28,24},{1,5},{5... | collective-permute-start | bytes 1880072 | tf_op jit(solution)/shard_map/ppermute | solution.py:529
  262.7 4.8 %collective-permute-start.44 = (bf16[2,1152,512]{2,1,0:T(8,128)(2,1)}, bf16[2,1152,512]{2,1,0:T(8,128)(2,1)S(1)}, u32[]{:S(2)}, u32[]{:S(2)}) collective-permute-start(bf16[2,1152,512]{2,1,0:T(8,128)(2,1)} %get-tuple-element.104), channel_id=1, source_target_pairs={{0,1},{1,0},{2,3},{3,2},{4,5},{5,4},{6,7},{7,6},{8,9},{9,8},{10,11... | collective-permute-start | bytes 7077896 | tf_op jit(solution)/shard_map/ppermute | solution.py:529
  270.7 41.1 %collective-permute-start.45 = (bf16[1152,512]{1,0:T(8,128)(2,1)}, bf16[1152,512]{1,0:T(8,128)(2,1)}, u32[]{:S(2)}, u32[]{:S(2)}) collective-permute-start(bf16[1152,512]{1,0:T(8,128)(2,1)} %fusion.4), channel_id=1, source_target_pairs={{0,2},{1,3},{2,0},{3,1},{4,6},{5,7},{6,4},{7,5},{8,10},{9,11},{10,... | collective-permute-start | bytes 3538952 | tf_op jit(solution)/shard_map/ppermute | solution.py:529
  (31 other events, 422.1 us)
Sparse Core Ops, SparseCore 0:
  11.0 166.6 all-gather.4
  243.9 65.7 all-gather.6
